TPU v7x, 32 devices: a whole 2x2x4 slice. The times are simulated.
32 devices in a mesh: crop: 2 (over x), row: 16 (over z, y, core).
Axes of the slice: x: 2, y: 2, z: 4, core: 2. Of those that a mesh axis runs over, the one named last changes fastest.
Arguments:
- pair: bfloat16 [2, 384, 384, 128], P('crop', 'row'), may hold values from -6 to 6
- crop_len: int32 [2], P('crop'), may hold values from 192 to 384, as said below
- targets: int32 [2, 384, 384], P('crop', 'row'), may hold values from 0 to 63
- neighbours: int32 [2, 384, 384], P('crop', 'row'), may hold values 0 or 1
- wide: float32 [128, 1152], P('row', 'crop'), may hold values from -0.5 to 0.5
- wide_rows: float32 [128], P('row'), may hold values from 2.0345052e-07 to 2.0616319e-05, as said below
- wide_cols: float32 [1152], P('crop'), may hold values from 2.0345052e-07 to 2.0616319e-05, as said below
- down: float32 [512, 128], P('row', 'crop'), may hold values from -0.25 to 0.25
- down_rows: float32 [512], P('row'), may hold values from 2.0345052e-07 to 2.0616319e-05, as said below
- down_cols: float32 [128], P('crop'), may hold values from 2.0345052e-07 to 2.0616319e-05, as said below
- gains: float32 [3, 128], replicated, may hold values from 0.45 to 2.75, as said below
- gain_second: float32 [3, 128], replicated, may hold values from 1e-05 to 4e-05
- small: float32 [128, 68], replicated, may hold values from -0.5 to 0.5
- small_second: float32 [128, 68], replicated, may hold values from 1.2885199e-06 to 5.1540796e-06
Outputs:
- loss_sum: float32 [], replicated
- pair_count: float32 [], replicated
- wide_grad: float32 [128, 1152], P('row', 'crop')
- wide_rows_new: float32 [128], P('row')
- wide_cols_new: float32 [1152], P('crop')
- wide_new: float32 [128, 1152], P('row', 'crop')
- down_grad: float32 [512, 128], P('row', 'crop')
- down_rows_new: float32 [512], P('row')
- down_cols_new: float32 [128], P('crop')
- down_new: float32 [512, 128], P('row', 'crop')
- gain_grad: float32 [3, 128], replicated
- gain_second_new: float32 [3, 128], replicated
- gains_new: float32 [3, 128], replicated
- small_grad: float32 [128, 68], replicated
- small_second_new: float32 [128, 68], replicated
- small_new: float32 [128, 68], replicated
Inputs may be any that keep to these rules, and one draw needn't show every extreme that they name: `crop_len`: the first entry is 384; the others lie between 192 and 384. `wide_rows`: Positive. `wide_cols`: Positive. `down_rows`: Positive. `down_cols`: Positive. `gains`: Positive.
All inputs are finite; a program needn't handle non-finite values. No bound on the sum of `neighbours` on one device may be relied on, other than what follows from the above.
Results may differ from a plain program's by a relative error of at most 0.0052.
The roundings to bfloat16 on the way count: a program that leaves them out, or rounds other values in their place, can miss the bound.
Values may be sent and summed in bfloat16 or wider, within the bound.
No kernel may reach another device: no remote copies, remote signals or barrier semaphores. Data moves between devices by JAX's collectives and lax.ppermute only.
A program may use at most 320 MiB of HBM per device.

v0:
```python
from functools import partial

import jax
import jax.numpy as jnp
from jax import lax
from jax.sharding import PartitionSpec as P

CZ = 128
HEADS = 4
HEAD_DIM = 32
FF = 512
BINS = 64


HIGH = lax.Precision.HIGHEST
DECAY = 1.0 - 10.0 ** (-0.8)
TINY = 1e-30


def rounded(v):
    return v.astype(jnp.bfloat16).astype(jnp.float32)


def normed(x, gain):
    centre = x - jnp.mean(x, -1, keepdims=True)
    var = jnp.mean(centre * centre, -1, keepdims=True)
    return centre * lax.rsqrt(var + 1e-05) * gain


def front(zfull, gain, w_qkvg, w_bias):
    zb = rounded(normed(zfull, gain))
    proj = jnp.einsum("ijc,cd->ijd", zb, w_qkvg, precision=HIGH)
    query = rounded(proj[..., :CZ])
    keys = rounded(proj[..., CZ : 2 * CZ])
    values = rounded(proj[..., 2 * CZ : 3 * CZ])
    bias_part = jnp.einsum("ijc,ch->hij", zb, w_bias, precision=HIGH)
    return (bias_part, query, keys, values, proj[..., 3 * CZ :])


def rest(
    zfull,
    key_bias,
    onehot,
    mask,
    query,
    keys,
    values,
    gate,
    bias,
    w_out,
    gain_one,
    w_in,
    w_down,
    gain_two,
    w_head,
):
    count_rows, width = (query.shape[0], query.shape[1])
    qh = query.reshape(count_rows, width, HEADS, HEAD_DIM)
    kh = keys.reshape(count_rows, width, HEADS, HEAD_DIM)
    vh = values.reshape(count_rows, width, HEADS, HEAD_DIM)
    score = jnp.einsum("ijhd,ikhd->ihjk", qh, kh, precision=HIGH) / jnp.sqrt(jnp.float32(HEAD_DIM))
    score = score + bias[None] + key_bias[None, None, None, :]
    probs = rounded(jax.nn.softmax(score, -1))
    attended = jnp.einsum("ihjk,ikhd->ijhd", probs, vh, precision=HIGH).reshape(
        count_rows, width, CZ
    )
    attended = rounded(attended * jax.nn.sigmoid(gate))
    z1 = zfull + jnp.einsum("ijc,cd->ijd", attended, w_out, precision=HIGH)
    zb2 = rounded(normed(z1, gain_one))
    hidden = rounded(jax.nn.silu(jnp.einsum("ijc,cd->ijd", zb2, w_in, precision=HIGH)))
    z2 = z1 + jnp.einsum("ijd,dc->ijc", hidden, w_down, precision=HIGH)
    zb3 = rounded(normed(z2, gain_two))
    logits = jnp.einsum("ijc,cb->ijb", zb3, w_head, precision=HIGH)
    logp = jax.nn.log_softmax(logits, -1)
    return -jnp.sum(jnp.sum(logp * onehot, -1) * mask)


def placed(length, values, start):
    return lax.dynamic_update_slice(jnp.zeros((length,), jnp.float32), values, (start,))


def plain(weight, grad, second, rate):
    second_new = DECAY * second + (1.0 - DECAY) * (grad * grad + TINY)
    update = grad * lax.rsqrt(second_new)
    clip = jnp.maximum(1.0, jnp.sqrt(jnp.mean(update * update)))
    return (second_new, weight - rate * update / clip)


def body(
    pair,
    crop_len,
    targets,
    neighbours,
    wide,
    wide_rows,
    wide_cols,
    down,
    down_rows,
    down_cols,
    gains,
    gain_second,
    small,
    small_second,
):
    row_index = lax.axis_index("row")
    crop_index = lax.axis_index("crop")
    zfull = pair[0].astype(jnp.float32)
    count_rows, width = (zfull.shape[0], zfull.shape[1])
    length = crop_len[0]
    columns = jnp.arange(width, dtype=jnp.int32)
    valid_col = columns < length
    valid_row = row_index * count_rows + jnp.arange(count_rows, dtype=jnp.int32) < length
    mask = (valid_row[:, None] & valid_col[None, :] & (neighbours[0] > 0)).astype(jnp.float32)
    key_bias = jnp.where(valid_col, 0.0, -1000000000.0).astype(jnp.float32)
    onehot = (targets[0][..., None] == jnp.arange(BINS, dtype=jnp.int32)).astype(jnp.float32)
    wide_part, down_part = (
        lax.all_gather(wide.astype(jnp.bfloat16), "row", axis=0, tiled=True),
        lax.all_gather(down.astype(jnp.bfloat16), "row", axis=0, tiled=True),
    )
    wide_full, down_full = (
        lax.all_gather(wide_part, "crop", axis=1, tiled=True),
        lax.all_gather(down_part, "crop", axis=1, tiled=True),
    )
    wide_f = wide_full.astype(jnp.float32)
    down_f = down_full.astype(jnp.float32)
    small_f = rounded(small)
    front_out, front_back = jax.vjp(
        partial(front, zfull), gains[0], wide_f[:, : 4 * CZ], small_f[:, :HEADS]
    )
    bias_part, query, keys, values, gate = front_out
    bias_full = lax.all_gather(bias_part.astype(jnp.bfloat16), "row", axis=1, tiled=True).astype(
        jnp.float32
    )
    later = (
        wide_f[:, 4 * CZ : 5 * CZ],
        gains[1],
        wide_f[:, 5 * CZ :],
        down_f,
        gains[2],
        small_f[:, HEADS:],
    )
    local_rest = partial(rest, zfull, key_bias, onehot, mask)
    loss_local, rest_back = jax.vjp(local_rest, query, keys, values, gate, bias_full, *later)
    loss_sum, pair_count = lax.psum((loss_local, jnp.sum(mask)), ("crop", "row"))
    grads = rest_back(jnp.float32(1.0) / pair_count)
    d_query, d_keys, d_values, d_gate, d_bias = grads[:5]
    d_out, d_gain_one, d_in, d_down, d_gain_two, d_head = grads[5:]
    d_part = rounded(lax.psum_scatter(d_bias, "row", scatter_dimension=1, tiled=True))
    d_gain_zero, d_qkvg, d_pbias = front_back((d_part, d_query, d_keys, d_values, d_gate))
    wide_terms = jnp.concatenate([d_qkvg, d_out, d_in], 1)
    wide_half, down_half = (
        lax.psum_scatter(
            wide_terms.astype(jnp.bfloat16), "crop", scatter_dimension=1, tiled=True
        ).astype(jnp.float32),
        lax.psum_scatter(
            d_down.astype(jnp.bfloat16), "crop", scatter_dimension=1, tiled=True
        ).astype(jnp.float32),
    )
    wide_g, down_g = (
        lax.psum_scatter(wide_half, "row", scatter_dimension=0, tiled=True),
        lax.psum_scatter(down_half, "row", scatter_dimension=0, tiled=True),
    )
    wide_r_len, wide_c_len = wide_g.shape
    down_r_len, down_c_len = down_g.shape
    first_crop = crop_index == 0
    first_row = row_index == 0
    wide_sq = wide_g * wide_g
    down_sq = down_g * down_g
    wide_r_term = placed(
        CZ,
        (1.0 - DECAY) * jnp.sum(wide_sq, 1) / (5 * CZ + FF)
        + jnp.where(first_crop, DECAY * wide_rows, 0.0),
        row_index * wide_r_len,
    )
    wide_c_term = placed(
        5 * CZ + FF,
        (1.0 - DECAY) * jnp.sum(wide_sq, 0) / CZ + jnp.where(first_row, DECAY * wide_cols, 0.0),
        crop_index * wide_c_len,
    )
    down_r_term = placed(
        FF,
        (1.0 - DECAY) * jnp.sum(down_sq, 1) / CZ + jnp.where(first_crop, DECAY * down_rows, 0.0),
        row_index * down_r_len,
    )
    down_c_term = placed(
        CZ,
        (1.0 - DECAY) * jnp.sum(down_sq, 0) / FF + jnp.where(first_row, DECAY * down_cols, 0.0),
        crop_index * down_c_len,
    )
    gain_terms = jnp.stack([d_gain_zero, d_gain_one, d_gain_two])
    small_terms = jnp.concatenate([d_pbias, d_head], 1)
    summed = lax.psum(
        (wide_r_term, wide_c_term, down_r_term, down_c_term, gain_terms, small_terms),
        ("crop", "row"),
    )
    wide_r_all, wide_c_all, down_r_all, down_c_all, gain_grad, small_grad = summed
    shift = (1.0 - DECAY) * TINY
    wide_r_all = wide_r_all + shift
    wide_c_all = wide_c_all + shift
    down_r_all = down_r_all + shift
    down_c_all = down_c_all + shift

    def factored_step(grad, rows_all, cols_all, row_start, col_start):
        rows_mine = lax.dynamic_slice_in_dim(rows_all, row_start, grad.shape[0])
        cols_mine = lax.dynamic_slice_in_dim(cols_all, col_start, grad.shape[1])
        second = rows_mine[:, None] * cols_mine[None, :] / jnp.mean(rows_all)
        return (grad * lax.rsqrt(second), rows_mine, cols_mine)

    wide_u, wide_r_new, wide_c_new = factored_step(
        wide_g, wide_r_all, wide_c_all, row_index * wide_r_len, crop_index * wide_c_len
    )
    down_u, down_r_new, down_c_new = factored_step(
        down_g, down_r_all, down_c_all, row_index * down_r_len, crop_index * down_c_len
    )
    wide_total, down_total = lax.psum(
        (jnp.sum(wide_u * wide_u), jnp.sum(down_u * down_u)), ("crop", "row")
    )
    wide_clip = jnp.maximum(0.1, jnp.sqrt(wide_total / (CZ * (5 * CZ + FF))))
    down_clip = jnp.maximum(0.1, jnp.sqrt(down_total / (FF * CZ)))
    wide_new = wide - 0.03 * wide_u / wide_clip
    down_new = down - 0.03 * down_u / down_clip
    gain_s, gain_n = plain(gains, gain_grad, gain_second, 0.3)
    small_s, small_n = plain(small, small_grad, small_second, 0.03)
    return (
        loss_sum,
        pair_count,
        wide_g,
        wide_r_new,
        wide_c_new,
        wide_new,
        down_g,
        down_r_new,
        down_c_new,
        down_new,
        gain_grad,
        gain_s,
        gain_n,
        small_grad,
        small_s,
        small_n,
    )


def solution(mesh):
    return jax.shard_map(
        body,
        mesh=mesh,
        in_specs=(
            P("crop", "row", None, None),
            P("crop"),
            P("crop", "row", None),
            P("crop", "row", None),
            P("row", "crop"),
            P("row"),
            P("crop"),
            P("row", "crop"),
            P("row"),
            P("crop"),
            P(),
            P(),
            P(),
            P(),
        ),
        out_specs=(
            P(),
            P(),
            P("row", "crop"),
            P("row"),
            P("crop"),
            P("row", "crop"),
            P("row", "crop"),
            P("row"),
            P("crop"),
            P("row", "crop"),
            P(),
            P(),
            P(),
            P(),
            P(),
            P(),
        ),
        check_vma=False,
    )
```

profile of v0, /device:TPU:0, one launch (start us, length us, event | category | flops | bytes accessed | tf_op | source)
XLA Modules:
  0.0 872.2 jit_solution(9780845283737829366)
XLA Ops:
  20.6 42.4 %psum.71 = f32[]{:T(128)} all-reduce(f32[]{:T(128)} %get-tuple-element.124), channel_id=1, replica_groups=mesh['crop'=2,'row'=16] {'crop','row'}, use_global_device_ids=true, to_apply=%region_14.15 | all-reduce | flops 1 | bytes 8 | tf_op jit(solution)/shard_map/psum | solution.py:144
  63.7 21.5 %all_gather.18 = bf16[512,64]{1,0:T(8,128)(2,1)S(1)} all-gather(bf16[32,64]{1,0:T(8,128)(2,1)S(1)} %convert_element_type.159), channel_id=1, replica_groups=mesh['crop'=2,'row'=16] {'row'}, dimensions={0}, use_global_device_ids=true | all-gather | bytes 69632 | tf_op jit(solution)/shard_map/all_gather | solution.py:118
  90.4 17.6 %all_gather.15 = bf16[128,576]{1,0:T(8,128)(2,1)S(1)} all-gather(bf16[8,576]{1,0:T(8,128)(2,1)S(1)} %convert_element_type.150), channel_id=1, replica_groups=mesh['crop'=2,'row'=16] {'row'}, dimensions={0}, use_global_device_ids=true | all-gather | bytes 156672 | tf_op jit(solution)/shard_map/all_gather | solution.py:117
  115.1 9.9 %fusion.112 = (bf16[24,384,512]{2,1,0:T(8,128)(2,1)S(1)}, f32[24,384,512]{2,1,0:T(8,128)}) fusion(bf16[24,384,128]{1,2,0:T(8,128)(2,1)} %copy-done.5, bf16[128,1152]{0,1:T(8,128)(2,1)S(1)} %all_gather.16), kind=kOutput, calls=%fused_computation.205 | convolution fusion | flops 1212678144 | bytes 30801920 | tf_op jit(solution)/shard_map/jvp(ijc,cd->ijd)/dot_general | solution.py:32
  141.8 22.4 %fusion.116 = f32[24,4,384,384]{2,3,1,0:T(8,128)} fusion(bf16[24,384,4,32]{1,3,2,0:T(8,128)(2,1)} %bitcast.159, bf16[24,384,4,32]{1,3,2,0:T(8,128)(2,1)} %bitcast.157), kind=kOutput, calls=%fused_computation.209 | convolution fusion | flops 905969664 | bytes 61341696 | tf_op jit(solution)/shard_map/jvp(ijhd,ikhd->ihjk)/dot_general | solution.py:61
  170.0 58.8 %fusion.113 = (f32[24,4,384]{2,1,0:T(4,128)S(1)}, f32[24,4,384,384]{2,3,1,0:T(8,128)}) fusion(f32[24,4,384,384]{2,3,1,0:T(8,128)} %fusion.116, f32[384]{0:T(512)S(1)} %broadcast_select_fusion.1, f32[4,384,384]{1,2,0:T(8,128)} %copy.177), kind=kOutput, calls=%fused_computation.206 | output fusion | flops 113246592 | bytes 115754496 | tf_op jit(solution)/shard_map/jvp()/sub | solution.py:63
  229.6 28.3 %divide_convert_fusion = bf16[24,4,384,384]{2,3,1,0:T(8,128)(2,1)} fusion(f32[24,4,384,384]{2,3,1,0:T(8,128)} %get-tuple-element.141, f32[24,4,384]{2,1,0:T(4,128)S(1)} %get-tuple-element.140), kind=kLoop, calls=%fused_computation.8 | loop fusion | flops 28311552 | bytes 85082112 | tf_op jit(solution)/shard_map/jvp()/convert_element_type | solution.py:21
  257.9 16.2 %fusion.117 = f32[24,4,32,384]{3,2,1,0:T(8,128)} fusion(bf16[24,384,4,32]{1,3,2,0:T(8,128)(2,1)} %bitcast.150, bf16[24,4,384,384]{2,3,1,0:T(8,128)(2,1)} %divide_convert_fusion), kind=kOutput, calls=%fused_computation.210 | convolution fusion | flops 905969664 | bytes 35389440 | tf_op jit(solution)/shard_map/jvp(ihjk,ikhd->ijhd)/dot_general | solution.py:64
  320.4 21.4 %fusion.16 = f32[24,384,512]{2,1,0:T(8,128)} fusion(f32[24,384,512]{2,1,0:T(8,128)} %get-tuple-element.145, f32[24,384,128]{1,2,0:T(8,128)} %copy-done.10, f32[24,384]{1,0:T(8,128)S(1)} %negate_multiply_fusion.1, bf16[512,128]{0,1:T(8,128)(2,1)S(1)} %copy-done.28), kind=kOutput, calls=%fused_computation.24 | convolution fusion | flops 7300841472 | bytes 42635264 | tf_op jit(solution)/shard_map/transpose(jvp(ijd,dc->ijc))/dot_general | solution.py:71
  341.9 11.4 %fusion.71 = bf16[128,512]{1,0:T(8,128)(2,1)} fusion(f32[24,384,512]{2,1,0:T(8,128)} %fusion.16, f32[24,384,128]{1,2,0:T(8,128)S(1)} %bitcast.147, f32[128]{0:T(128)S(1)} %get-tuple-element.134, f32[24,384]{1,0:T(8,128)S(1)} %fusion.84, f32[24,384]{1,0:T(8,128)S(1)} %broadcast_multiply_fusion.1), kind=kOutput, calls=%fused_computation.108 | convolution fusion | flops 7252541440 | bytes 23798272 | tf_op jit(solution)/shard_map/transpose(jvp(ijc,cd->ijd))/dot_general | solution.py:70
  353.2 15.2 %fusion.36 = (f32[24,384]{1,0:T(8,128)S(1)}, bf16[24,384,128]{1,2,0:T(8,128)(2,1)S(1)}) fusion(f32[24,384,128]{1,2,0:T(8,128)S(1)} %bitcast.147, f32[128]{0:T(128)S(1)} %get-tuple-element.134, f32[24,384]{1,0:T(8,128)S(1)} %broadcast_multiply_fusion.1, f32[24,384,512]{2,1,0:T(8,128)} %fusion.16, bf16[128,1152]{0,1:T(8,128)(2,1)S(1)} %all_gather.16), kind=kOutput, calls=%fused_computation.59 | convolution fusion | flops 7254825984 | bytes 26157568 | tf_op jit(solution)/shard_map/transpose(jvp(ijc,cd->ijd))/dot_general | solution.py:70
  372.1 10.3 %convert_multiply_fusion.3 = (f32[24,384,128]{2,1,0:T(8,128)}, f32[24,384,128]{2,1,0:T(8,128)}) fusion(f32[24,384,512]{2,1,0:T(8,128)} %get-tuple-element.139, f32[24,384,128]{2,1,0:T(8,128)S(1)} %bitcast.154, bf16[128,1152]{0,1:T(8,128)(2,1)S(1)} %all_gather.16, f32[24,384,128]{1,2,0:T(8,128)S(1)} %bitcast.156, f32[24,384]{1,0:T(8,128)S(1)} %negate_multiply_fusion, ...), kind=kOutput, calls=%fused_computation.39 | convolution fusion | flops 1835532288 | bytes 30888448 | tf_op jit(solution)/shard_map/transpose(jvp(ijc,cd->ijd))/dot_general | solution.py:68
  393.9 31.1 %convolution_convert_fusion.1 = bf16[24,4,32,384]{3,2,1,0:T(8,128)(2,1)} fusion(f32[24,4,32,384]{3,2,1,0:T(8,128)} %bitcast.148, bf16[24,4,384,384]{2,3,1,0:T(8,128)(2,1)} %divide_convert_fusion), kind=kOutput, calls=%fused_computation.90 | convolution fusion | flops 5436997632 | bytes 35389440 | tf_op jit(solution)/shard_map/transpose(jvp(ihjk,ikhd->ijhd))/dot_general | solution.py:64
  425.0 36.5 %fusion.5 = (f32[24,4,384]{2,1,0:T(4,128)S(1)}, bf16[24,4,384,384]{2,3,1,0:T(8,128)(2,1)}) fusion(f32[24,4,384,384]{2,3,1,0:T(8,128)} %get-tuple-element.141, f32[24,4,384]{2,1,0:T(4,128)S(1)} %copy-done.27, f32[24,4,32,384]{3,2,1,0:T(8,128)S(1)} %bitcast.149, bf16[24,384,4,32]{1,3,2,0:T(8,128)(2,1)S(1)} %bitcast.151), kind=kOutput, calls=%fused_computation.7 | convolution fusion | flops 5506560000 | bytes 92307456 | tf_op jit(solution)/shard_map/transpose(jvp(ihjk,ikhd->ijhd))/dot_general | solution.py:64
  461.6 37.7 %fusion.53 = bf16[24,4,384,32]{2,3,1,0:T(8,128)(2,1)} fusion(bf16[24,384,4,32]{1,3,2,0:T(8,128)(2,1)} %bitcast.158, f32[24,4,384,384]{2,3,1,0:T(8,128)} %get-tuple-element.141, bf16[24,4,384,384]{2,3,1,0:T(8,128)(2,1)} %get-tuple-element.154, f32[24,4,384]{2,1,0:T(4,128)S(1)} %neg.36, f32[24,4,384]{2,1,0:T(4,128)S(1)} %copy-done.19), kind=kOutput, calls=%fused_computation.88 | convolution fusion | flops 5507776512 | bytes 89948160 | tf_op jit(solution)/shard_map/transpose(jvp(ijhd,ikhd->ihjk))/dot_general | solution.py:61
  499.3 46.9 %fusion.50 = bf16[24,4,384,32]{2,3,1,0:T(8,128)(2,1)} fusion(bf16[24,384,4,32]{1,3,2,0:T(8,128)(2,1)S(1)} %bitcast.160, f32[24,4,384,384]{2,3,1,0:T(8,128)} %get-tuple-element.141, bf16[24,4,384,384]{2,3,1,0:T(8,128)(2,1)} %get-tuple-element.154, f32[24,4,384]{2,1,0:T(4,128)S(1)} %neg.36, f32[24,4,384]{2,1,0:T(4,128)S(1)} %copy-done.19), kind=kOutput, calls=%fused_computation.87 | convolution fusion | flops 5507776512 | bytes 89948160 | tf_op jit(solution)/shard_map/transpose(jvp(ijhd,ikhd->ihjk))/dot_general | solution.py:61
  546.2 28.1 %fusion.108 = f32[4,384,384]{1,2,0:T(8,128)} fusion(f32[24,4,384,384]{2,3,1,0:T(8,128)} %get-tuple-element.141, f32[24,4,384]{2,1,0:T(4,128)S(1)} %neg.36, f32[24,4,384]{2,1,0:T(4,128)S(1)} %copy-done.19, bf16[24,4,384,384]{2,3,1,0:T(8,128)(2,1)} %get-tuple-element.154), kind=kLoop, calls=%fused_computation.202 | loop fusion | flops 70189056 | bytes 87588864 | tf_op jit(solution)/shard_map/transpose(jvp())/reduce_sum | solution.py:62
  586.0 10.6 %fusion.72 = bf16[128,512]{1,0:T(8,128)(2,1)S(1)} fusion(bf16[24,384,128]{1,2,0:T(8,128)(2,1)S(1)} %copy-done.6, f32[24,384,128]{2,1,0:T(8,128)} %get-tuple-element.127, bf16[24,384,128]{2,1,0:T(8,128)(2,1)} %copy.195, bf16[24,384,128]{2,1,0:T(8,128)(2,1)} %copy.193, bf16[24,384,128]{2,1,0:T(8,128)(2,1)} %copy.191), kind=kOutput, calls=%fused_computation.109 | convolution fusion | flops 7276134400 | bytes 14286848 | tf_op jit(solution)/shard_map/transpose(jvp(ijc,cd->ijd))/dot_general | solution.py:32
  596.7 13.4 %fusion.18 = f32[24,384,128]{1,2,0:T(8,128)} fusion(f32[24,384,128]{2,1,0:T(8,128)} %get-tuple-element.127, bf16[24,384,128]{2,1,0:T(8,128)(2,1)S(1)} %copy-done.16, bf16[24,384,128]{2,1,0:T(8,128)(2,1)S(1)} %copy-done.17, bf16[24,384,128]{2,1,0:T(8,128)(2,1)S(1)} %copy-done.15, bf16[128,1152]{0,1:T(8,128)(2,1)} %copy-done.20), kind=kOutput, calls=%fused_computation.30 | convolution fusion | flops 7276068864 | bytes 16646144 | tf_op jit(solution)/shard_map/transpose(jvp(ijc,cd->ijd))/dot_general | solution.py:32
  626.8 51.0 %reduce-scatter.12.cloned.1.call-done = f32[32,64]{1,0:T(8,128)} async-done(((f32[512,64]{1,0:T(8,128)}), f32[32,64]{1,0:T(8,128)}) %reduce-scatter.12.cloned.1.call-update) | async-done | bytes 8208
  678.9 12.0 %reduce-scatter.10.cloned.1.call-done = bf16[576,128]{1,0:T(8,128)(2,1)} async-done(((bf16[1152,128]{1,0:T(8,128)(2,1)}), bf16[576,128]{1,0:T(8,128)(2,1)}) %reduce-scatter.10.cloned.1.call-update) | async-done | bytes 147472
  692.0 76.4 %all-reduce.10 = (f32[128,576]{1,0:T(8,128)S(1)}, bf16[4,384,384]{2,0,1:T(4,128)(2,1)}) all-reduce(bf16[128,576]{1,0:T(8,128)(2,1)S(1)} %copy.225, f32[4,384,384]{2,0,1:T(4,128)} %copy.198), channel_id=3, replica_groups=mesh['crop'=2,'row'=16] {'row'}, use_global_device_ids=true, to_apply=%region_22.23.clone | all-reduce | flops 663552 | bytes 3981312
  775.1 37.1 %all-reduce.7 = (f32[128]{0:T(128)S(1)}, f32[1152]{0:T(1024)S(1)}, f32[512]{0:T(512)S(1)}, f32[128]{0:T(128)S(1)}) all-reduce(f32[128]{0:T(128)S(1)} %fusion.90, f32[1152]{0:T(1024)S(1)} %add_dynamic-update-slice_fusion, f32[512]{0:T(512)S(1)} %fusion.92, f32[128]{0:T(128)S(1)} %fusion.94), channel_id=1, replica_groups=mesh['crop'=2,'row'=16] {'crop','row'}, use_global_device_ids=true, to_apply=%region_24.25 | all-reduce | flops 1920 | bytes 15360 | tf_op jit(solution)/shard_map/psum | solution.py:192
  816.4 42.2 %all-reduce.6 = (f32[]{:T(128)}, f32[]{:T(128)}, f32[]{:T(128)}, f32[3,128]{1,0:T(4,128)S(1)}, f32[128,68]{0,1:T(8,128)S(1)}) all-reduce(f32[]{:T(128)S(6)} %neg.31, f32[]{:T(128)} %multiply_reduce_fusion.6, f32[]{:T(128)} %multiply_reduce_fusion.3, ...), channel_id=1, replica_groups=mesh['crop'=2,'row'=16] {'crop','row'}, use_global_device_ids=true, to_apply=%region_12.13 | all-reduce | flops 9091 | bytes 72728 | tf_op jit(solution)/shard_map/psum | solution.py:144
  (263 shorter events, 151.3 us)
Async XLA Ops:
  7.2 157.0 %all-gather.2.cloned.1.call-start = ((), (), s32[]{:S(2)}) async-start(), calls=%async_computation.3 | async-start | bytes 1253376 | tf_op jit(solution)/shard_map/all_gather | solution.py:131
  12.3 272.8 %copy-start.2 = (bf16[1,24,384,128]{2,3,1,0:T(8,128)(2,1)}, bf16[1,24,384,128]{2,3,1,0:T(8,128)(2,1)S(1)}, u32[]{:S(2)}) copy-start(bf16[1,24,384,128]{2,3,1,0:T(8,128)(2,1)S(1)} %copy.168) | copy-start | bytes 7077892
  12.8 50.9 %copy-start.47 = (f32[8,576]{1,0:T(8,128)S(1)}, f32[8,576]{1,0:T(8,128)}, u32[]{:S(2)}) copy-start(f32[8,576]{1,0:T(8,128)} %param.18) | copy-start | bytes 55300
  17.2 601.1 %reduce-scatter.8.cloned.1.call-start = ((), (), s32[]{:S(2)}) async-start(), calls=%async_computation.4 | async-start | bytes 196608 | tf_op jit(solution)/shard_map/reduce_scatter | solution.py:155
  20.6 121.2 %copy-start.43 = (pred[24,384]{1,0:T(8,128)(4,1)}, pred[24,384]{1,0:T(8,128)(4,1)S(1)}, u32[]{:S(2)}) copy-start(pred[24,384]{1,0:T(8,128)(4,1)S(1)} %get-tuple-element.125) | copy-start | bytes 27652
  115.1 257.0 %copy-start.20 = (bf16[128,1152]{0,1:T(8,128)(2,1)}, bf16[128,1152]{0,1:T(8,128)(2,1)S(1)}, u32[]{:S(2)}) copy-start(bf16[128,1152]{0,1:T(8,128)(2,1)S(1)} %all_gather.16) | copy-start | bytes 884740
  141.8 165.0 %copy-start.32 = (f32[24,384]{1,0:T(8,128)}, f32[24,384]{1,0:T(8,128)S(1)}, u32[]{:S(2)}) copy-start(f32[24,384]{1,0:T(8,128)S(1)} %broadcast_select_fusion) | copy-start | bytes 110596
  610.2 67.6 %reduce-scatter.12.cloned.1.call-start = ((), (), s32[]{:S(2)}) async-start(), calls=%async_computation.6 | async-start | bytes 278528
  615.7 63.1 %copy-start.66 = (f32[64]{0:T(128)S(1)}, f32[64]{0:T(128)}, u32[]{:S(2)}) copy-start(f32[64]{0:T(128)} %param.23) | copy-start | bytes 772
  615.7 63.2 %copy-start.67 = (f32[32]{0:T(128)S(1)}, f32[32]{0:T(128)}, u32[]{:S(2)}) copy-start(f32[32]{0:T(128)} %param.22) | copy-start | bytes 388
  620.0 71.0 %reduce-scatter.10.cloned.1.call-start = ((), (), s32[]{:S(2)}) async-start(), calls=%async_computation.5 | async-start | bytes 442368
  622.4 148.6 %copy-start.3 = (bf16[1,24,384,128]{2,3,1,0:T(8,128)(2,1)S(1)}, bf16[1,24,384,128]{2,3,1,0:T(8,128)(2,1)}, u32[]{:S(2)}) copy-start(bf16[1,24,384,128]{2,3,1,0:T(8,128)(2,1)} %copy-done.2) | copy-start | bytes 7077892
  622.4 148.6 %copy-start.26 = (f32[24,384]{1,0:T(8,128)S(1)}, f32[24,384]{1,0:T(8,128)}, u32[]{:S(2)}) copy-start(f32[24,384]{1,0:T(8,128)} %copy-done.25) | copy-start | bytes 110596
  622.4 148.6 %copy-start.31 = (f32[24,384]{1,0:T(8,128)S(1)}, f32[24,384]{1,0:T(8,128)}, u32[]{:S(2)}) copy-start(f32[24,384]{1,0:T(8,128)} %copy-done.30) | copy-start | bytes 110596
  768.4 92.4 %copy-start.64 = (f32[3,128]{1,0:T(4,128)S(1)}, f32[3,128]{1,0:T(4,128)}, u32[]{:S(2)}) copy-start(f32[3,128]{1,0:T(4,128)} %param.25) | copy-start | bytes 4612
  768.4 93.7 %copy-start.48 = (f32[8,576]{1,0:T(8,128)S(1)}, f32[8,576]{1,0:T(8,128)}, u32[]{:S(2)}) copy-start(f32[8,576]{1,0:T(8,128)} %param.18) | copy-start | bytes 55300
  768.5 94.4 %copy-start.51 = (f32[128,68]{0,1:T(8,128)S(1)}, f32[128,68]{0,1:T(8,128)}, u32[]{:S(2)}) copy-start(f32[128,68]{0,1:T(8,128)} %param.27) | copy-start | bytes 104452
  768.5 95.7 %copy-start.59 = (f32[3,128]{1,0:T(4,128)S(1)}, f32[3,128]{1,0:T(4,128)}, u32[]{:S(2)}) copy-start(f32[3,128]{1,0:T(4,128)} %param.24) | copy-start | bytes 4612
  768.5 96.3 %copy-start.41 = (f32[128,68]{0,1:T(8,128)S(1)}, f32[128,68]{0,1:T(8,128)}, u32[]{:S(2)}) copy-start(f32[128,68]{0,1:T(8,128)} %param.26) | copy-start | bytes 104452
  774.8 90.6 %copy-start.34 = (f32[8,576]{1,0:T(8,128)}, f32[8,576]{1,0:T(8,128)S(1)}, u32[]{:S(2)}) copy-start(f32[8,576]{1,0:T(8,128)S(1)} %get-tuple-element.121) | copy-start | bytes 55300
  812.8 52.6 %copy-start.63 = (f32[8]{0:T(128)}, f32[8]{0:T(128)S(1)}, u32[]{:S(2)}) copy-start(f32[8]{0:T(128)S(1)} %dynamic_slice.12) | copy-start | bytes 100
  812.9 52.6 %copy-start.61 = (f32[64]{0:T(128)}, f32[64]{0:T(128)S(1)}, u32[]{:S(2)}) copy-start(f32[64]{0:T(128)S(1)} %dynamic_slice.15) | copy-start | bytes 772
  813.5 51.9 %copy-start.62 = (f32[32]{0:T(128)}, f32[32]{0:T(128)S(1)}, u32[]{:S(2)}) copy-start(f32[32]{0:T(128)S(1)} %dynamic_slice.14) | copy-start | bytes 388
  813.6 51.8 %copy-start.52 = (f32[576]{0:T(1024)}, f32[576]{0:T(1024)S(1)}, u32[]{:S(2)}) copy-start(f32[576]{0:T(1024)S(1)} %dynamic-slice_add_fusion) | copy-start | bytes 6916
  (57 other events, 837.0 us)
Sparse Core Ops, SparseCore 0:
  17.4 41.0 all-gather.1
  610.3 7.9 reduce-scatter.7
  622.5 55.3 reduce-scatter.11
  679.9 11.0 reduce-scatter.9
where the time goes:
time: 878 us; the launch traced here: 872 us
  matrix products  325 us (37%)
  blocking collectives  249 us (28%)
  other arithmetic  146 us (17%)
  waiting for transfers between devices  65.8 us (7%)
  local copies, waits for them, and re-layouts  63.4 us (7%)
  between operations  22.5 us (3%)
    dot_general x3, matrix products, rest(): jnp.einsum('ijhd,ikhd->ihjk', qh, kh, precision=HIGH)  107 us
    psum x2, blocking collectives, body(): lax.psum((loss_local, jnp.sum(mask)), ('crop', 'row'))  84.6 us
    dot_general x3, matrix products, rest(): jnp.einsum('ihjk,ikhd->ijhd', probs, vh, precision=HIGH)  83.8 us
    unnamed x1, blocking collectives  76.4 us
    unnamed x6, waiting for transfers between devices  63.1 us
    sub x1, other arithmetic, rest(): probs = rounded(jax.nn.softmax(score, -1))  58.8 us
    psum x1, blocking collectives, body(): lax.psum((wide_r_term, wide_c_term, down_r_term, down_c_term, gain_terms,...  37.1 us
    dot_general x3, matrix products, rest(): jnp.einsum('ijc,cd->ijd', zb2, w_in, precision=HIGH)  36.2 us
  transfers between devices with their start and end apart: 4, of which 3 were waited for; matrix products, arithmetic and copies ran while one was open for 7% of the time, Pallas kernels for 0%

commit v1 on v0

v1 whole, which is shorter than its diff:
```python
import math

import jax
import jax.numpy as jnp
from jax import lax
from jax.experimental import pallas as pl
from jax.experimental.pallas import tpu as pltpu
from jax.sharding import PartitionSpec as P

CZ = 128
HEADS = 4
HEAD_DIM = 32
FF = 512
BINS = 64
WIDE = 5 * CZ + FF

DECAY = 1.0 - 10.0 ** (-0.8)
TINY = 1e-30
LOG2E = math.log2(math.e)
ROOT = 1.0 / math.sqrt(HEAD_DIM)
BLK = 256

f32 = jnp.float32
bf16 = jnp.bfloat16


def dot(a, b):
    return lax.dot_general(a, b, (((1,), (0,)), ((), ())), preferred_element_type=f32)


def dot_nt(a, b):
    return lax.dot_general(a, b, (((1,), (1,)), ((), ())), preferred_element_type=f32)


def rounded(v):
    return v.astype(bf16).astype(f32)


def halves(v):
    high = v.astype(bf16)
    return high, (v - high.astype(f32)).astype(bf16)


def normed(x):
    centre = x - jnp.sum(x, 0, keepdims=True) * (1.0 / CZ)
    var = jnp.sum(centre * centre, 0, keepdims=True) * (1.0 / CZ)
    inv = lax.rsqrt(var + 1e-05)
    return centre * inv, inv


def normed_back(d, xhat, inv):
    one = jnp.sum(d, 0, keepdims=True) * (1.0 / CZ)
    two = jnp.sum(d * xhat, 0, keepdims=True) * (1.0 / CZ)
    return inv * (d - one - xhat * two)


def sigmoid(x):
    return 0.5 * jnp.tanh(0.5 * x) + 0.5


def front_kernel(pair_ref, gain_ref, wb_ref, zt_ref, zbt_ref, bias_ref):
    x = pair_ref[0].astype(f32).T
    zt_ref[0] = x.astype(bf16)
    xhat, _ = normed(x)
    zb = (xhat * gain_ref[...]).astype(bf16)
    zbt_ref[0] = zb
    bias_ref[0] = dot(wb_ref[...], zb)[:HEADS].astype(bf16)


def middle_kernel(
    order_ref,
    scale_ref,
    bias_ref,
    kb_ref,
    wide_ref,
    down_ref,
    head_ref,
    g1_ref,
    g2_ref,
    zt_ref,
    zbt_ref,
    tgt_ref,
    msk_ref,
    p_ref,
    qkvd_ref,
    dgt_ref,
    dd_ref,
    dwo_ref,
    dwin_ref,
    ddown_ref,
    dhead_ref,
    loss_ref,
    biast,
    nat,
    wqt,
    wot,
    wint,
    wdownt,
    wht,
    wo2,
    wdown2,
    wh2,
    qbd,
):
    width = zt_ref.shape[2]
    shards, _, rows, _ = bias_ref.shape

    @pl.when(pl.program_id(0) == 0)
    def _():
        for h in range(HEADS):
            for s in range(shards):
                nat[s * rows : (s + 1) * rows, :] = bias_ref[order_ref[s], h].astype(f32)
            biast[:, h * width : (h + 1) * width] = (nat[...] * LOG2E + kb_ref[...]).T
        wide = wide_ref[...].astype(f32)
        wqt[...] = wide[:, : 4 * CZ].T.astype(bf16)
        wot[...] = wide[:, 4 * CZ : 5 * CZ].T.astype(bf16)
        wint[...] = wide[:, 5 * CZ :].T.astype(bf16)
        wdownt[...] = down_ref[...].astype(f32).T.astype(bf16)
        wht[...] = head_ref[...].astype(f32).T.astype(bf16)
        wo = wide_ref[:, 4 * CZ : 5 * CZ]
        wo2[...] = jnp.concatenate([wo, wo], 1)
        wdown2[...] = jnp.concatenate([down_ref[...], down_ref[...]], 1)
        wh2[...] = jnp.concatenate([head_ref[...], head_ref[...]], 1)
        qbd[...] = jnp.zeros_like(qbd)
        dwo_ref[...] = jnp.zeros_like(dwo_ref)
        dwin_ref[...] = jnp.zeros_like(dwin_ref)
        ddown_ref[...] = jnp.zeros_like(ddown_ref)
        dhead_ref[...] = jnp.zeros_like(dhead_ref)
        loss_ref[...] = jnp.zeros_like(loss_ref)

    proj = dot(wqt[...], zbt_ref[0])
    q = proj[:CZ].astype(bf16)
    k = proj[CZ : 2 * CZ].astype(bf16)
    v = proj[2 * CZ : 3 * CZ].astype(bf16)
    gate = sigmoid(proj[3 * CZ :])
    qkvd_ref[0, :CZ] = q
    qkvd_ref[0, CZ : 2 * CZ] = k
    qkvd_ref[0, 2 * CZ : 3 * CZ] = v
    kn = k.T
    kk = jnp.concatenate([kn, kn], 1)
    high, low = halves(q.astype(f32) * (LOG2E * ROOT))
    for h in range(HEADS):
        a, b = h * HEAD_DIM, (h + 1) * HEAD_DIM
        qbd[a:b, h * width : (h + 1) * width] = high[a:b]
        qbd[CZ + a : CZ + b, h * width : (h + 1) * width] = low[a:b]
    for c in range(0, HEADS * width, BLK):
        s = dot(kk, qbd[:, c : c + BLK]) + biast[:, c : c + BLK]
        e = jnp.exp2(s - jnp.max(s, 0, keepdims=True))
        r = 1.0 / jnp.sum(e, 0, keepdims=True)
        p_ref[0, :, c : c + BLK] = (e * r).astype(bf16)
    o = jnp.concatenate(
        [
            dot(v[h * HEAD_DIM : (h + 1) * HEAD_DIM], p_ref[0, :, h * width : (h + 1) * width])
            for h in range(HEADS)
        ],
        0,
    )
    og = (o * gate).astype(bf16)

    z1 = zt_ref[0].astype(f32) + dot(wot[...], og)
    xhat1, inv1 = normed(z1)
    zb2 = (xhat1 * g1_ref[...]).astype(bf16)
    hid = dot(wint[...], zb2)
    sg = sigmoid(hid)
    a = (hid * sg).astype(bf16)
    z2 = z1 + dot(wdownt[...], a)
    xhat2, inv2 = normed(z2)
    zb3 = (xhat2 * g2_ref[...]).astype(bf16)
    logits = dot(wht[...], zb3)
    top = jnp.max(logits, 0, keepdims=True)
    ex = jnp.exp(logits - top)
    total = jnp.sum(ex, 0, keepdims=True)
    hot = lax.broadcasted_iota(jnp.int32, logits.shape, 0) == tgt_ref[0]
    picked = jnp.sum(jnp.where(hot, logits, 0.0), 0, keepdims=True)
    mask = msk_ref[0]
    loss_ref[...] += (jnp.log(total) + top - picked) * mask

    weight = mask * scale_ref[0]
    dl = ex * (weight / total) - jnp.where(hot, weight, 0.0)
    dl2 = jnp.concatenate(halves(dl), 0)
    dhead_ref[...] += dot_nt(dl2, zb3)
    dzb3 = rounded(dot(wh2[...], dl2))
    dz2 = normed_back(dzb3 * g2_ref[...], xhat2, inv2)
    high2, low2 = halves(dz2)
    da = rounded(dot(wdown2[...], jnp.concatenate([high2, low2], 0)))
    dh = (da * (sg * (1.0 + hid * (1.0 - sg)))).astype(bf16)
    ddown_ref[...] += dot_nt(high2, a)
    dzb2 = rounded(dot(wide_ref[:, 5 * CZ :], dh))
    dwin_ref[...] += dot_nt(zb2, dh)
    dz1 = dz2 + normed_back(dzb2 * g1_ref[...], xhat1, inv1)
    high1, low1 = halves(dz1)
    dwo_ref[...] += dot_nt(og, high1)
    dog = rounded(dot(wo2[...], jnp.concatenate([high1, low1], 0)))
    do = dog * gate
    doo = do * o
    dgt_ref[0] = (doo * (1.0 - gate)).astype(bf16)
    qkvd_ref[0, 3 * CZ :] = do.astype(bf16)
    for h in range(HEADS):
        dd_ref[0, :, h * width : (h + 1) * width] = jnp.sum(
            doo[h * HEAD_DIM : (h + 1) * HEAD_DIM], 0, keepdims=True
        )


def back_kernel(
    p_ref, qkvd_ref, dgt_ref, dd_ref, zbt_ref, dbias_ref, dwq_ref, acc, dobd, dst
):
    width = zbt_ref.shape[2]
    step = pl.program_id(0)

    @pl.when(step == 0)
    def _():
        dobd[...] = jnp.zeros_like(dobd)
        acc[...] = jnp.zeros_like(acc)
        dwq_ref[...] = jnp.zeros_like(dwq_ref)

    q = qkvd_ref[0, :CZ]
    k = qkvd_ref[0, CZ : 2 * CZ]
    v = qkvd_ref[0, 2 * CZ : 3 * CZ]
    do = qkvd_ref[0, 3 * CZ :]
    vv = jnp.concatenate([v.T, jnp.ones((width, CZ), bf16)], 1)
    minus = -dd_ref[0]
    high = rounded(minus)
    dobd[CZ : CZ + 16, :] = jnp.concatenate(
        [high, minus - high, jnp.zeros((14, HEADS * width), f32)], 0
    ).astype(bf16)
    for h in range(HEADS):
        a, b = h * HEAD_DIM, (h + 1) * HEAD_DIM
        dobd[a:b, h * width : (h + 1) * width] = do[a:b]
    for c in range(0, HEADS * width, BLK):
        ds = dot(vv, dobd[:, c : c + BLK]) * p_ref[0, :, c : c + BLK].astype(f32)
        acc[:, c : c + BLK] += ds
        dst[:, c : c + BLK] = ds.astype(bf16)
    dq, dk, dv = [], [], []
    for h in range(HEADS):
        a, b = h * HEAD_DIM, (h + 1) * HEAD_DIM
        mine = dst[:, h * width : (h + 1) * width]
        dq.append(dot(k[a:b], mine) * ROOT)
        dk.append(dot_nt(q[a:b], mine) * ROOT)
        dv.append(dot_nt(do[a:b], p_ref[0, :, h * width : (h + 1) * width]))
    dproj = jnp.concatenate(dq + dk + dv, 0).astype(bf16)
    dproj = jnp.concatenate([dproj, dgt_ref[0]], 0)
    dwq_ref[...] += dot_nt(zbt_ref[0], dproj)

    @pl.when(step == pl.num_programs(0) - 1)
    def _():
        for h in range(HEADS):
            dbias_ref[h] = acc[:, h * width : (h + 1) * width].T.astype(bf16)


def whole(shape):
    return pl.BlockSpec(shape, lambda i: (0,) * len(shape))


def by_row(shape):
    return pl.BlockSpec((1,) + shape, lambda i: (i,) + (0,) * len(shape))


SMEM = pl.BlockSpec(memory_space=pltpu.SMEM)
PARAMS = pltpu.CompilerParams(vmem_limit_bytes=56 * 1024 * 1024)


def front(pair, gain, w_bias):
    count_rows, width = pair.shape[0], pair.shape[1]
    return pl.pallas_call(
        front_kernel,
        grid=(count_rows,),
        in_specs=[by_row((width, CZ)), whole((CZ, width)), whole((16, CZ))],
        out_specs=[by_row((CZ, width)), by_row((CZ, width)), by_row((HEADS, width))],
        out_shape=[
            jax.ShapeDtypeStruct((count_rows, CZ, width), bf16),
            jax.ShapeDtypeStruct((count_rows, CZ, width), bf16),
            jax.ShapeDtypeStruct((count_rows, HEADS, width), bf16),
        ],
        compiler_params=PARAMS,
        name="front",
    )(pair, gain, w_bias)


def middle(order, scale, bias, kb, wide, down, head, g1, g2, zt, zbt, tgt, msk):
    count_rows, _, width = zt.shape
    return pl.pallas_call(
        middle_kernel,
        grid=(count_rows,),
        in_specs=[
            SMEM,
            SMEM,
            whole(bias.shape),
            whole((1, width)),
            whole((CZ, WIDE)),
            whole((FF, CZ)),
            whole((CZ, BINS)),
            whole((CZ, width)),
            whole((CZ, width)),
            by_row((CZ, width)),
            by_row((CZ, width)),
            by_row((1, width)),
            by_row((1, width)),
        ],
        out_specs=[
            by_row((width, HEADS * width)),
            by_row((4 * CZ, width)),
            by_row((CZ, width)),
            by_row((1, HEADS * width)),
            whole((CZ, CZ)),
            whole((CZ, FF)),
            whole((CZ, FF)),
            whole((2 * BINS, CZ)),
            whole((1, width)),
        ],
        out_shape=[
            jax.ShapeDtypeStruct((count_rows, width, HEADS * width), bf16),
            jax.ShapeDtypeStruct((count_rows, 4 * CZ, width), bf16),
            jax.ShapeDtypeStruct((count_rows, CZ, width), bf16),
            jax.ShapeDtypeStruct((count_rows, 1, HEADS * width), f32),
            jax.ShapeDtypeStruct((CZ, CZ), f32),
            jax.ShapeDtypeStruct((CZ, FF), f32),
            jax.ShapeDtypeStruct((CZ, FF), f32),
            jax.ShapeDtypeStruct((2 * BINS, CZ), f32),
            jax.ShapeDtypeStruct((1, width), f32),
        ],
        scratch_shapes=[
            pltpu.VMEM((width, HEADS * width), f32),
            pltpu.VMEM((width, width), f32),
            pltpu.VMEM((4 * CZ, CZ), bf16),
            pltpu.VMEM((CZ, CZ), bf16),
            pltpu.VMEM((FF, CZ), bf16),
            pltpu.VMEM((CZ, FF), bf16),
            pltpu.VMEM((BINS, CZ), bf16),
            pltpu.VMEM((CZ, 2 * CZ), bf16),
            pltpu.VMEM((FF, 2 * CZ), bf16),
            pltpu.VMEM((CZ, 2 * BINS), bf16),
            pltpu.VMEM((2 * CZ, HEADS * width), bf16),
        ],
        compiler_params=PARAMS,
        name="middle",
    )(order, scale, bias, kb, wide, down, head, g1, g2, zt, zbt, tgt, msk)


def back(p, qkvd, dgt, dd, zbt):
    count_rows, _, width = zbt.shape
    return pl.pallas_call(
        back_kernel,
        grid=(count_rows,),
        in_specs=[
            by_row((width, HEADS * width)),
            by_row((4 * CZ, width)),
            by_row((CZ, width)),
            by_row((1, HEADS * width)),
            by_row((CZ, width)),
        ],
        out_specs=[whole((HEADS, width, width)), whole((CZ, 4 * CZ))],
        out_shape=[
            jax.ShapeDtypeStruct((HEADS, width, width), bf16),
            jax.ShapeDtypeStruct((CZ, 4 * CZ), f32),
        ],
        scratch_shapes=[
            pltpu.VMEM((width, HEADS * width), f32),
            pltpu.VMEM((2 * CZ, HEADS * width), bf16),
            pltpu.VMEM((width, HEADS * width), bf16),
        ],
        compiler_params=PARAMS,
        name="back",
    )(p, qkvd, dgt, dd, zbt)


def bits(n):
    return [1 << t for t in reversed(range(n.bit_length() - 1))]


def swap(x, axes, size, mask):
    return lax.ppermute(x, axes, [(i, i ^ mask) for i in range(size)])


def gathered(x, axes, size, masks):
    x = x[None]
    for mask in masks:
        x = jnp.concatenate([x, swap(x, axes, size, mask)], 0)
    return x


def places(me, size, masks):
    apart = jnp.arange(size, dtype=jnp.int32) ^ me
    place = jnp.zeros((size,), jnp.int32)
    for t, mask in enumerate(masks):
        place = place + jnp.where((apart & mask) != 0, 1 << t, 0)
    return place


def summed(x, axes, size, masks):
    for mask in masks:
        x = x + swap(x, axes, size, mask)
    return x


def plain(weight, grad, second, rate):
    second_new = DECAY * second + (1.0 - DECAY) * (grad * grad + TINY)
    update = grad * lax.rsqrt(second_new)
    clip = jnp.maximum(1.0, jnp.sqrt(jnp.mean(update * update)))
    return (second_new, weight - rate * update / clip)


def factored(grad_all, rows_all, cols_all, grad, weight, row_start, col_start):
    sq = grad_all * grad_all
    rows_new = DECAY * rows_all + (1.0 - DECAY) * (jnp.mean(sq, 1) + TINY)
    cols_new = DECAY * cols_all + (1.0 - DECAY) * (jnp.mean(sq, 0) + TINY)
    mean = jnp.mean(rows_new)
    size = jnp.mean(sq * (mean / (rows_new[:, None] * cols_new[None, :])))
    clip = jnp.maximum(0.1, jnp.sqrt(size))
    rows_mine = lax.dynamic_slice_in_dim(rows_new, row_start, grad.shape[0])
    cols_mine = lax.dynamic_slice_in_dim(cols_new, col_start, grad.shape[1])
    second = rows_mine[:, None] * cols_mine[None, :] / mean
    return rows_mine, cols_mine, weight - 0.03 * (grad * lax.rsqrt(second)) / clip


def build(crops, rows):
    both = ("crop", "row")
    devices = crops * rows
    row_masks = bits(rows)
    all_masks = row_masks[:-1] + [m * rows for m in bits(crops)] + row_masks[-1:]

    def split(x):
        r, c = x.shape[0] // rows, x.shape[1] // crops
        return x.reshape(rows, r, crops, c).transpose(2, 0, 1, 3).reshape(devices, r * c)

    def joined(x, r, c):
        return x.reshape(crops, rows, r, c).transpose(1, 2, 0, 3).reshape(rows * r, crops * c)

    def body(
        pair,
        crop_len,
        targets,
        neighbours,
        wide,
        wide_rows,
        wide_cols,
        down,
        down_rows,
        down_cols,
        gains,
        gain_second,
        small,
        small_second,
    ):
        row_index = lax.axis_index("row")
        crop_index = lax.axis_index("crop")
        me = crop_index * rows + row_index
        count_rows, width = pair.shape[1], pair.shape[2]
        length = crop_len[0]
        columns = jnp.arange(width, dtype=jnp.int32)
        valid_col = columns < length
        valid_row = row_index * count_rows + jnp.arange(count_rows, dtype=jnp.int32) < length
        mask = (valid_row[:, None] & valid_col[None, :] & (neighbours[0] > 0)).astype(f32)
        kb = jnp.where(valid_col, 0.0, -1000000000.0 * LOG2E).astype(f32)[None, :]

        wide_size, down_size = wide.size, down.size
        stat_size = wide_rows.size + wide_cols.size + down_rows.size + down_cols.size
        count = jnp.sum(mask)
        digit = jnp.floor(count * (1.0 / 128.0))
        sizes = wide_size + down_size
        pad = -(sizes + 2) % 1024
        packed = jnp.concatenate(
            [
                wide.astype(bf16).reshape(-1),
                down.astype(bf16).reshape(-1),
                jnp.stack([digit, count - 128.0 * digit]).astype(bf16),
                jnp.zeros((pad,), bf16),
            ]
        ).reshape(-1, 128)
        packs = gathered(packed, both, devices, all_masks)
        packs = jnp.take(packs, places(me, devices, all_masks), axis=0).reshape(devices, -1)
        wide_full = joined(packs[:, :wide_size], *wide.shape)
        down_full = joined(packs[:, wide_size:sizes], *down.shape)
        digits = packs[:, sizes : sizes + 2].astype(f32)
        pair_count = jnp.sum(digits[:, 0]) * 128.0 + jnp.sum(digits[:, 1])

        gain_wide = jnp.broadcast_to(gains[:, :, None], (3, CZ, width))
        w_bias = jnp.zeros((16, CZ), bf16).at[:HEADS].set(small[:, :HEADS].T.astype(bf16))
        zt, zbt, bias_part = front(pair[0], gain_wide[0], w_bias)
        bias = gathered(bias_part.transpose(1, 0, 2), "row", rows, row_masks)
        order = places(row_index, rows, row_masks)
        if count_rows % 8:
            bias = jnp.take(bias, order, axis=0).transpose(1, 0, 2, 3)
            bias = bias.reshape(1, HEADS, width, width)
            order = jnp.zeros((1,), jnp.int32)

        p, qkvd, dgt, dd, d_out, d_in, d_down, d_head, loss = middle(
            order,
            (1.0 / pair_count).reshape(1),
            bias,
            kb,
            wide_full,
            down_full,
            small[:, HEADS:].astype(bf16),
            gain_wide[1],
            gain_wide[2],
            zt,
            zbt,
            targets[0][:, None, :],
            mask[:, None, :],
        )
        d_bias, d_qkvg = back(p, qkvd, dgt, dd, zbt)

        parts = d_bias.reshape(HEADS, rows, count_rows, width).transpose(1, 0, 2, 3)
        parts = lax.all_to_all(parts, "row", 0, 0, tiled=True)
        mine = jnp.sum(parts.astype(f32), 0).astype(bf16)
        d_pbias = lax.dot_general(
            mine, zbt, (((1, 2), (0, 2)), ((), ())), preferred_element_type=f32
        )

        blocks = jnp.concatenate(
            [split(jnp.concatenate([d_qkvg, d_out, d_in], 1)), split(d_down.T)], 1
        ).astype(bf16)
        blocks = jnp.pad(blocks, ((0, 0), (0, -sizes % 128)))
        own = lax.all_to_all(blocks.reshape(devices, -1, 128), both, 0, 0, tiled=True)
        own = jnp.sum(own.astype(f32), 0)
        grads = gathered(own.astype(bf16), both, devices, all_masks)
        grads = jnp.take(grads, places(me, devices, all_masks), axis=0)
        grads = grads.reshape(devices, -1).astype(f32)
        own = own.reshape(-1)
        wide_g = own[:wide_size].reshape(wide.shape)
        down_g = own[wide_size:sizes].reshape(down.shape)
        wide_all = joined(grads[:, :wide_size], *wide.shape)
        down_all = joined(grads[:, wide_size:sizes], *down.shape)

        few = jnp.concatenate(
            [
                d_head[:BINS] + d_head[BINS:],
                d_pbias,
                jnp.broadcast_to(jnp.sum(loss), (4, CZ)),
            ],
            0,
        )
        few = summed(few, both, devices, all_masks)
        small_grad = jnp.concatenate([few[BINS : BINS + HEADS], few[:BINS]], 0).T
        loss_sum = few[BINS + HEADS, 0]

        stats = jnp.concatenate([wide_rows, wide_cols, down_rows, down_cols])
        stats = gathered(
            jnp.pad(stats, (0, -stat_size % 128)).reshape(-1, 128), both, devices, all_masks
        )
        stats = jnp.take(stats, places(me, devices, all_masks), axis=0).reshape(crops, rows, -1)
        ends = [0, wide_rows.size]
        for part in (wide_cols, down_rows, down_cols):
            ends.append(ends[-1] + part.size)
        wide_rows_all = stats[0, :, ends[0] : ends[1]].reshape(-1)
        wide_cols_all = stats[:, 0, ends[1] : ends[2]].reshape(-1)
        down_rows_all = stats[0, :, ends[2] : ends[3]].reshape(-1)
        down_cols_all = stats[:, 0, ends[3] : ends[4]].reshape(-1)

        wide_w = wide_full.astype(f32)
        small_w = rounded(small)
        through = wide_all * wide_w
        behind = small_grad * small_w
        gain_grad = (
            jnp.stack(
                [
                    jnp.sum(through[:, : 4 * CZ], 1) + jnp.sum(behind[:, :HEADS], 1),
                    jnp.sum(through[:, 5 * CZ :], 1),
                    jnp.sum(behind[:, HEADS:], 1),
                ]
            )
            / gains
        )

        wide_r_new, wide_c_new, wide_new = factored(
            wide_all,
            wide_rows_all,
            wide_cols_all,
            wide_g,
            wide,
            row_index * wide.shape[0],
            crop_index * wide.shape[1],
        )
        down_r_new, down_c_new, down_new = factored(
            down_all,
            down_rows_all,
            down_cols_all,
            down_g,
            down,
            row_index * down.shape[0],
            crop_index * down.shape[1],
        )
        gain_s, gain_n = plain(gains, gain_grad, gain_second, 0.3)
        small_s, small_n = plain(small, small_grad, small_second, 0.03)
        return (
            loss_sum,
            pair_count,
            wide_g,
            wide_r_new,
            wide_c_new,
            wide_new,
            down_g,
            down_r_new,
            down_c_new,
            down_new,
            gain_grad,
            gain_s,
            gain_n,
            small_grad,
            small_s,
            small_n,
        )

    return body


def solution(mesh):
    return jax.shard_map(
        build(mesh.shape["crop"], mesh.shape["row"]),
        mesh=mesh,
        in_specs=(
            P("crop", "row", None, None),
            P("crop"),
            P("crop", "row", None),
            P("crop", "row", None),
            P("row", "crop"),
            P("row"),
            P("crop"),
            P("row", "crop"),
            P("row"),
            P("crop"),
            P(),
            P(),
            P(),
            P(),
        ),
        out_specs=(
            P(),
            P(),
            P("row", "crop"),
            P("row"),
            P("crop"),
            P("row", "crop"),
            P("row", "crop"),
            P("row"),
            P("crop"),
            P("row", "crop"),
            P(),
            P(),
            P(),
            P(),
            P(),
            P(),
        ),
        check_vma=False,
    )
```

time: 878 us -> 315 us (0.36)
  matrix products: 325 us -> 1.68 us
  blocking collectives: 249 us -> 0 us
  Pallas kernels: 0 us -> 143 us
  other arithmetic: 146 us -> 22.1 us
  starting transfers between devices: 0.34 us -> 34.7 us
  local copies, waits for them, and re-layouts: 63.4 us -> 29.9 us
  between operations: 22.5 us -> 10.2 us
    dot_general x24 -> x1, matrix products: 325 us -> 1.68 us  [body(): lax.dot_general(mine, zbt, (((1, 2), (0, 2)), ((), ())), preferred_elemen...]
    pallas_call x0 -> x3, Pallas kernels: none -> 143 us  [the longest x1 85.2 us: middle(): pl.pallas_call(middle_kernel, grid=(count_rows,), in_specs=[SMEM, SMEM, w...]
    psum x3 -> x0, blocking collectives: 122 us -> none  [the longest x2 84.6 us: body(): lax.psum((loss_local, jnp.sum(mask)), ('crop', 'row'))]
    unnamed x1 -> x0, blocking collectives: 76.4 us -> none
    unnamed x6 -> x0, waiting for transfers between devices: 63.1 us -> none
    ppermute x0 -> x24, waiting for transfers between devices: none -> 62.9 us  [swap(): return lax.ppermute(x, axes, [(i, i ^ mask) for i in range(size)])]
    sub x4 -> x2, other arithmetic: 63 us -> 1.38 us  [factored(): weight - 0.03 * (grad * lax.rsqrt(second)) / clip]
    all_gather x4 -> x0, blocking collectives: 51.1 us -> none  [the longest x1 21.5 us: body(): lax.all_gather(down.astype(jnp.bfloat16), 'row', axis=0, tiled=True)]
  transfers between devices with their start and end apart: 4 -> 26, of which waited for: 3 -> 16; matrix products, arithmetic and copies ran while one was open for 7% -> 14% of each run, Pallas kernels for 0% -> 46%
where the time goes in v1:
time: 315 us; the launch traced here: 313 us
  Pallas kernels  143 us (45%)
  waiting for transfers between devices  71.4 us (23%)
  starting transfers between devices  34.7 us (11%)
  local copies, waits for them, and re-layouts  29.9 us (9%)
  other arithmetic  22.1 us (7%)
  between operations  10.2 us (3%)
    pallas_call x1, Pallas kernels, middle(): pl.pallas_call(middle_kernel, grid=(count_rows,), in_specs=[SMEM, SMEM, w...  85.2 us
    ppermute x24, waiting for transfers between devices, swap(): return lax.ppermute(x, axes, [(i, i ^ mask) for i in range(size)])  62.9 us
    pallas_call x1, Pallas kernels, back(): pl.pallas_call(back_kernel, grid=(count_rows,), in_specs=[by_row((width,...  42.1 us
    ppermute x24, starting transfers between devices, swap(): return lax.ppermute(x, axes, [(i, i ^ mask) for i in range(size)])  27.9 us
    pallas_call x1, Pallas kernels, front(): pl.pallas_call(front_kernel, grid=(count_rows,), in_specs=[by_row((width,...  15.7 us
    all_to_all x1, waiting for transfers between devices, body(): lax.all_to_all(blocks.reshape(devices, -1, 128), both, 0, 0, tiled=True)  8.5 us
    unnamed x100, local copies, waits for them, and re-layouts  7.11 us
  transfers between devices with their start and end apart: 26, of which 16 were waited for; matrix products, arithmetic and copies ran while one was open for 14% of the time, Pallas kernels for 46%

profile of v1, /device:TPU:0, one launch (start us, length us, event | category | flops | bytes accessed | tf_op | source)
XLA Modules:
  0.0 313.0 jit_solution(18145095063209815746)
XLA Ops:
  5.8 4.0 %collective-permute-start = (bf16[1,56,128]{2,1,0:T(8,128)(2,1)S(1)}, bf16[1,56,128]{2,1,0:T(8,128)(2,1)S(1)}, u32[]{:S(2)}, u32[]{:S(2)}) collective-permute-start(bf16[1,56,128]{2,1,0:T(8,128)(2,1)S(1)} %bitcast.114), channel_id=1, source_target_pairs={{0,8},{1,9},{2,10},{3,11},{4,12},{5,13},{6,14},{7,15},{8,0},{9,1},... | collective-permute-start | bytes 43016 | tf_op jit(solution)/shard_map/ppermute | solution.py:371
  13.0 15.7 %front.1 = (bf16[24,128,384]{2,1,0:T(8,128)(2,1)}, bf16[24,128,384]{2,1,0:T(8,128)(2,1)}, bf16[24,4,384]{2,1,0:T(4,128)(2,1)}) custom-call(bf16[24,384,128]{2,1,0:T(8,128)(2,1)} %bitcast.101, f32[128,384]{1,0:T(8,128)} %broadcast_in_dim.145.gain_ref, bf16[16,128]{1,0:T(8,128)(2,1)} %scatter.4.clone.wb_ref), custom_call_target="tpu_custom_call" | custom-call | tf_op jit(solution)/shard_map/front/pallas_call | solution.py:264
  30.4 2.9 collective-permute-start.14
  43.2 1.6 collective-permute-start.1
  53.0 3.4 %collective-permute-done.3 = bf16[8,56,128]{2,1,0:T(8,128)(2,1)S(1)} collective-permute-done((bf16[8,56,128]{2,1,0:T(8,128)(2,1)S(1)}, bf16[8,56,128]{2,1,0:T(8,128)(2,1)S(1)}, u32[]{:S(2)}, u32[]{:S(2)}) %collective-permute-start.3) | collective-permute-done | bytes 114720 | tf_op jit(solution)/shard_map/ppermute | solution.py:371
  56.6 1.6 collective-permute-start.7
  58.9 7.1 %collective-permute-done.7 = bf16[4,4,24,384]{3,2,1,0:T(8,128)(2,1)S(1)} collective-permute-done((bf16[4,4,24,384]{3,2,1,0:T(8,128)(2,1)S(1)}, bf16[4,4,24,384]{3,2,1,0:T(8,128)(2,1)S(1)}, u32[]{:S(2)}, u32[]{:S(2)}) %collective-permute-start.7) | collective-permute-done | bytes 294944 | tf_op jit(solution)/shard_map/ppermute | solution.py:371
  74.2 85.2 %middle.1 = (bf16[24,384,1536]{2,1,0:T(8,128)(2,1)}, bf16[24,512,384]{2,1,0:T(8,128)(2,1)}, bf16[24,128,384]{2,1,0:T(8,128)(2,1)}, f32[24,1,1536]{2,1,0:T(1,128)...) custom-call(s32[16]{0:T(128)} %fusion.13.order_ref, ...), custom_call_target="tpu_custom_call" | custom-call | tf_op jit(solution)/shard_map/middle/pallas_call | solution.py:281
  159.5 42.1 %back.1 = (bf16[4,384,384]{2,1,0:T(8,128)(2,1)}, f32[128,512]{1,0:T(8,128)}) custom-call(bf16[24,384,1536]{2,1,0:T(8,128)(2,1)} %get-tuple-element.46.p_ref, bf16[24,512,384]{2,1,0:T(8,128)(2,1)} %get-tuple-element.47.qkvd_ref, bf16[24,128,384]{2,1,0:T(8,128)(2,1)} %get-tuple-element.48.dgt_ref, f32[24,1,1536]{2,1,0:T(1,128)} %get-tuple-element.49.dd_ref, ...), custom_call_target="tpu_custom_call" | custom-call | tf_op jit(solution)/shard_map/back/pallas_call | solution.py:341
  205.3 2.9 all-to-all-start.1
  214.2 8.5 %all-to-all-done.1 = bf16[32,52,128]{2,1,0:T(8,128)(2,1)S(1)} async-done(((bf16[32,52,128]{2,1,0:T(8,128)(2,1)}), bf16[32,52,128]{2,1,0:T(8,128)(2,1)S(1)}, u32[]{:S(2)}, u32[]{:S(2)}) %all-to-all-start.1) | async-done | bytes 426016 | tf_op jit(solution)/shard_map/all_to_all | solution.py:514
  222.7 3.9 %all-to-all-start = ((bf16[16,4,24,384]{3,2,1,0:T(8,128)(2,1)}), bf16[16,4,24,384]{3,2,1,0:T(8,128)(2,1)S(1)}, u32[]{:S(2)}, u32[]{:S(2)}) async-start(bf16[16,4,24,384]{3,2,1,0:T(8,128)(2,1)} %bitcast.93), calls=%async_computation | async-start | bytes 2359296 | tf_op jit(solution)/shard_map/all_to_all | solution.py:504
  226.7 2.8 collective-permute-start.19
  229.5 27.0 %collective-permute-done.19 = bf16[1,52,128]{2,1,0:T(8,128)(2,1)S(1)} collective-permute-done((bf16[1,52,128]{2,1,0:T(8,128)(2,1)S(1)}, bf16[1,52,128]{2,1,0:T(8,128)(2,1)S(1)}, u32[]{:S(2)}, u32[]{:S(2)}) %collective-permute-start.19) | collective-permute-done | bytes 13344 | tf_op jit(solution)/shard_map/ppermute | solution.py:371
  256.5 3.8 %collective-permute-done.20 = bf16[2,52,128]{2,1,0:T(8,128)(2,1)S(1)} collective-permute-done((bf16[2,52,128]{2,1,0:T(8,128)(2,1)S(1)}, bf16[2,52,128]{2,1,0:T(8,128)(2,1)S(1)}, u32[]{:S(2)}, u32[]{:S(2)}) %collective-permute-start.20) | collective-permute-done | bytes 26656 | tf_op jit(solution)/shard_map/ppermute | solution.py:371
  260.4 1.6 collective-permute-start.21
  262.0 2.6 collective-permute-done.21
  265.8 3.8 %collective-permute-done.22 = bf16[8,52,128]{2,1,0:T(8,128)(2,1)S(1)} collective-permute-done((bf16[8,52,128]{2,1,0:T(8,128)(2,1)S(1)}, bf16[8,52,128]{2,1,0:T(8,128)(2,1)S(1)}, u32[]{:S(2)}, u32[]{:S(2)}) %collective-permute-start.22) | collective-permute-done | bytes 106528 | tf_op jit(solution)/shard_map/ppermute | solution.py:371
  279.8 2.2 convert_multiply_fusion
  282.8 1.7 convolution_bitcast_fusion
  286.1 4.8 %collective-permute-done.9 = f32[72,128]{0,1:T(8,128)S(1)} collective-permute-done((f32[72,128]{0,1:T(8,128)S(1)}, f32[72,128]{0,1:T(8,128)S(1)}, u32[]{:S(2)}, u32[]{:S(2)}) %collective-permute-start.9) | collective-permute-done | bytes 36896 | tf_op jit(solution)/shard_map/ppermute | solution.py:371
  291.8 3.5 %collective-permute-done.10 = f32[72,128]{0,1:T(8,128)S(1)} collective-permute-done((f32[72,128]{0,1:T(8,128)S(1)}, f32[72,128]{0,1:T(8,128)S(1)}, u32[]{:S(2)}, u32[]{:S(2)}) %collective-permute-start.10) | collective-permute-done | bytes 36896 | tf_op jit(solution)/shard_map/ppermute | solution.py:371
  295.4 1.6 collective-permute-start.11
  301.5 2.6 collective-permute-done.12
  (274 shorter events, 65.9 us)
Async XLA Ops:
  5.8 37.4 %collective-permute-start = (bf16[1,56,128]{2,1,0:T(8,128)(2,1)S(1)}, bf16[1,56,128]{2,1,0:T(8,128)(2,1)S(1)}, u32[]{:S(2)}, u32[]{:S(2)}) collective-permute-start(bf16[1,56,128]{2,1,0:T(8,128)(2,1)S(1)} %bitcast.114), channel_id=1, source_target_pairs={{0,8},{1,9},{2,10},{3,11},{4,12},{5,13},{6,14},{7,15},{8,0},{9,1},... | collective-permute-start | bytes 43016 | tf_op jit(solution)/shard_map/ppermute | solution.py:371
  29.6 19.8 %collective-permute-start.5 = (bf16[1,4,24,384]{3,2,1,0:T(8,128)(2,1)S(1)}, bf16[1,4,24,384]{3,2,1,0:T(8,128)(2,1)S(1)}, u32[]{:S(2)}, u32[]{:S(2)}) collective-permute-start(bf16[1,4,24,384]{3,2,1,0:T(8,128)(2,1)S(1)} %bitcast.106), channel_id=1, source_target_pairs={{0,8},{1,9},{2,10},{3,11},{4,12},{5,13},{6,14},{7,15},{8,0},{9,1},... | collective-permute-start | bytes 221192 | tf_op jit(solution)/shard_map/ppermute | solution.py:371
  30.4 7.0 %collective-permute-start.14 = (f32[1,6,128]{2,1,0:T(8,128)S(1)}, f32[1,6,128]{2,1,0:T(8,128)S(1)}, u32[]{:S(2)}, u32[]{:S(2)}) collective-permute-start(f32[1,6,128]{2,1,0:T(8,128)S(1)} %get-tuple-element.120), channel_id=1, source_target_pairs={{0,8},{1,9},{2,10},{3,11},{4,12},{5,13},{6,14},{7,15},{8,0},{9,1},... | collective-permute-start | bytes 9224 | tf_op jit(solution)/shard_map/ppermute | solution.py:371
  37.4 3.7 %collective-permute-start.15 = (f32[2,6,128]{2,1,0:T(8,128)S(1)}, f32[2,6,128]{2,1,0:T(8,128)S(1)}, u32[]{:S(2)}, u32[]{:S(2)}) collective-permute-start(f32[2,6,128]{2,1,0:T(8,128)S(1)} %pad_maximum_fusion.13), channel_id=1, source_target_pairs={{0,4},{1,5},{2,6},{3,7},{4,0},{5,1},{6,2},{7,3},{8,12},{9,13},{10,... | collective-permute-start | bytes 18440 | tf_op jit(solution)/shard_map/ppermute | solution.py:371
  41.1 3.8 %collective-permute-start.16 = (f32[4,6,128]{2,1,0:T(8,128)S(1)}, f32[4,6,128]{2,1,0:T(8,128)S(1)}, u32[]{:S(2)}, u32[]{:S(2)}) collective-permute-start(f32[4,6,128]{2,1,0:T(8,128)S(1)} %pad_maximum_fusion.12), channel_id=1, source_target_pairs={{0,2},{1,3},{2,0},{3,1},{4,6},{5,7},{6,4},{7,5},{8,10},{9,11},{10,... | collective-permute-start | bytes 36872 | tf_op jit(solution)/shard_map/ppermute | solution.py:371
  43.2 3.9 %collective-permute-start.1 = (bf16[2,56,128]{2,1,0:T(8,128)(2,1)S(1)}, bf16[2,56,128]{2,1,0:T(8,128)(2,1)S(1)}, u32[]{:S(2)}, u32[]{:S(2)}) collective-permute-start(bf16[2,56,128]{2,1,0:T(8,128)(2,1)S(1)} %pad_maximum_fusion.10), channel_id=1, source_target_pairs={{0,4},{1,5},{2,6},{3,7},{4,0},{5,1},{6,2},{7,3},{8,12},{9,13},{10,... | collective-permute-start | bytes 86024 | tf_op jit(solution)/shard_map/ppermute | solution.py:371
  44.9 4.0 %collective-permute-start.17 = (f32[8,6,128]{2,1,0:T(8,128)S(1)}, f32[8,6,128]{2,1,0:T(8,128)S(1)}, u32[]{:S(2)}, u32[]{:S(2)}) collective-permute-start(f32[8,6,128]{2,1,0:T(8,128)S(1)} %pad_maximum_fusion.9), channel_id=1, source_target_pairs={{0,16},{1,17},{2,18},{3,19},{4,20},{5,21},{6,22},{7,23},{8,24},{9,... | collective-permute-start | bytes 73736 | tf_op jit(solution)/shard_map/ppermute | solution.py:371
  47.1 4.2 %collective-permute-start.2 = (bf16[4,56,128]{2,1,0:T(8,128)(2,1)S(1)}, bf16[4,56,128]{2,1,0:T(8,128)(2,1)S(1)}, u32[]{:S(2)}, u32[]{:S(2)}) collective-permute-start(bf16[4,56,128]{2,1,0:T(8,128)(2,1)S(1)} %pad_maximum_fusion.7), channel_id=1, source_target_pairs={{0,2},{1,3},{2,0},{3,1},{4,6},{5,7},{6,4},{7,5},{8,10},{9,11},{10,... | collective-permute-start | bytes 172040 | tf_op jit(solution)/shard_map/ppermute | solution.py:371
  49.5 159.5 %collective-permute-start.18 = (f32[16,6,128]{2,1,0:T(8,128)}, f32[16,6,128]{2,1,0:T(8,128)S(1)}, u32[]{:S(2)}, u32[]{:S(2)}) collective-permute-start(f32[16,6,128]{2,1,0:T(8,128)} %get-tuple-element.142), channel_id=1, source_target_pairs={{0,1},{1,0},{2,3},{3,2},{4,5},{5,4},{6,7},{7,6},{8,9},{9,8},{10,11... | collective-permute-start | bytes 147464 | tf_op jit(solution)/shard_map/ppermute | solution.py:371
  49.5 7.0 %collective-permute-start.6 = (bf16[2,4,24,384]{3,2,1,0:T(8,128)(2,1)S(1)}, bf16[2,4,24,384]{3,2,1,0:T(8,128)(2,1)S(1)}, u32[]{:S(2)}, u32[]{:S(2)}) collective-permute-start(bf16[2,4,24,384]{3,2,1,0:T(8,128)(2,1)S(1)} %pad_maximum_fusion.4), channel_id=1, source_target_pairs={{0,4},{1,5},{2,6},{3,7},{4,0},{5,1},{6,2},{7,3},{8,12},{9,13},{10,... | collective-permute-start | bytes 442376 | tf_op jit(solution)/shard_map/ppermute | solution.py:371
  51.4 5.0 %collective-permute-start.3 = (bf16[8,56,128]{2,1,0:T(8,128)(2,1)S(1)}, bf16[8,56,128]{2,1,0:T(8,128)(2,1)S(1)}, u32[]{:S(2)}, u32[]{:S(2)}) collective-permute-start(bf16[8,56,128]{2,1,0:T(8,128)(2,1)S(1)} %pad_maximum_fusion.5), channel_id=1, source_target_pairs={{0,16},{1,17},{2,18},{3,19},{4,20},{5,21},{6,22},{7,23},{8,24},{9,... | collective-permute-start | bytes 344072 | tf_op jit(solution)/shard_map/ppermute | solution.py:371
  56.4 1.8 collective-permute-start.4
  56.6 9.5 %collective-permute-start.7 = (bf16[4,4,24,384]{3,2,1,0:T(8,128)(2,1)S(1)}, bf16[4,4,24,384]{3,2,1,0:T(8,128)(2,1)S(1)}, u32[]{:S(2)}, u32[]{:S(2)}) collective-permute-start(bf16[4,4,24,384]{3,2,1,0:T(8,128)(2,1)S(1)} %pad_maximum_fusion.2), channel_id=1, source_target_pairs={{0,2},{1,3},{2,0},{3,1},{4,6},{5,7},{6,4},{7,5},{8,10},{9,11},{10,... | collective-permute-start | bytes 884744 | tf_op jit(solution)/shard_map/ppermute | solution.py:371
  66.1 5.3 %collective-permute-start.8 = (bf16[8,4,24,384]{3,2,1,0:T(8,128)(2,1)S(1)}, bf16[8,4,24,384]{3,2,1,0:T(8,128)(2,1)}, u32[]{:S(2)}, u32[]{:S(2)}) collective-permute-start(bf16[8,4,24,384]{3,2,1,0:T(8,128)(2,1)S(1)} %pad_maximum_fusion), channel_id=1, source_target_pairs={{0,1},{1,0},{2,3},{3,2},{4,5},{5,4},{6,7},{7,6},{8,9},{9,8},{10,11... | collective-permute-start | bytes 1769480 | tf_op jit(solution)/shard_map/ppermute | solution.py:371
  205.3 17.4 %all-to-all-start.1 = ((bf16[32,52,128]{2,1,0:T(8,128)(2,1)}), bf16[32,52,128]{2,1,0:T(8,128)(2,1)S(1)}, u32[]{:S(2)}, u32[]{:S(2)}) async-start(bf16[32,52,128]{2,1,0:T(8,128)(2,1)} %convert_element_type.68), calls=%async_computation.1 | async-start | bytes 917504 | tf_op jit(solution)/shard_map/all_to_all | solution.py:514
  222.7 59.3 %all-to-all-start = ((bf16[16,4,24,384]{3,2,1,0:T(8,128)(2,1)}), bf16[16,4,24,384]{3,2,1,0:T(8,128)(2,1)S(1)}, u32[]{:S(2)}, u32[]{:S(2)}) async-start(bf16[16,4,24,384]{3,2,1,0:T(8,128)(2,1)} %bitcast.93), calls=%async_computation | async-start | bytes 2359296 | tf_op jit(solution)/shard_map/all_to_all | solution.py:504
  226.7 29.8 %collective-permute-start.19 = (bf16[1,52,128]{2,1,0:T(8,128)(2,1)S(1)}, bf16[1,52,128]{2,1,0:T(8,128)(2,1)S(1)}, u32[]{:S(2)}, u32[]{:S(2)}) collective-permute-start(bf16[1,52,128]{2,1,0:T(8,128)(2,1)S(1)} %get-tuple-element.118), channel_id=1, source_target_pairs={{0,8},{1,9},{2,10},{3,11},{4,12},{5,13},{6,14},{7,15},{8,0},{9,1},... | collective-permute-start | bytes 39944 | tf_op jit(solution)/shard_map/ppermute | solution.py:371
  256.5 3.9 %collective-permute-start.20 = (bf16[2,52,128]{2,1,0:T(8,128)(2,1)S(1)}, bf16[2,52,128]{2,1,0:T(8,128)(2,1)S(1)}, u32[]{:S(2)}, u32[]{:S(2)}) collective-permute-start(bf16[2,52,128]{2,1,0:T(8,128)(2,1)S(1)} %pad_maximum_fusion.11), channel_id=1, source_target_pairs={{0,4},{1,5},{2,6},{3,7},{4,0},{5,1},{6,2},{7,3},{8,12},{9,13},{10,... | collective-permute-start | bytes 79880 | tf_op jit(solution)/shard_map/ppermute | solution.py:371
  260.4 4.2 %collective-permute-start.21 = (bf16[4,52,128]{2,1,0:T(8,128)(2,1)S(1)}, bf16[4,52,128]{2,1,0:T(8,128)(2,1)S(1)}, u32[]{:S(2)}, u32[]{:S(2)}) collective-permute-start(bf16[4,52,128]{2,1,0:T(8,128)(2,1)S(1)} %pad_maximum_fusion.8), channel_id=1, source_target_pairs={{0,2},{1,3},{2,0},{3,1},{4,6},{5,7},{6,4},{7,5},{8,10},{9,11},{10,... | collective-permute-start | bytes 159752 | tf_op jit(solution)/shard_map/ppermute | solution.py:371
  264.7 4.9 %collective-permute-start.22 = (bf16[8,52,128]{2,1,0:T(8,128)(2,1)S(1)}, bf16[8,52,128]{2,1,0:T(8,128)(2,1)S(1)}, u32[]{:S(2)}, u32[]{:S(2)}) collective-permute-start(bf16[8,52,128]{2,1,0:T(8,128)(2,1)S(1)} %pad_maximum_fusion.6), channel_id=1, source_target_pairs={{0,16},{1,17},{2,18},{3,19},{4,20},{5,21},{6,22},{7,23},{8,24},{9,... | collective-permute-start | bytes 319496 | tf_op jit(solution)/shard_map/ppermute | solution.py:371
  284.6 6.3 %collective-permute-start.9 = (f32[72,128]{0,1:T(8,128)S(1)}, f32[72,128]{0,1:T(8,128)S(1)}, u32[]{:S(2)}, u32[]{:S(2)}) collective-permute-start(f32[72,128]{0,1:T(8,128)S(1)} %maximum_maximum_fusion), channel_id=1, source_target_pairs={{0,8},{1,9},{2,10},{3,11},{4,12},{5,13},{6,14},{7,15},{8,0},{9,1},... | collective-permute-start | bytes 110600 | tf_op jit(solution)/shard_map/ppermute | solution.py:371
  291.0 4.3 %collective-permute-start.10 = (f32[72,128]{0,1:T(8,128)S(1)}, f32[72,128]{0,1:T(8,128)S(1)}, u32[]{:S(2)}, u32[]{:S(2)}) collective-permute-start(f32[72,128]{0,1:T(8,128)S(1)} %fusion.28), channel_id=1, source_target_pairs={{0,4},{1,5},{2,6},{3,7},{4,0},{5,1},{6,2},{7,3},{8,12},{9,13},{10,... | collective-permute-start | bytes 110600 | tf_op jit(solution)/shard_map/ppermute | solution.py:371
  295.4 4.3 %collective-permute-start.11 = (f32[72,128]{0,1:T(8,128)S(1)}, f32[72,128]{0,1:T(8,128)S(1)}, u32[]{:S(2)}, u32[]{:S(2)}) collective-permute-start(f32[72,128]{0,1:T(8,128)S(1)} %add.320), channel_id=1, source_target_pairs={{0,2},{1,3},{2,0},{3,1},{4,6},{5,7},{6,4},{7,5},{8,10},{9,11},{10,... | collective-permute-start | bytes 110600 | tf_op jit(solution)/shard_map/ppermute | solution.py:371
  299.7 4.3 %collective-permute-start.12 = (f32[72,128]{0,1:T(8,128)S(1)}, f32[72,128]{0,1:T(8,128)S(1)}, u32[]{:S(2)}, u32[]{:S(2)}) collective-permute-start(f32[72,128]{0,1:T(8,128)S(1)} %add.321), channel_id=1, source_target_pairs={{0,16},{1,17},{2,18},{3,19},{4,20},{5,21},{6,22},{7,23},{8,24},{9,... | collective-permute-start | bytes 110600 | tf_op jit(solution)/shard_map/ppermute | solution.py:371
  (41 other events, 506.5 us)

commit v2 on v0

v2 whole, which is shorter than its diff:
```python
import math
from functools import partial

import jax
import jax.numpy as jnp
from jax import lax
from jax.experimental import pallas as pl
from jax.experimental.pallas import tpu as pltpu
from jax.sharding import PartitionSpec as P

CZ = 128
HEADS = 4
HEAD_DIM = 32
FF = 512
BINS = 64
WIDE = 5 * CZ + FF

DECAY = 1.0 - 10.0 ** (-0.8)
TINY = 1e-30
LOG2E = math.log2(math.e)
ROOT = 1.0 / math.sqrt(HEAD_DIM)
BLK = 256
SAFE = 40.0

GATE_BLOCK, OUT_BLOCK, IN_BLOCK, DOWN_BLOCK, HEAD_BLOCK, BLOCKS = 0, 1, 2, 6, 10, 12

f32 = jnp.float32
bf16 = jnp.bfloat16


def dot(a, b):
    return lax.dot_general(a, b, (((1,), (0,)), ((), ())), preferred_element_type=f32)


def dot_nt(a, b):
    return lax.dot_general(a, b, (((1,), (1,)), ((), ())), preferred_element_type=f32)


def rounded(v):
    return v.astype(bf16).astype(f32)


def halves(v):
    high = v.astype(bf16)
    return high, (v - high.astype(f32)).astype(bf16)


def normed(x):
    centre = x - jnp.sum(x, 0, keepdims=True) * (1.0 / CZ)
    var = jnp.sum(centre * centre, 0, keepdims=True) * (1.0 / CZ)
    inv = lax.rsqrt(var + 1e-05)
    return centre * inv, inv


def normed_back(d, xhat, inv):
    one = jnp.sum(d, 0, keepdims=True) * (1.0 / CZ)
    two = jnp.sum(d * xhat, 0, keepdims=True) * (1.0 / CZ)
    return inv * (d - one - xhat * two)


def sigmoid(x):
    return 0.5 * jnp.tanh(0.5 * x) + 0.5


def wider(column, x):
    return jnp.concatenate([column] * (x.shape[1] // 128), 1)


def lanes(ref):
    return jnp.concatenate([ref[g] for g in range(ref.shape[0])], 1)


def spread(ref, x):
    width = ref.shape[2]
    for g in range(ref.shape[0]):
        ref[g] = x[:, g * width : (g + 1) * width]


def columns_of(gains_ref, which, scratch):
    scratch[...] = jnp.broadcast_to(gains_ref[...].T[:, which : which + 1], (CZ, CZ))


def place(source, me, masks):
    apart = source ^ me
    where = 0
    for t, mask in enumerate(masks):
        where = where + ((apart >> (mask.bit_length() - 1)) & 1) * (1 << t)
    return where


def front_kernel(
    pair_ref,
    gains_ref,
    small_ref,
    wide_ref,
    down_ref,
    stats_ref,
    zt_ref,
    zbt_ref,
    bias_ref,
    pack_ref,
    gain,
    wb,
    part,
    pack,
):
    rows, width, _ = pair_ref.shape
    step = pl.program_id(0)

    @pl.when(step == 0)
    def _():
        columns_of(gains_ref, 0, gain)
        wb[...] = small_ref[:16].astype(bf16)
        lines, cols = wide_ref.shape
        span = down_ref.shape[1]
        pack[...] = jnp.zeros_like(pack)
        pack[:lines, :cols] = wide_ref[...]
        for at in range(FF // CZ):
            pack[:lines, cols + at * span : cols + (at + 1) * span] = down_ref[
                at * lines : (at + 1) * lines, :
            ]
        after = cols + (FF // CZ) * span
        stats = stats_ref[...]
        upper = rounded(stats)
        pack[0:1, after : after + stats.shape[1]] = upper
        pack[1:2, after : after + stats.shape[1]] = stats - upper
        pack_ref[...] = pack[...].astype(bf16)

    x = pair_ref[...].astype(f32).reshape(rows * width, CZ).T
    spread(zt_ref, x.astype(bf16))
    xhat, _ = normed(x)
    zb = (xhat * wider(gain[...], x)).astype(bf16)
    spread(zbt_ref, zb)
    bias = dot(wb[...], zb)
    for g in range(rows):
        for h in range(HEADS):
            part[h, pl.ds(step * rows + g, 1), :] = bias[h : h + 1, g * width : (g + 1) * width]

    @pl.when(step == pl.num_programs(0) - 1)
    def _():
        bias_ref[...] = part[...].astype(bf16)


def project_kernel(
    crops,
    rows,
    masks,
    info_ref,
    packs_ref,
    zbt_ref,
    qkv_ref,
    gate_ref,
    kvn_ref,
    norm_ref,
    wide_ref,
    down_ref,
    wide_s,
    down_s,
    wqt,
):
    lines, cols, span = CZ // rows, WIDE // crops, CZ // crops

    @pl.when(pl.program_id(0) == 0)
    def _():
        me = info_ref[1] * rows + info_ref[0]
        for c in range(crops):
            for r in range(rows):
                block = packs_ref[place(c * rows + r, me, masks)].astype(f32)[:lines]
                wide_s[r * lines : (r + 1) * lines, c * cols : (c + 1) * cols] = block[:, :cols]
                for part in range(FF // CZ):
                    at = (r * (FF // CZ) + part) * lines
                    down_s[at : at + lines, c * span : (c + 1) * span] = block[
                        :, cols + part * span : cols + (part + 1) * span
                    ]
        wide_ref[...] = wide_s[...].astype(bf16)
        down_ref[...] = down_s[...].astype(bf16)
        wqt[...] = wide_s[:, : 4 * CZ].T.astype(bf16)

    proj = dot(wqt[...], lanes(zbt_ref))
    qkv = proj[: 3 * CZ].astype(bf16)
    spread(qkv_ref, qkv)
    spread(gate_ref, sigmoid(proj[3 * CZ :]))
    q = qkv[:CZ].astype(f32)
    k = qkv[CZ : 2 * CZ].astype(f32)
    kvn_ref[...] = qkv[CZ:].T.reshape(kvn_ref.shape)
    norm_ref[...] = jnp.concatenate(
        [
            jnp.sum((x * x)[h * HEAD_DIM : (h + 1) * HEAD_DIM], 0, keepdims=True)
            for x in (q, k)
            for h in range(HEADS)
        ],
        0,
    )


def attend_kernel(
    masks,
    info_ref,
    norm_ref,
    bias_ref,
    q_ref,
    kn_ref,
    v_ref,
    p_ref,
    o_ref,
    r_ref,
    biast,
    nat,
    qbd,
    kk,
    bound,
):
    group, _, width = q_ref.shape
    shards, _, rows, _ = bias_ref.shape
    step = pl.program_id(0)

    @pl.when(step == 0)
    def _():
        top = 0.0
        key = lax.broadcasted_iota(jnp.int32, (1, width), 1)
        kb = jnp.where(key < info_ref[2], 0.0, -1000000000.0 * LOG2E)
        for h in range(HEADS):
            for s in range(shards):
                nat[s * rows : (s + 1) * rows, :] = bias_ref[place(s, info_ref[0], masks), h].astype(f32)
            top = jnp.maximum(top, jnp.max(jnp.abs(nat[...])))
            biast[:, h * width : (h + 1) * width] = (nat[...] * LOG2E + kb).T
        bound[0] = top * LOG2E
        qbd[...] = jnp.zeros_like(qbd)
        r_ref[...] = jnp.zeros_like(r_ref)

    def attend(shift):
        for g in range(group):
            high, low = halves(q_ref[g].astype(f32) * (LOG2E * ROOT))
            for h in range(HEADS):
                a, b = h * HEAD_DIM, (h + 1) * HEAD_DIM
                qbd[g, a:b, h * width : (h + 1) * width] = high[a:b]
                qbd[g, CZ + a : CZ + b, h * width : (h + 1) * width] = low[a:b]
            kk[g, :, :CZ] = kn_ref[g]
            kk[g, :, CZ:] = kn_ref[g]
            sums = []
            for c in range(0, HEADS * width, BLK):
                s = dot(kk[g], qbd[g, :, c : c + BLK]) + biast[:, c : c + BLK]
                if shift:
                    s = s - jnp.max(s, 0, keepdims=True)
                e = jnp.exp2(s)
                sums.append(jnp.sum(e, 0, keepdims=True))
                p_ref[g, :, c : c + BLK] = e.astype(bf16)
            r = 1.0 / jnp.concatenate(sums, 1)
            for h in range(HEADS):
                a, b = h * HEAD_DIM, (h + 1) * HEAD_DIM
                mine = r[:, h * width : (h + 1) * width]
                r_ref[g, h : h + 1] = mine
                o_ref[g, a:b] = dot(v_ref[g, a:b], p_ref[g, :, h * width : (h + 1) * width]) * mine

    norms = jnp.max(norm_ref[...], 1, keepdims=True)
    reach = jnp.max(jnp.sqrt(norms[:HEADS] * norms[HEADS:])) * (1.01 * LOG2E * ROOT)
    safe = reach + bound[0] < SAFE

    @pl.when(safe)
    def _():
        attend(False)

    @pl.when(jnp.logical_not(safe))
    def _():
        attend(True)


def middle_kernel(
    info_ref,
    wide_ref,
    down_ref,
    head_ref,
    gains_ref,
    zt_ref,
    zbt_ref,
    o_ref,
    gate_ref,
    r_ref,
    tgt_ref,
    nbr_ref,
    do_ref,
    nd_ref,
    grads_ref,
    scalars_ref,
    acc,
    sums,
    g1,
    g2,
    wot,
    wint,
    wdownt,
    wht,
    wo2,
    wdown2,
    wh2,
):
    step = pl.program_id(0)

    @pl.when(step == 0)
    def _():
        wo = wide_ref[:, 4 * CZ : 5 * CZ]
        wot[...] = wo.T
        wint[...] = wide_ref[:, 5 * CZ :].T
        wdownt[...] = down_ref[...].T
        head = head_ref[...][HEADS:]
        wht[...] = head.astype(bf16)
        head = head.T.astype(bf16)
        wo2[...] = jnp.concatenate([wo, wo], 1)
        wdown2[...] = jnp.concatenate([down_ref[...], down_ref[...]], 1)
        wh2[...] = jnp.concatenate([head, head], 1)
        acc[...] = jnp.zeros_like(acc)
        columns_of(gains_ref, 1, g1)
        columns_of(gains_ref, 2, g2)
        sums[...] = jnp.zeros_like(sums)

    o = lanes(o_ref)
    gate = lanes(gate_ref)
    gain1 = wider(g1[...], o)
    gain2 = wider(g2[...], o)

    def add(block, grad):
        for c in range(0, grad.shape[1], CZ):
            acc[block + c // CZ] += grad[:, c : c + CZ]

    og = (o * gate).astype(bf16)
    z1 = lanes(zt_ref).astype(f32) + dot(wot[...], og)
    xhat1, inv1 = normed(z1)
    zb2 = (xhat1 * gain1).astype(bf16)
    hidden, slopes = [], []
    for f in range(0, FF, CZ):
        hid = dot(wint[f : f + CZ], zb2)
        sg = sigmoid(hid)
        act = hid * sg
        hidden.append(act.astype(bf16))
        slopes.append(sg + act * (1.0 - sg))
    a = jnp.concatenate(hidden, 0)
    z2 = z1 + dot(wdownt[...], a)
    xhat2, inv2 = normed(z2)
    zb3 = (xhat2 * gain2).astype(bf16)
    logits = dot(wht[...], zb3)
    top = jnp.max(logits, 0, keepdims=True)
    ex = jnp.exp(logits - top)
    total = jnp.sum(ex, 0, keepdims=True)
    group, _, width = o_ref.shape
    first = step * group
    target = jnp.concatenate([tgt_ref[0, pl.ds(first + g, 1), :] for g in range(group)], 1)
    hot = lax.broadcasted_iota(jnp.int32, logits.shape, 0) == target
    picked = jnp.sum(jnp.where(hot, logits, 0.0), 0, keepdims=True)
    column = lax.broadcasted_iota(jnp.int32, (1, width), 1)
    length = info_ref[2]
    mask = jnp.concatenate(
        [
            jnp.where(
                (nbr_ref[0, pl.ds(first + g, 1), :] > 0)
                & (column < jnp.where(info_ref[0] * info_ref[3] + first + g < length, length, 0)),
                1.0,
                0.0,
            )
            for g in range(group)
        ],
        1,
    )
    sums[0:1] += (jnp.log(total) + top - picked) * mask
    sums[1:2] += mask

    dl = ex * (mask / total) - jnp.where(hot, mask, 0.0)
    dl2 = jnp.concatenate(halves(dl), 0)
    add(HEAD_BLOCK, dot_nt(dl2, zb3))
    dzb3 = rounded(dot(wh2[...], dl2))
    dz2 = normed_back(dzb3 * gain2, xhat2, inv2)
    high2, low2 = halves(dz2)
    both2 = jnp.concatenate([high2, low2], 0)
    dh = jnp.concatenate(
        [
            (dot(wdown2[f : f + CZ], both2) * slopes[f // CZ]).astype(bf16)
            for f in range(0, FF, CZ)
        ],
        0,
    )
    add(DOWN_BLOCK, dot_nt(high2, a))
    dzb2 = rounded(dot(wide_ref[:, 5 * CZ :], dh))
    add(IN_BLOCK, dot_nt(zb2, dh))
    dz1 = dz2 + normed_back(dzb2 * gain1, xhat1, inv1)
    high1, low1 = halves(dz1)
    add(OUT_BLOCK, dot_nt(og, high1))
    dog = rounded(dot(wo2[...], jnp.concatenate([high1, low1], 0)))
    do = dog * gate
    doo = do * o
    add(GATE_BLOCK, dot_nt(lanes(zbt_ref), (doo * (1.0 - gate)).astype(bf16)))
    r = lanes(r_ref)
    parts, minus = [], []
    for h in range(HEADS):
        x, y = h * HEAD_DIM, (h + 1) * HEAD_DIM
        mine = r[h : h + 1]
        parts.append((do[x:y] * mine).astype(bf16))
        less = -jnp.sum(doo[x:y], 0, keepdims=True) * mine
        upper = rounded(less)
        minus.append(
            jnp.concatenate([upper, less - upper, jnp.zeros((14, less.shape[1]), f32)], 0)
        )
    spread(do_ref, jnp.concatenate(parts, 0))
    spread(nd_ref, jnp.concatenate(minus, 0).astype(bf16))

    @pl.when(step == pl.num_programs(0) - 1)
    def _():
        for block in range(BLOCKS):
            grads_ref[block] = acc[block].astype(bf16)
        both = jnp.sum(sums[...], 1, keepdims=True)
        lane = lax.broadcasted_iota(jnp.int32, scalars_ref.shape, 1)
        out = jnp.zeros(scalars_ref.shape, f32)
        for part in range(3):
            upper = rounded(both)
            for which in range(2):
                out = jnp.where(lane == 2 * part + which, upper[which : which + 1], out)
            both = both - upper
        scalars_ref[...] = out.astype(bf16)


def score_kernel(p_ref, vn_ref, do_ref, nd_ref, dbias_ref, acc, dobd, vv):
    group, _, width = do_ref.shape
    step = pl.program_id(0)

    @pl.when(step == 0)
    def _():
        acc[...] = jnp.zeros_like(acc)
        prepare(dobd, vv)

    for g in range(group):
        score_operands(g, vn_ref, do_ref, nd_ref, dobd, vv)
        for c in range(0, HEADS * width, BLK):
            acc[:, c : c + BLK] += dot(vv[g], dobd[g, :, c : c + BLK]) * p_ref[
                g, :, c : c + BLK
            ].astype(f32)

    @pl.when(step == pl.num_programs(0) - 1)
    def _():
        owners, _, lines, _ = dbias_ref.shape
        for h in range(HEADS):
            mine = acc[:, h * width : (h + 1) * width].T
            for r in range(owners):
                dbias_ref[r, h] = mine[r * lines : (r + 1) * lines].astype(bf16)


def prepare(dobd, vv):
    dobd[...] = jnp.zeros_like(dobd)
    vv[...] = jnp.ones_like(vv)


def score_operands(g, vn_ref, do_ref, nd_ref, dobd, vv):
    width = do_ref.shape[2]
    vv[g, :, :CZ] = vn_ref[g]
    for h in range(HEADS):
        a, b = h * HEAD_DIM, (h + 1) * HEAD_DIM
        at = slice(h * width, (h + 1) * width)
        dobd[g, a:b, at] = do_ref[g, a:b]
        dobd[g, CZ : CZ + 16, at] = nd_ref[g, 16 * h : 16 * (h + 1)]


def back_kernel(
    p_ref, q_ref, k_ref, vn_ref, do_ref, nd_ref, zbt_ref, dwq_ref, dobd, dst, vv, dproj
):
    group, _, width = do_ref.shape

    @pl.when(pl.program_id(0) == 0)
    def _():
        dwq_ref[...] = jnp.zeros_like(dwq_ref)
        prepare(dobd, vv)

    for g in range(group):
        score_operands(g, vn_ref, do_ref, nd_ref, dobd, vv)
        for c in range(0, HEADS * width, BLK):
            ds = dot(vv[g], dobd[g, :, c : c + BLK]) * p_ref[g, :, c : c + BLK].astype(f32)
            dst[g, :, c : c + BLK] = ds.astype(bf16)
        at = slice(g * width, (g + 1) * width)
        for h in range(HEADS):
            a, b = h * HEAD_DIM, (h + 1) * HEAD_DIM
            mine = dst[g, :, h * width : (h + 1) * width]
            dproj[a:b, at] = (dot(k_ref[g, a:b], mine) * ROOT).astype(bf16)
            dproj[CZ + a : CZ + b, at] = (dot_nt(q_ref[g, a:b], mine) * ROOT).astype(bf16)
            dproj[2 * CZ + a : 2 * CZ + b, at] = dot_nt(
                do_ref[g, a:b], p_ref[g, :, h * width : (h + 1) * width]
            ).astype(bf16)
    grad = dot_nt(lanes(zbt_ref), dproj[...])
    for block in range(3):
        dwq_ref[block] += grad[:, block * CZ : (block + 1) * CZ]


def factored(grad_ref, rows, cols, weight_ref, crop, row_start, scratch, outs):
    grad_out, rows_out, cols_out, new_out = outs
    lines, span = weight_ref.shape
    grad = grad_ref[...]
    count, columns = grad.shape
    sq = grad * grad
    rows_new = DECAY * rows + (1.0 - DECAY) * (jnp.sum(sq, 1, keepdims=True) / columns + TINY)
    cols_new = DECAY * cols + (1.0 - DECAY) * (jnp.sum(sq, 0, keepdims=True) / count + TINY)
    mean = jnp.sum(rows_new, 0, keepdims=True) / count
    rows_factor = mean / rows_new
    cols_factor = 1.0 / cols_new
    size = jnp.sum(jnp.sum(sq * rows_factor * cols_factor, 1, keepdims=True), 0, keepdims=True)
    clip = jnp.maximum(0.1, jnp.sqrt(size / (count * columns)))
    scratch[...] = rows_factor
    mine = grad_ref[pl.ds(row_start, lines), :]
    update = mine * lax.rsqrt((1.0 / scratch[pl.ds(row_start, lines), :]) * (1.0 / cols_factor))
    update = weight_step(update, clip)
    scratch[...] = rows_new
    own_rows = jnp.broadcast_to(scratch[pl.ds(row_start, lines), :], (lines, CZ))
    rows_out[...] = own_rows.T[:1]

    def own(x):
        part = x[:, :span]
        for c in range(1, columns // span):
            part = jnp.where(crop == c, x[:, c * span : (c + 1) * span], part)
        return part

    grad_out[...] = own(mine)
    cols_out[...] = own(cols_new)
    new_out[...] = weight_ref[...] - own(update)


def weight_step(update, clip):
    return update * (0.03 / clip)


def plain(weight, grad, second, rate, outs):
    second_new = DECAY * second + (1.0 - DECAY) * (grad * grad + TINY)
    update = grad * lax.rsqrt(second_new)
    square = jnp.sum(jnp.sum(update * update, 1, keepdims=True), 0, keepdims=True)
    clip = jnp.maximum(1.0, jnp.sqrt(square / (grad.shape[0] * grad.shape[1])))
    outs[0][...] = grad
    outs[1][...] = second_new
    outs[2][...] = weight - rate * update / clip


def finish_kernel(
    info_ref,
    late_ref,
    early_ref,
    full_ref,
    wide_rows_ref,
    wide_cols_ref,
    down_rows_ref,
    down_cols_ref,
    wide_ref,
    down_ref,
    gains_ref,
    gain_second_ref,
    small_ref,
    small_second_ref,
    *refs,
):
    outs, (flat, wide_s, down_s, wide_c, down_c) = refs[:14], refs[14:]
    devices, lines, _ = early_ref.shape
    lines -= 16
    tail = jnp.zeros((1, CZ), f32)
    for d in range(devices):
        block = early_ref[d].astype(f32)
        flat[d * lines : (d + 1) * lines, :] = block[:lines]
        tail += block[lines : lines + 1]
    scale = 1.0 / (tail[:, 1:2] + tail[:, 3:4] + tail[:, 5:6])

    def early(block):
        return flat[block * CZ : (block + 1) * CZ, :] * scale

    for block in range(3):
        wide_s[:, block * CZ : (block + 1) * CZ] = (
            late_ref[block * CZ : (block + 1) * CZ, :] * scale
        )
    for block in range(GATE_BLOCK, DOWN_BLOCK):
        wide_s[:, (3 + block) * CZ : (4 + block) * CZ] = early(block)
    for block in range(DOWN_BLOCK, HEAD_BLOCK):
        down_s[(block - DOWN_BLOCK) * CZ : (block - DOWN_BLOCK + 1) * CZ, :] = early(block).T
    head = early(HEAD_BLOCK)
    pbias = late_ref[3 * CZ : 3 * CZ + 16, :] * scale
    small_grad = jnp.concatenate([pbias[:HEADS], head[:BINS] + head[BINS:]], 0)
    small = small_ref[...]
    plain(small, small_grad, small_second_ref[...], 0.03, outs[11:])

    through = wide_s[...] * full_ref[...].astype(f32)
    behind = small_grad * rounded(small)
    lane = lax.broadcasted_iota(jnp.int32, (CZ, CZ), 1)
    table = jnp.where(
        lane == 0,
        jnp.sum(through[:, : 4 * CZ], 1, keepdims=True),
        jnp.sum(through[:, 5 * CZ :], 1, keepdims=True),
    ).T
    table = jnp.concatenate(
        [
            table[:1] + jnp.sum(behind[:HEADS], 0, keepdims=True),
            table[1:2],
            jnp.sum(behind[HEADS:], 0, keepdims=True),
        ],
        0,
    )
    gains = gains_ref[...]
    plain(gains, table / gains, gain_second_ref[...], 0.3, outs[8:11])

    row, crop = info_ref[0], info_ref[1]
    factored(
        wide_s,
        wide_rows_ref[...],
        wide_cols_ref[...],
        wide_ref,
        crop,
        row * wide_ref.shape[0],
        wide_c,
        outs[:4],
    )
    factored(
        down_s,
        down_rows_ref[...],
        down_cols_ref[...],
        down_ref,
        crop,
        row * down_ref.shape[0],
        down_c,
        outs[4:8],
    )


def whole(shape):
    return pl.BlockSpec(shape, lambda i: (0,) * len(shape))


def rows_of(group, lines, columns, line=0, column=0):
    return pl.BlockSpec((group, lines, columns), lambda i: (i, line, column))


def of(shape, dtype):
    return jax.ShapeDtypeStruct(shape, dtype)


SMEM = pl.BlockSpec(memory_space=pltpu.SMEM)


def call(kernel, name, micros, grid, in_specs, outs, scratch, args):
    return pl.pallas_call(
        kernel,
        grid=(grid,),
        in_specs=in_specs,
        out_specs=[o[0] for o in outs],
        out_shape=[of(o[1], o[2]) for o in outs],
        scratch_shapes=scratch,
        compiler_params=pltpu.CompilerParams(vmem_limit_bytes=56 * 1024 * 1024),
        cost_estimate=pl.CostEstimate(
            flops=int(micros * 8e8), bytes_accessed=1 << 20, transcendentals=0
        ),
        name=name,
    )(*args)


def group_of(count, most):
    return next(g for g in range(most, 0, -1) if count % g == 0)


def front(pair, gains, small, wide, down, stats):
    count, width = pair.shape[0], pair.shape[1]
    columns = wide.shape[1] + (FF // CZ) * down.shape[1] + CZ
    g = group_of(count, 4)
    return call(
        front_kernel,
        "front",
        6,
        count // g,
        [rows_of(g, width, CZ)] + [whole(x.shape) for x in (gains, small, wide, down, stats)],
        [
            (rows_of(g, CZ, width), (count, CZ, width), bf16),
            (rows_of(g, CZ, width), (count, CZ, width), bf16),
            (whole((HEADS, count, width)), (HEADS, count, width), bf16),
            (whole((8, columns)), (8, columns), bf16),
        ],
        [
            pltpu.VMEM((CZ, CZ), f32),
            pltpu.VMEM((16, CZ), bf16),
            pltpu.VMEM((HEADS, count, width), f32),
            pltpu.VMEM((8, columns), f32),
        ],
        (pair, gains, small, wide, down, stats),
    )


def project(crops, rows, masks, info, packs, zbt):
    count, _, width = zbt.shape
    g = group_of(count, 4)
    return call(
        partial(project_kernel, crops, rows, masks),
        "project",
        8,
        count // g,
        [SMEM, whole(packs.shape), rows_of(g, CZ, width)],
        [
            (rows_of(g, 3 * CZ, width), (count, 3 * CZ, width), bf16),
            (rows_of(g, CZ, width), (count, CZ, width), f32),
            (rows_of(g, width, 2 * CZ), (count, width, 2 * CZ), bf16),
            (pl.BlockSpec((8, g * width), lambda i: (0, i)), (8, count * width), f32),
            (whole((CZ, WIDE)), (CZ, WIDE), bf16),
            (whole((FF, CZ)), (FF, CZ), bf16),
        ],
        [pltpu.VMEM((CZ, WIDE), f32), pltpu.VMEM((FF, CZ), f32), pltpu.VMEM((4 * CZ, CZ), bf16)],
        (info, packs, zbt),
    )


ATTEND_ROWS = 4
MIDDLE_ROWS = 4
SCORE_ROWS = 3
BACK_ROWS = 3


def attend(masks, info, norms, bias, kvn, qkv):
    count, _, width = qkv.shape
    g = group_of(count, ATTEND_ROWS)
    return call(
        partial(attend_kernel, masks),
        "attend",
        25,
        count // g,
        [
            SMEM,
            pl.BlockSpec((8, g * width), lambda i: (0, i)),
            whole(bias.shape),
            rows_of(g, CZ, width),
            rows_of(g, width, CZ),
            rows_of(g, CZ, width, 2),
        ],
        [
            (rows_of(g, width, HEADS * width), (count, width, HEADS * width), bf16),
            (rows_of(g, CZ, width), (count, CZ, width), f32),
            (rows_of(g, 8, width), (count, 8, width), f32),
        ],
        [
            pltpu.VMEM((width, HEADS * width), f32),
            pltpu.VMEM((width, width), f32),
            pltpu.VMEM((g, 2 * CZ, HEADS * width), bf16),
            pltpu.VMEM((g, width, 2 * CZ), bf16),
            pltpu.SMEM((1,), f32),
        ],
        (info, norms, bias, qkv, kvn, qkv),
    )


def middle(info, wide, down, small, gains, zt, zbt, o, gate, r, tgt, nbr):
    count, _, width = zt.shape
    g = group_of(count, MIDDLE_ROWS)
    return call(
        middle_kernel,
        "middle",
        30,
        count // g,
        [
            SMEM,
            whole((CZ, WIDE)),
            whole((FF, CZ)),
            whole(small.shape),
            whole(gains.shape),
            rows_of(g, CZ, width),
            rows_of(g, CZ, width),
            rows_of(g, CZ, width),
            rows_of(g, CZ, width),
            rows_of(g, 8, width),
            whole(tgt.shape),
            whole(nbr.shape),
        ],
        [
            (rows_of(g, CZ, width), (count, CZ, width), bf16),
            (rows_of(g, 16 * HEADS, width), (count, 16 * HEADS, width), bf16),
            (whole((BLOCKS, CZ, CZ)), (BLOCKS, CZ, CZ), bf16),
            (whole((16, CZ)), (16, CZ), bf16),
        ],
        [
            pltpu.VMEM((BLOCKS, CZ, CZ), f32),
            pltpu.VMEM((2, g * width), f32),
            pltpu.VMEM((CZ, CZ), f32),
            pltpu.VMEM((CZ, CZ), f32),
            pltpu.VMEM((CZ, CZ), bf16),
            pltpu.VMEM((FF, CZ), bf16),
            pltpu.VMEM((CZ, FF), bf16),
            pltpu.VMEM((BINS, CZ), bf16),
            pltpu.VMEM((CZ, 2 * CZ), bf16),
            pltpu.VMEM((FF, 2 * CZ), bf16),
            pltpu.VMEM((CZ, 2 * BINS), bf16),
        ],
        (info, wide, down, small, gains, zt, zbt, o, gate, r, tgt, nbr),
    )


def score(p, kvn, do, nd):
    count, _, width = do.shape
    g = group_of(count, SCORE_ROWS)
    shape = (width // count, HEADS, count, width)
    return call(
        score_kernel,
        "score",
        17,
        count // g,
        [
            rows_of(g, width, HEADS * width),
            rows_of(g, width, CZ, 0, 1),
            rows_of(g, CZ, width),
            rows_of(g, 16 * HEADS, width),
        ],
        [(whole(shape), shape, bf16)],
        [
            pltpu.VMEM((width, HEADS * width), f32),
            pltpu.VMEM((g, 2 * CZ, HEADS * width), bf16),
            pltpu.VMEM((g, width, 2 * CZ), bf16),
        ],
        (p, kvn, do, nd),
    )[0]


def back(p, qkv, kvn, do, nd, zbt):
    count, _, width = zbt.shape
    g = group_of(count, BACK_ROWS)
    return call(
        back_kernel,
        "back",
        38,
        count // g,
        [
            rows_of(g, width, HEADS * width),
            rows_of(g, CZ, width),
            rows_of(g, CZ, width, 1),
            rows_of(g, width, CZ, 0, 1),
            rows_of(g, CZ, width),
            rows_of(g, 16 * HEADS, width),
            rows_of(g, CZ, width),
        ],
        [(whole((3, CZ, CZ)), (3, CZ, CZ), f32)],
        [
            pltpu.VMEM((g, 2 * CZ, HEADS * width), bf16),
            pltpu.VMEM((g, width, HEADS * width), bf16),
            pltpu.VMEM((g, width, 2 * CZ), bf16),
            pltpu.VMEM((3 * CZ, g * width), bf16),
        ],
        (p, qkv, qkv, kvn, do, nd, zbt),
    )[0]


def finish(*args):
    wide, down, gains, small = args[8], args[9], args[10], args[12]
    shapes = []
    for weight in (wide, down):
        shapes += [weight.shape, (1, weight.shape[0]), (1, weight.shape[1]), weight.shape]
    shapes += [gains.shape] * 3 + [small.shape] * 3
    return call(
        finish_kernel,
        "finish",
        4,
        1,
        [SMEM] + [whole(x.shape) for x in args[1:]],
        [(whole(shape), shape, f32) for shape in shapes],
        [
            pltpu.VMEM((BLOCKS * CZ, CZ), f32),
            pltpu.VMEM((CZ, WIDE), f32),
            pltpu.VMEM((FF, CZ), f32),
            pltpu.VMEM((CZ, 1), f32),
            pltpu.VMEM((FF, 1), f32),
        ],
        args,
    )


def bits(n):
    return [1 << t for t in reversed(range(n.bit_length() - 1))]


def swap(x, axes, size, mask):
    return lax.ppermute(x, axes, [(i, i ^ mask) for i in range(size)])


def gathered(x, axes, size, masks):
    x = x[None]
    for mask in masks:
        x = jnp.concatenate([x, swap(x, axes, size, mask)], 0)
    return x


def places(me, size, masks):
    apart = jnp.arange(size, dtype=jnp.int32) ^ me
    place = jnp.zeros((size,), jnp.int32)
    for t, mask in enumerate(masks):
        place = place + jnp.where((apart & mask) != 0, 1 << t, 0)
    return place


def exact_halves(v):
    high = lax.reduce_precision(v, 8, 7)
    return high.astype(bf16), (v - high).astype(bf16)


def build(crops, rows):
    both = ("crop", "row")
    devices = crops * rows
    row_masks = bits(rows)
    all_masks = row_masks[:-1] + [m * rows for m in bits(crops)] + row_masks[-1:]

    def total(x, core):
        half = x.shape[0] // 2
        keep = lax.dynamic_slice_in_dim(x, core * half, half)
        give = lax.dynamic_slice_in_dim(x, (1 - core) * half, half)
        keep = keep + swap(give, both, devices, 1)
        for mask in all_masks[:-1]:
            keep = keep + swap(keep, both, devices, mask)
        other = swap(keep, both, devices, 1)
        first = core == 0
        return jnp.concatenate([jnp.where(first, keep, other), jnp.where(first, other, keep)], 0)

    def body(
        pair,
        crop_len,
        targets,
        neighbours,
        wide,
        wide_rows,
        wide_cols,
        down,
        down_rows,
        down_cols,
        gains,
        gain_second,
        small,
        small_second,
    ):
        row_index = lax.axis_index("row")
        crop_index = lax.axis_index("crop")
        count_rows, width = pair.shape[1], pair.shape[2]
        info = jnp.stack([row_index, crop_index, crop_len[0], jnp.int32(count_rows)])

        lines, cols = wide.shape
        cols_stat = jnp.concatenate([wide_cols, down_cols])
        cols_stat = jnp.pad(cols_stat, (0, -cols_stat.size % rows))
        share = cols_stat.size // rows
        stats = jnp.concatenate(
            [
                wide_rows,
                down_rows,
                lax.dynamic_slice_in_dim(cols_stat, row_index * share, share),
            ]
        )
        small_t = small.T
        zt, zbt, bias_part, pack = front(pair[0], gains, small_t, wide, down, stats[None, :])
        packs = gathered(pack, both, devices, all_masks)
        bias = gathered(bias_part, "row", rows, row_masks[:-1])
        qkv, gate, kvn, norms, wide_full, down_full = project(
            crops, rows, all_masks, info, packs, zbt
        )
        bias, norms = lax.optimization_barrier((bias, norms))
        bias = jnp.concatenate([bias, swap(bias, "row", rows, row_masks[-1])], 0)
        if count_rows % 8:
            bias = jnp.take(bias, places(row_index, rows, row_masks), axis=0)
            bias = bias.transpose(1, 0, 2, 3).reshape(1, HEADS, width, width)
        bias_masks = [] if count_rows % 8 else row_masks
        p, o, r = attend(bias_masks, info, norms, bias, kvn, qkv)
        do, nd, early, scalars = middle(
            info,
            wide_full,
            down_full,
            small_t,
            gains,
            zt,
            zbt,
            o,
            gate,
            r,
            targets,
            neighbours,
        )

        early = lax.all_to_all(early.reshape(devices, -1, CZ), both, 0, 0, tiled=True)
        d_bias = score(p, kvn, do, nd)
        early, d_bias = lax.optimization_barrier((early, d_bias))
        early = jnp.sum(early.astype(f32), 0).astype(bf16)
        early = jnp.concatenate([early, scalars], 0)
        early = jnp.broadcast_to(early[None], (devices, *early.shape))
        early, d_bias, do = lax.optimization_barrier((early, d_bias, do))
        early = lax.all_to_all(early, both, 0, 0, tiled=True)
        scalars = jnp.sum(early[:, -16, :6].astype(f32), 0).reshape(3, 2)
        loss_sum, pair_count = jnp.sum(scalars[:, 0]), jnp.sum(scalars[:, 1])

        d_bias = lax.all_to_all(d_bias, "row", 0, 0, tiled=True)
        d_qkv = back(p, qkv, kvn, do, nd, zbt)
        d_bias = jnp.sum(d_bias.astype(f32), 0).astype(bf16)
        d_pbias = lax.dot_general(
            d_bias, zbt, (((1, 2), (0, 2)), ((), ())), preferred_element_type=f32
        )
        late = total(
            jnp.concatenate(
                [d_qkv.reshape(3 * CZ, CZ), jnp.pad(d_pbias, ((0, 16 - HEADS), (0, 0)))], 0
            ),
            row_index & 1,
        )

        after = cols + (FF // CZ) * down.shape[1]
        extras = jnp.sum(packs[:, :2, after : after + stats.size].astype(f32), 1)
        extras = jnp.take(
            extras, places(crop_index * rows + row_index, devices, all_masks), axis=0
        )
        wide_rows_all = extras[:rows, :lines].reshape(-1)
        down_rows_all = extras[:rows, lines : lines + down_rows.size].reshape(-1)
        cols_all = extras[:, lines + down_rows.size :].reshape(crops, -1)
        wide_cols_all = cols_all[:, :cols].reshape(-1)
        down_cols_all = cols_all[:, cols : cols + down_cols.size].reshape(-1)

        (
            wide_g,
            wide_r_new,
            wide_c_new,
            wide_new,
            down_g,
            down_r_new,
            down_c_new,
            down_new,
            gain_grad,
            gain_s,
            gain_n,
            small_grad,
            small_s,
            small_n,
        ) = finish(
            info,
            late,
            early,
            wide_full,
            wide_rows_all[:, None],
            wide_cols_all[None, :],
            down_rows_all[:, None],
            down_cols_all[None, :],
            wide,
            down,
            gains,
            gain_second,
            small_t,
            small_second.T,
        )
        return (
            loss_sum,
            pair_count,
            wide_g,
            wide_r_new.reshape(-1),
            wide_c_new.reshape(-1),
            wide_new,
            down_g,
            down_r_new.reshape(-1),
            down_c_new.reshape(-1),
            down_new,
            gain_grad,
            gain_s,
            gain_n,
            small_grad.T,
            small_s.T,
            small_n.T,
        )

    return body


def solution(mesh):
    return jax.shard_map(
        build(mesh.shape["crop"], mesh.shape["row"]),
        mesh=mesh,
        in_specs=(
            P("crop", "row", None, None),
            P("crop"),
            P("crop", "row", None),
            P("crop", "row", None),
            P("row", "crop"),
            P("row"),
            P("crop"),
            P("row", "crop"),
            P("row"),
            P("crop"),
            P(),
            P(),
            P(),
            P(),
        ),
        out_specs=(
            P(),
            P(),
            P("row", "crop"),
            P("row"),
            P("crop"),
            P("row", "crop"),
            P("row", "crop"),
            P("row"),
            P("crop"),
            P("row", "crop"),
            P(),
            P(),
            P(),
            P(),
            P(),
            P(),
        ),
        check_vma=False,
    )
```

time: 878 us -> 226 us (0.26)
  matrix products: 325 us -> 1.63 us
  blocking collectives: 249 us -> 0 us
  Pallas kernels: 0 us -> 135 us
  other arithmetic: 146 us -> 13.5 us
  local copies, waits for them, and re-layouts: 63.4 us -> 6.55 us
  waiting for transfers between devices: 65.8 us -> 29.5 us
  starting transfers between devices: 0.34 us -> 36.3 us
  between operations: 22.5 us -> 1.56 us
    dot_general x24 -> x1, matrix products: 325 us -> 1.63 us  [body(): lax.dot_general(d_bias, zbt, (((1, 2), (0, 2)), ((), ())), preferred_elem...]
    pallas_call x0 -> x7, Pallas kernels: none -> 135 us  [call(): pl.pallas_call(kernel, grid=(grid,), in_specs=in_specs, out_specs=[o[0] f...]
    psum x3 -> x0, blocking collectives: 122 us -> none  [the longest x2 84.6 us: body(): lax.psum((loss_local, jnp.sum(mask)), ('crop', 'row'))]
    unnamed x1 -> x0, blocking collectives: 76.4 us -> none
    sub x6 -> x0, other arithmetic: 64.2 us -> none  [the longest x1 58.8 us: rest(): probs = rounded(jax.nn.softmax(score, -1))]
    unnamed x6 -> x0, waiting for transfers between devices: 63.1 us -> none
    all_gather x4 -> x0, blocking collectives: 51.1 us -> none  [the longest x1 21.5 us: body(): lax.all_gather(down.astype(jnp.bfloat16), 'row', axis=0, tiled=True)]
    reduce_sum x16 -> x5, other arithmetic: 41.4 us -> 3.47 us  [the longest x1 1.02 us: body(): extras = jnp.sum(packs[:, :2, after:after + stats.size].astype(f32), 1)]
  transfers between devices with their start and end apart: 4 -> 18, of which waited for: 3 -> 11; matrix products, arithmetic and copies ran while one was open for 7% -> 6% of each run, Pallas kernels for 0% -> 28%
where the time goes in v2:
time: 226 us; the launch traced here: 224 us
  Pallas kernels  135 us (60%)
  starting transfers between devices  36.3 us (16%)
  waiting for transfers between devices  29.5 us (13%)
  other arithmetic  13.5 us (6%)
  local copies, waits for them, and re-layouts  6.55 us (3%)
    pallas_call x7, Pallas kernels, call(): pl.pallas_call(kernel, grid=(grid,), in_specs=in_specs, out_specs=[o[0] f...  135 us
    ppermute x15, waiting for transfers between devices, swap(): return lax.ppermute(x, axes, [(i, i ^ mask) for i in range(size)])  29.4 us
    ppermute x15, starting transfers between devices, swap(): return lax.ppermute(x, axes, [(i, i ^ mask) for i in range(size)])  19.2 us
    all_to_all x1, starting transfers between devices, body(): early = lax.all_to_all(early, both, 0, 0, tiled=True)  6.26 us
    all_to_all x1, starting transfers between devices, body(): d_bias = lax.all_to_all(d_bias, 'row', 0, 0, tiled=True)  5.93 us
    all_to_all x1, starting transfers between devices, body(): lax.all_to_all(early.reshape(devices, -1, CZ), both, 0, 0, tiled=True)  4.89 us
  transfers between devices with their start and end apart: 18, of which 11 were waited for; matrix products, arithmetic and copies ran while one was open for 6% of the time, Pallas kernels for 28%

profile of v2, /device:TPU:0, one launch (start us, length us, event | category | flops | bytes accessed | tf_op | source)
XLA Modules:
  0.0 224.5 jit_solution(1826760516504940602)
XLA Ops:
  2.8 6.9 %front.1 = (bf16[24,128,384]{2,1,0:T(8,128)(2,1)}, bf16[24,128,384]{2,1,0:T(8,128)(2,1)}, bf16[4,24,384]{2,1,0:T(8,128)(2,1)}, bf16[8,960]{1,0:T(8,128)(2,1)}) custom-call(bf16[24,384,128]{2,1,0:T(8,128)(2,1)} %bitcast.36, f32[3,128]{1,0:T(4,128)} %gains_ref.5, f32[68,128]{1,0:T(8,128)} %bitcast.37, f32[8,576]{1,0:T(8,128)} %wide_ref.3, f32[32,64]{1,0:T(8,128)} %down_ref.3, ...), custom_call_target="tpu_custom_call" | custom-call | flops 4800000000 | bytes 1048576 | tf_op jit(solution)/shard_map/front/pallas_call | solution.py:636
  9.7 4.1 %collective-permute-start = (bf16[1,8,960]{2,1,0:T(8,128)(2,1)}, bf16[1,8,960]{2,1,0:T(8,128)(2,1)S(1)}, u32[]{:S(2)}, u32[]{:S(2)}) collective-permute-start(bf16[1,8,960]{2,1,0:T(8,128)(2,1)} %bitcast.30), channel_id=1, source_target_pairs={{0,8},{1,9},{2,10},{3,11},{4,12},{5,13},{6,14},{7,15},{8,0},{9,1},... | collective-permute-start | bytes 46088 | tf_op jit(solution)/shard_map/ppermute | solution.py:868
  16.4 2.0 collective-permute-start.1
  18.4 1.9 collective-permute-done.1
  21.1 2.0 collective-permute-start.2
  23.1 2.3 %collective-permute-done.2 = bf16[4,8,960]{2,1,0:T(8,128)(2,1)S(1)} collective-permute-done((bf16[4,8,960]{2,1,0:T(8,128)(2,1)S(1)}, bf16[4,8,960]{2,1,0:T(8,128)(2,1)S(1)}, u32[]{:S(2)}, u32[]{:S(2)}) %collective-permute-start.2) | collective-permute-done | bytes 61472 | tf_op jit(solution)/shard_map/ppermute | solution.py:868
  26.1 2.0 collective-permute-start.3
  32.5 1.7 collective-permute-done.6
  35.1 1.6 collective-permute-start.7
  37.6 9.3 %project.1 = (bf16[24,384,384]{2,1,0:T(8,128)(2,1)}, f32[24,128,384]{2,1,0:T(8,128)}, bf16[24,384,256]{2,1,0:T(8,128)(2,1)}, f32[8,9216]{1,0:T(8,128)}, bf16[128...) custom-call(s32[4]{0:T(128)} %pad_add_fusion.info_ref, bf16[32,8,960]{2,1,0:T(8,128)(2,1)} %copy-done.4, ...), custom_call_target="tpu_custom_call" | custom-call | flops 6400000000 | bytes 1048576 | tf_op jit(solution)/shard_map/project/pallas_call | solution.py:636
  47.1 2.0 collective-permute-done.8
  50.2 27.9 %attend.1 = (bf16[24,384,1536]{2,1,0:T(8,128)(2,1)}, f32[24,128,384]{2,1,0:T(8,128)}, f32[24,8,384]{2,1,0:T(8,128)}) custom-call(s32[4]{0:T(128)} %pad_add_fusion.info_ref, f32[8,9216]{1,0:T(8,128)} %get-tuple-element.61.norm_ref, bf16[16,4,24,384]{3,2,1,0:T(8,128)(2,1)} %pad_maximum_fusion.bias_ref, ...), custom_call_target="tpu_custom_call" | custom-call | flops 20000000000 | bytes 1048576 | tf_op jit(solution)/shard_map/attend/pallas_call | solution.py:636
  78.1 35.1 %middle.1 = (bf16[24,128,384]{2,1,0:T(8,128)(2,1)}, bf16[24,64,384]{2,1,0:T(8,128)(2,1)}, bf16[12,128,128]{2,1,0:T(8,128)(2,1)}, bf16[16,128]{1,0:T(8,128)(2,1)}) custom-call(s32[4]{0:T(128)} %pad_add_fusion.info_ref, bf16[128,1152]{1,0:T(8,128)(2,1)} %get-tuple-element.56.wide_ref.full_ref, bf16[512,128]{1,0:T(8,128)(2,1)} %get-tuple-element.57.down_ref, ...), custom_call_target="tpu_custom_call" | custom-call | flops 24000000000 | bytes 1048576 | tf_op jit(solution)/shard_map/middle/pallas_call | solution.py:636
  113.2 4.9 %all-to-all-start = ((bf16[32,48,128]{2,1,0:T(8,128)(2,1)}), bf16[32,48,128]{2,1,0:T(8,128)(2,1)S(1)}, u32[]{:S(2)}, u32[]{:S(2)}) async-start(bf16[32,48,128]{2,1,0:T(8,128)(2,1)} %bitcast.29), calls=%async_computation | async-start | bytes 786432 | tf_op jit(solution)/shard_map/all_to_all | solution.py:969
  118.1 16.6 %score.1 = bf16[16,4,24,384]{3,2,1,0:T(8,128)(2,1)} custom-call(bf16[24,384,1536]{2,1,0:T(8,128)(2,1)} %get-tuple-element.69.p_ref, bf16[24,384,256]{2,1,0:T(8,128)(2,1)} %get-tuple-element.64.kn_ref.vn_ref, bf16[24,128,384]{2,1,0:T(8,128)(2,1)} %get-tuple-element.76.do_ref, bf16[24,64,384]{2,1,0:T(8,128)(2,1)} %get-tuple-element.71.nd_ref), custom_call_target="tpu_custom_call" | custom-call | flops 13600000000 | bytes 1048576 | tf_op jit(solution)/shard_map/score/pallas_call | solution.py:636
  135.7 5.9 %all-to-all-start.2 = ((bf16[16,4,24,384]{3,2,1,0:T(8,128)(2,1)}), bf16[16,4,24,384]{3,2,1,0:T(8,128)(2,1)S(1)}, u32[]{:S(2)}, u32[]{:S(2)}) async-start(bf16[16,4,24,384]{3,2,1,0:T(8,128)(2,1)} %score.1), calls=%async_computation.2 | async-start | bytes 2359296 | tf_op jit(solution)/shard_map/all_to_all | solution.py:980
  141.7 36.5 %back.1 = f32[3,128,128]{2,1,0:T(8,128)} custom-call(bf16[24,384,1536]{2,1,0:T(8,128)(2,1)} %get-tuple-element.69.p_ref, bf16[24,384,384]{2,1,0:T(8,128)(2,1)} %get-tuple-element.63.q_ref.v_ref.k_ref, bf16[24,384,384]{2,1,0:T(8,128)(2,1)} %get-tuple-element.63.q_ref.v_ref.k_ref, bf16[24,384,256]{2,1,0:T(8,128)(2,1)} %get-tuple-element.64.kn_ref.vn_ref, ...), custom_call_target="tpu_custom_call" | custom-call | flops 30400000000 | bytes 1048576 | tf_op jit(solution)/shard_map/back/pallas_call | solution.py:636
  178.2 6.3 %all-to-all-start.1 = ((bf16[32,64,128]{2,1,0:T(8,128)(2,1)}), bf16[32,64,128]{2,1,0:T(8,128)(2,1)}, u32[]{:S(2)}, u32[]{:S(2)}) async-start(bf16[32,64,128]{2,1,0:T(8,128)(2,1)} %broadcast_in_dim.48), calls=%async_computation.1 | async-start | bytes 1048576 | tf_op jit(solution)/shard_map/all_to_all | solution.py:976
  185.3 1.6 convolution_bitcast_fusion
  188.4 2.5 %collective-permute-start.10 = (f32[200,128]{1,0:T(8,128)S(1)}, f32[200,128]{1,0:T(8,128)S(1)}, u32[]{:S(2)}, u32[]{:S(2)}) collective-permute-start(f32[200,128]{1,0:T(8,128)S(1)} %dynamic-slice_add_fusion), channel_id=1, source_target_pairs={{0,8},{1,9},{2,10},{3,11},{4,12},{5,13},{6,14},{7,15},{8,0},{9,1},... | collective-permute-start | bytes 307208 | tf_op jit(solution)/shard_map/ppermute | solution.py:868
  190.8 12.7 %collective-permute-done.10 = f32[200,128]{1,0:T(8,128)S(1)} collective-permute-done((f32[200,128]{1,0:T(8,128)S(1)}, f32[200,128]{1,0:T(8,128)S(1)}, u32[]{:S(2)}, u32[]{:S(2)}) %collective-permute-start.10) | collective-permute-done | bytes 102432 | tf_op jit(solution)/shard_map/ppermute | solution.py:868
  205.2 3.0 %collective-permute-done.11 = f32[200,128]{1,0:T(8,128)S(1)} collective-permute-done((f32[200,128]{1,0:T(8,128)S(1)}, f32[200,128]{1,0:T(8,128)S(1)}, u32[]{:S(2)}, u32[]{:S(2)}) %collective-permute-start.11) | collective-permute-done | bytes 102432 | tf_op jit(solution)/shard_map/ppermute | solution.py:868
  215.7 2.2 collective-permute-done.13
  220.0 3.2 %finish.1 = (f32[8,576]{1,0:T(8,128)}, f32[1,8]{1,0:T(1,128)}, f32[1,576]{1,0:T(1,128)}, f32[8,576]{1,0:T(8,128)}, f32[32,64]{1,0:T(8,128)}, /*index=5*/f32[1,32...) custom-call(s32[4]{0:T(128)} %pad_add_fusion.info_ref, ...), custom_call_target="tpu_custom_call" | custom-call | flops 3200000000 | bytes 1048576 | tf_op jit(solution)/shard_map/finish/pallas_call | solution.py:636
  (79 shorter events, 28.8 us)
Async XLA Ops:
  9.7 6.0 %collective-permute-start = (bf16[1,8,960]{2,1,0:T(8,128)(2,1)}, bf16[1,8,960]{2,1,0:T(8,128)(2,1)S(1)}, u32[]{:S(2)}, u32[]{:S(2)}) collective-permute-start(bf16[1,8,960]{2,1,0:T(8,128)(2,1)} %bitcast.30), channel_id=1, source_target_pairs={{0,8},{1,9},{2,10},{3,11},{4,12},{5,13},{6,14},{7,15},{8,0},{9,1},... | collective-permute-start | bytes 46088 | tf_op jit(solution)/shard_map/ppermute | solution.py:868
  13.8 14.4 %collective-permute-start.5 = (bf16[1,4,24,384]{3,2,1,0:T(8,128)(2,1)}, bf16[1,4,24,384]{3,2,1,0:T(8,128)(2,1)S(1)}, u32[]{:S(2)}, u32[]{:S(2)}) collective-permute-start(bf16[1,4,24,384]{3,2,1,0:T(8,128)(2,1)} %bitcast.25), channel_id=1, source_target_pairs={{0,8},{1,9},{2,10},{3,11},{4,12},{5,13},{6,14},{7,15},{8,0},{9,1},... | collective-permute-start | bytes 221192 | tf_op jit(solution)/shard_map/ppermute | solution.py:868
  16.4 3.9 %collective-permute-start.1 = (bf16[2,8,960]{2,1,0:T(8,128)(2,1)S(1)}, bf16[2,8,960]{2,1,0:T(8,128)(2,1)S(1)}, u32[]{:S(2)}, u32[]{:S(2)}) collective-permute-start(bf16[2,8,960]{2,1,0:T(8,128)(2,1)S(1)} %pad_maximum_fusion.7), channel_id=1, source_target_pairs={{0,4},{1,5},{2,6},{3,7},{4,0},{5,1},{6,2},{7,3},{8,12},{9,13},{10,... | collective-permute-start | bytes 92168 | tf_op jit(solution)/shard_map/ppermute | solution.py:868
  21.1 4.3 %collective-permute-start.2 = (bf16[4,8,960]{2,1,0:T(8,128)(2,1)S(1)}, bf16[4,8,960]{2,1,0:T(8,128)(2,1)S(1)}, u32[]{:S(2)}, u32[]{:S(2)}) collective-permute-start(bf16[4,8,960]{2,1,0:T(8,128)(2,1)S(1)} %pad_maximum_fusion.6), channel_id=1, source_target_pairs={{0,2},{1,3},{2,0},{3,1},{4,6},{5,7},{6,4},{7,5},{8,10},{9,11},{10,... | collective-permute-start | bytes 184328 | tf_op jit(solution)/shard_map/ppermute | solution.py:868
  26.1 5.0 %collective-permute-start.3 = (bf16[8,8,960]{2,1,0:T(8,128)(2,1)S(1)}, bf16[8,8,960]{2,1,0:T(8,128)(2,1)S(1)}, u32[]{:S(2)}, u32[]{:S(2)}) collective-permute-start(bf16[8,8,960]{2,1,0:T(8,128)(2,1)S(1)} %pad_maximum_fusion.5), channel_id=1, source_target_pairs={{0,16},{1,17},{2,18},{3,19},{4,20},{5,21},{6,22},{7,23},{8,24},{9,... | collective-permute-start | bytes 368648 | tf_op jit(solution)/shard_map/ppermute | solution.py:868
  29.0 5.2 %collective-permute-start.6 = (bf16[2,4,24,384]{3,2,1,0:T(8,128)(2,1)S(1)}, bf16[2,4,24,384]{3,2,1,0:T(8,128)(2,1)S(1)}, u32[]{:S(2)}, u32[]{:S(2)}) collective-permute-start(bf16[2,4,24,384]{3,2,1,0:T(8,128)(2,1)S(1)} %pad_maximum_fusion.4), channel_id=1, source_target_pairs={{0,4},{1,5},{2,6},{3,7},{4,0},{5,1},{6,2},{7,3},{8,12},{9,13},{10,... | collective-permute-start | bytes 442376 | tf_op jit(solution)/shard_map/ppermute | solution.py:868
  31.2 5.6 %collective-permute-start.4 = (bf16[16,8,960]{2,1,0:T(8,128)(2,1)S(1)}, bf16[16,8,960]{2,1,0:T(8,128)(2,1)S(1)}, u32[]{:S(2)}, u32[]{:S(2)}) collective-permute-start(bf16[16,8,960]{2,1,0:T(8,128)(2,1)S(1)} %get-tuple-element.96), channel_id=1, source_target_pairs={{0,1},{1,0},{2,3},{3,2},{4,5},{5,4},{6,7},{7,6},{8,9},{9,8},{10,11... | collective-permute-start | bytes 737288 | tf_op jit(solution)/shard_map/ppermute | solution.py:868
  35.1 11.8 %collective-permute-start.7 = (bf16[4,4,24,384]{3,2,1,0:T(8,128)(2,1)S(1)}, bf16[4,4,24,384]{3,2,1,0:T(8,128)(2,1)S(1)}, u32[]{:S(2)}, u32[]{:S(2)}) collective-permute-start(bf16[4,4,24,384]{3,2,1,0:T(8,128)(2,1)S(1)} %pad_maximum_fusion.2), channel_id=1, source_target_pairs={{0,2},{1,3},{2,0},{3,1},{4,6},{5,7},{6,4},{7,5},{8,10},{9,11},{10,... | collective-permute-start | bytes 884744 | tf_op jit(solution)/shard_map/ppermute | solution.py:868
  36.8 0.8 copy-start.4
  37.6 9.3 %copy-start.1 = (bf16[4,24,384]{2,1,0:T(8,128)(2,1)S(1)}, bf16[4,24,384]{2,1,0:T(8,128)(2,1)}, u32[]{:S(2)}) copy-start(bf16[4,24,384]{2,1,0:T(8,128)(2,1)} %get-tuple-element.59) | copy-start | bytes 221188
  47.0 2.1 collective-permute-start.8
  113.2 21.5 %all-to-all-start = ((bf16[32,48,128]{2,1,0:T(8,128)(2,1)}), bf16[32,48,128]{2,1,0:T(8,128)(2,1)S(1)}, u32[]{:S(2)}, u32[]{:S(2)}) async-start(bf16[32,48,128]{2,1,0:T(8,128)(2,1)} %bitcast.29), calls=%async_computation | async-start | bytes 786432 | tf_op jit(solution)/shard_map/all_to_all | solution.py:969
  118.1 16.7 %copy-start.3 = (bf16[16,128]{1,0:T(8,128)(2,1)S(1)}, bf16[16,128]{1,0:T(8,128)(2,1)}, u32[]{:S(2)}) copy-start(bf16[16,128]{1,0:T(8,128)(2,1)} %get-tuple-element.73) | copy-start | bytes 12292
  135.7 42.5 %all-to-all-start.2 = ((bf16[16,4,24,384]{3,2,1,0:T(8,128)(2,1)}), bf16[16,4,24,384]{3,2,1,0:T(8,128)(2,1)S(1)}, u32[]{:S(2)}, u32[]{:S(2)}) async-start(bf16[16,4,24,384]{3,2,1,0:T(8,128)(2,1)} %score.1), calls=%async_computation.2 | async-start | bytes 2359296 | tf_op jit(solution)/shard_map/all_to_all | solution.py:980
  141.6 43.6 %copy-start = (bf16[24,128,384]{2,1,0:T(8,128)(2,1)S(1)}, bf16[24,128,384]{2,1,0:T(8,128)(2,1)}, u32[]{:S(2)}) copy-start(bf16[24,128,384]{2,1,0:T(8,128)(2,1)} %get-tuple-element.55.zbt_ref) | copy-start | bytes 7077892
  178.2 36.5 %all-to-all-start.1 = ((bf16[32,64,128]{2,1,0:T(8,128)(2,1)}), bf16[32,64,128]{2,1,0:T(8,128)(2,1)}, u32[]{:S(2)}, u32[]{:S(2)}) async-start(bf16[32,64,128]{2,1,0:T(8,128)(2,1)} %broadcast_in_dim.48), calls=%async_computation.1 | async-start | bytes 1048576 | tf_op jit(solution)/shard_map/all_to_all | solution.py:976
  185.3 1.6 copy-start.2
  187.0 1.4 collective-permute-start.9
  188.4 15.1 %collective-permute-start.10 = (f32[200,128]{1,0:T(8,128)S(1)}, f32[200,128]{1,0:T(8,128)S(1)}, u32[]{:S(2)}, u32[]{:S(2)}) collective-permute-start(f32[200,128]{1,0:T(8,128)S(1)} %dynamic-slice_add_fusion), channel_id=1, source_target_pairs={{0,8},{1,9},{2,10},{3,11},{4,12},{5,13},{6,14},{7,15},{8,0},{9,1},... | collective-permute-start | bytes 307208 | tf_op jit(solution)/shard_map/ppermute | solution.py:868
  203.5 4.7 %collective-permute-start.11 = (f32[200,128]{1,0:T(8,128)S(1)}, f32[200,128]{1,0:T(8,128)S(1)}, u32[]{:S(2)}, u32[]{:S(2)}) collective-permute-start(f32[200,128]{1,0:T(8,128)S(1)} %add.110), channel_id=1, source_target_pairs={{0,4},{1,5},{2,6},{3,7},{4,0},{5,1},{6,2},{7,3},{8,12},{9,13},{10,... | collective-permute-start | bytes 307208 | tf_op jit(solution)/shard_map/ppermute | solution.py:868
  208.3 4.9 %collective-permute-start.12 = (f32[200,128]{1,0:T(8,128)S(1)}, f32[200,128]{1,0:T(8,128)S(1)}, u32[]{:S(2)}, u32[]{:S(2)}) collective-permute-start(f32[200,128]{1,0:T(8,128)S(1)} %add.111), channel_id=1, source_target_pairs={{0,2},{1,3},{2,0},{3,1},{4,6},{5,7},{6,4},{7,5},{8,10},{9,11},{10,... | collective-permute-start | bytes 307208 | tf_op jit(solution)/shard_map/ppermute | solution.py:868
  213.2 4.7 %collective-permute-start.13 = (f32[200,128]{1,0:T(8,128)S(1)}, f32[200,128]{1,0:T(8,128)S(1)}, u32[]{:S(2)}, u32[]{:S(2)}) collective-permute-start(f32[200,128]{1,0:T(8,128)S(1)} %add.112), channel_id=1, source_target_pairs={{0,16},{1,17},{2,18},{3,19},{4,20},{5,21},{6,22},{7,23},{8,24},{9,... | collective-permute-start | bytes 307208 | tf_op jit(solution)/shard_map/ppermute | solution.py:868
  217.9 1.4 collective-permute-start.14

commit v3 on v2

--- a/solution.py
+++ b/solution.py
@@ -21,6 +21,7 @@
 ROOT = 1.0 / math.sqrt(HEAD_DIM)
 BLK = 256
 SAFE = 40.0
+STATS = 256
 
 GATE_BLOCK, OUT_BLOCK, IN_BLOCK, DOWN_BLOCK, HEAD_BLOCK, BLOCKS = 0, 1, 2, 6, 10, 12
 
@@ -88,21 +89,35 @@
     return where
 
 
+def pack_kernel(
+    wide_ref, down_ref, wide_rows_ref, down_rows_ref, wide_cols_ref, down_cols_ref, pack_ref, pack
+):
+    lines, cols = wide_ref.shape
+    span = down_ref.shape[1]
+    pack[...] = jnp.zeros_like(pack)
+    for at, ref in ((0, wide_rows_ref), (lines, down_rows_ref)):
+        some = ref[...].reshape(1, -1)
+        upper = rounded(some)
+        pack[0:1, at : at + some.shape[1]] = upper
+        pack[1:2, at : at + some.shape[1]] = some - upper
+    stats = jnp.concatenate(
+        [wide_cols_ref[...].reshape(1, -1), down_cols_ref[...].reshape(1, -1)], 1
+    )
+    for part in range(-(-stats.shape[1] // STATS)):
+        some = stats[:, part * STATS : (part + 1) * STATS]
+        upper = rounded(some)
+        pack[2 + part : 3 + part, : some.shape[1]] = upper
+        pack[5 + part : 6 + part, : some.shape[1]] = some - upper
+    pack[:lines, STATS : STATS + cols] = wide_ref[...]
+    for part in range(FF // CZ):
+        at = STATS + cols + part * span
+        pack[:lines, at : at + span] = down_ref[part * lines : (part + 1) * lines, :]
+    for peer in range(pack_ref.shape[0]):
+        pack_ref[peer] = pack[...].astype(bf16)
+
+
 def front_kernel(
-    pair_ref,
-    gains_ref,
-    small_ref,
-    wide_ref,
-    down_ref,
-    stats_ref,
-    zt_ref,
-    zbt_ref,
-    bias_ref,
-    pack_ref,
-    gain,
-    wb,
-    part,
-    pack,
+    pair_ref, gains_ref, small_ref, zt_ref, zbt_ref, bias_ref, gain, wb, part
 ):
     rows, width, _ = pair_ref.shape
     step = pl.program_id(0)
@@ -111,20 +126,6 @@
     def _():
         columns_of(gains_ref, 0, gain)
         wb[...] = small_ref[:16].astype(bf16)
-        lines, cols = wide_ref.shape
-        span = down_ref.shape[1]
-        pack[...] = jnp.zeros_like(pack)
-        pack[:lines, :cols] = wide_ref[...]
-        for at in range(FF // CZ):
-            pack[:lines, cols + at * span : cols + (at + 1) * span] = down_ref[
-                at * lines : (at + 1) * lines, :
-            ]
-        after = cols + (FF // CZ) * span
-        stats = stats_ref[...]
-        upper = rounded(stats)
-        pack[0:1, after : after + stats.shape[1]] = upper
-        pack[1:2, after : after + stats.shape[1]] = stats - upper
-        pack_ref[...] = pack[...].astype(bf16)
 
     x = pair_ref[...].astype(f32).reshape(rows * width, CZ).T
     spread(zt_ref, x.astype(bf16))
@@ -141,19 +142,27 @@
         bias_ref[...] = part[...].astype(bf16)
 
 
+def pick(info_ref, mine_ref, other_ref, crop, row, rows):
+    chip = crop * (rows // 2) + row // 2
+    side = info_ref[0] & 1
+    return jnp.where(
+        side == row % 2, mine_ref[chip].astype(f32), other_ref[chip].astype(f32)
+    )
+
+
 def project_kernel(
     crops,
     rows,
-    masks,
     info_ref,
-    packs_ref,
+    mine_ref,
+    other_ref,
     zbt_ref,
     qkv_ref,
-    gate_ref,
-    kvn_ref,
+    vn_ref,
     norm_ref,
     wide_ref,
     down_ref,
+    done_ref,
     wide_s,
     down_s,
     wqt,
@@ -162,27 +171,26 @@
 
     @pl.when(pl.program_id(0) == 0)
     def _():
-        me = info_ref[1] * rows + info_ref[0]
         for c in range(crops):
             for r in range(rows):
-                block = packs_ref[place(c * rows + r, me, masks)].astype(f32)[:lines]
-                wide_s[r * lines : (r + 1) * lines, c * cols : (c + 1) * cols] = block[:, :cols]
+                block = pick(info_ref, mine_ref, other_ref, c, r, rows)[:lines]
+                wide_s[r * lines : (r + 1) * lines, c * cols : (c + 1) * cols] = block[
+                    :, STATS : STATS + cols
+                ]
                 for part in range(FF // CZ):
                     at = (r * (FF // CZ) + part) * lines
-                    down_s[at : at + lines, c * span : (c + 1) * span] = block[
-                        :, cols + part * span : cols + (part + 1) * span
-                    ]
+                    left = STATS + cols + part * span
+                    down_s[at : at + lines, c * span : (c + 1) * span] = block[:, left : left + span]
         wide_ref[...] = wide_s[...].astype(bf16)
         down_ref[...] = down_s[...].astype(bf16)
-        wqt[...] = wide_s[:, : 4 * CZ].T.astype(bf16)
-
-    proj = dot(wqt[...], lanes(zbt_ref))
-    qkv = proj[: 3 * CZ].astype(bf16)
+        wqt[...] = wide_s[:, : 3 * CZ].T.astype(bf16)
+        done_ref[...] = jnp.zeros_like(done_ref)
+
+    qkv = dot(wqt[...], lanes(zbt_ref)).astype(bf16)
     spread(qkv_ref, qkv)
-    spread(gate_ref, sigmoid(proj[3 * CZ :]))
     q = qkv[:CZ].astype(f32)
     k = qkv[CZ : 2 * CZ].astype(f32)
-    kvn_ref[...] = qkv[CZ:].T.reshape(kvn_ref.shape)
+    vn_ref[...] = qkv[2 * CZ :].T.reshape(vn_ref.shape)
     norm_ref[...] = jnp.concatenate(
         [
             jnp.sum((x * x)[h * HEAD_DIM : (h + 1) * HEAD_DIM], 0, keepdims=True)
@@ -198,8 +206,9 @@
     info_ref,
     norm_ref,
     bias_ref,
+    other_bias_ref,
     q_ref,
-    kn_ref,
+    k_ref,
     v_ref,
     p_ref,
     o_ref,
@@ -211,7 +220,8 @@
     bound,
 ):
     group, _, width = q_ref.shape
-    shards, _, rows, _ = bias_ref.shape
+    rows = bias_ref.shape[2]
+    shards = width // rows
     step = pl.program_id(0)
 
     @pl.when(step == 0)
@@ -221,7 +231,12 @@
         kb = jnp.where(key < info_ref[2], 0.0, -1000000000.0 * LOG2E)
         for h in range(HEADS):
             for s in range(shards):
-                nat[s * rows : (s + 1) * rows, :] = bias_ref[place(s, info_ref[0], masks), h].astype(f32)
+                at = place(s, info_ref[0], masks[:-1])
+                block = bias_ref[at, h].astype(f32)
+                if shards > 1:
+                    here = (info_ref[0] & 1) == s % 2
+                    block = jnp.where(here, block, other_bias_ref[at, h].astype(f32))
+                nat[s * rows : (s + 1) * rows, :] = block
             top = jnp.maximum(top, jnp.max(jnp.abs(nat[...])))
             biast[:, h * width : (h + 1) * width] = (nat[...] * LOG2E + kb).T
         bound[0] = top * LOG2E
@@ -235,8 +250,9 @@
                 a, b = h * HEAD_DIM, (h + 1) * HEAD_DIM
                 qbd[g, a:b, h * width : (h + 1) * width] = high[a:b]
                 qbd[g, CZ + a : CZ + b, h * width : (h + 1) * width] = low[a:b]
-            kk[g, :, :CZ] = kn_ref[g]
-            kk[g, :, CZ:] = kn_ref[g]
+            kn = k_ref[g].T
+            kk[g, :, :CZ] = kn
+            kk[g, :, CZ:] = kn
             sums = []
             for c in range(0, HEADS * width, BLK):
                 s = dot(kk[g], qbd[g, :, c : c + BLK]) + biast[:, c : c + BLK]
@@ -274,7 +290,6 @@
     zt_ref,
     zbt_ref,
     o_ref,
-    gate_ref,
     r_ref,
     tgt_ref,
     nbr_ref,
@@ -286,6 +301,7 @@
     sums,
     g1,
     g2,
+    wgt,
     wot,
     wint,
     wdownt,
@@ -300,106 +316,142 @@
     def _():
         wo = wide_ref[:, 4 * CZ : 5 * CZ]
         wot[...] = wo.T
-        wint[...] = wide_ref[:, 5 * CZ :].T
+        wgt[...] = wide_ref[:, 3 * CZ : 4 * CZ].T
+        wint[...] = wide_ref[:, 5 * CZ :].T * 0.5
         wdownt[...] = down_ref[...].T
         head = head_ref[...][HEADS:]
         wht[...] = head.astype(bf16)
         head = head.T.astype(bf16)
         wo2[...] = jnp.concatenate([wo, wo], 1)
-        wdown2[...] = jnp.concatenate([down_ref[...], down_ref[...]], 1)
+        wdown2[...] = jnp.concatenate([down_ref[...], down_ref[...]], 1) * 0.5
         wh2[...] = jnp.concatenate([head, head], 1)
         acc[...] = jnp.zeros_like(acc)
         columns_of(gains_ref, 1, g1)
         columns_of(gains_ref, 2, g2)
         sums[...] = jnp.zeros_like(sums)
 
-    o = lanes(o_ref)
-    gate = lanes(gate_ref)
-    gain1 = wider(g1[...], o)
-    gain2 = wider(g2[...], o)
+    group, _, width = o_ref.shape
+    first = step * group
 
     def add(block, grad):
         for c in range(0, grad.shape[1], CZ):
             acc[block + c // CZ] += grad[:, c : c + CZ]
 
-    og = (o * gate).astype(bf16)
-    z1 = lanes(zt_ref).astype(f32) + dot(wot[...], og)
-    xhat1, inv1 = normed(z1)
-    zb2 = (xhat1 * gain1).astype(bf16)
-    hidden, slopes = [], []
-    for f in range(0, FF, CZ):
-        hid = dot(wint[f : f + CZ], zb2)
-        sg = sigmoid(hid)
-        act = hid * sg
-        hidden.append(act.astype(bf16))
-        slopes.append(sg + act * (1.0 - sg))
-    a = jnp.concatenate(hidden, 0)
-    z2 = z1 + dot(wdownt[...], a)
-    xhat2, inv2 = normed(z2)
-    zb3 = (xhat2 * gain2).astype(bf16)
-    logits = dot(wht[...], zb3)
-    top = jnp.max(logits, 0, keepdims=True)
-    ex = jnp.exp(logits - top)
-    total = jnp.sum(ex, 0, keepdims=True)
-    group, _, width = o_ref.shape
-    first = step * group
-    target = jnp.concatenate([tgt_ref[0, pl.ds(first + g, 1), :] for g in range(group)], 1)
-    hot = lax.broadcasted_iota(jnp.int32, logits.shape, 0) == target
-    picked = jnp.sum(jnp.where(hot, logits, 0.0), 0, keepdims=True)
-    column = lax.broadcasted_iota(jnp.int32, (1, width), 1)
-    length = info_ref[2]
-    mask = jnp.concatenate(
-        [
-            jnp.where(
-                (nbr_ref[0, pl.ds(first + g, 1), :] > 0)
-                & (column < jnp.where(info_ref[0] * info_ref[3] + first + g < length, length, 0)),
-                1.0,
-                0.0,
+    def stages(low, high):
+        spots = [divmod(block * 128, width) for block in range(low, high)]
+
+        def mine(ref):
+            return jnp.concatenate([ref[g, :, at : at + 128] for g, at in spots], 1)
+
+        def line(ref):
+            return jnp.concatenate(
+                [ref[0, pl.ds(first + g, 1), :][:, at : at + 128] for g, at in spots], 1
             )
-            for g in range(group)
-        ],
-        1,
-    )
-    sums[0:1] += (jnp.log(total) + top - picked) * mask
-    sums[1:2] += mask
-
-    dl = ex * (mask / total) - jnp.where(hot, mask, 0.0)
-    dl2 = jnp.concatenate(halves(dl), 0)
-    add(HEAD_BLOCK, dot_nt(dl2, zb3))
-    dzb3 = rounded(dot(wh2[...], dl2))
-    dz2 = normed_back(dzb3 * gain2, xhat2, inv2)
-    high2, low2 = halves(dz2)
-    both2 = jnp.concatenate([high2, low2], 0)
-    dh = jnp.concatenate(
-        [
-            (dot(wdown2[f : f + CZ], both2) * slopes[f // CZ]).astype(bf16)
-            for f in range(0, FF, CZ)
-        ],
-        0,
-    )
-    add(DOWN_BLOCK, dot_nt(high2, a))
-    dzb2 = rounded(dot(wide_ref[:, 5 * CZ :], dh))
-    add(IN_BLOCK, dot_nt(zb2, dh))
-    dz1 = dz2 + normed_back(dzb2 * gain1, xhat1, inv1)
-    high1, low1 = halves(dz1)
-    add(OUT_BLOCK, dot_nt(og, high1))
-    dog = rounded(dot(wo2[...], jnp.concatenate([high1, low1], 0)))
-    do = dog * gate
-    doo = do * o
-    add(GATE_BLOCK, dot_nt(lanes(zbt_ref), (doo * (1.0 - gate)).astype(bf16)))
-    r = lanes(r_ref)
-    parts, minus = [], []
-    for h in range(HEADS):
-        x, y = h * HEAD_DIM, (h + 1) * HEAD_DIM
-        mine = r[h : h + 1]
-        parts.append((do[x:y] * mine).astype(bf16))
-        less = -jnp.sum(doo[x:y], 0, keepdims=True) * mine
-        upper = rounded(less)
-        minus.append(
-            jnp.concatenate([upper, less - upper, jnp.zeros((14, less.shape[1]), f32)], 0)
+
+        def out(ref, x):
+            for n, (g, at) in enumerate(spots):
+                ref[g, :, at : at + 128] = x[:, n * 128 : (n + 1) * 128]
+
+        o = mine(o_ref)
+        zb = mine(zbt_ref)
+        gate = sigmoid(dot(wgt[...], zb))
+        gain1 = wider(g1[...], o)
+        gain2 = wider(g2[...], o)
+        og = (o * gate).astype(bf16)
+        z1 = mine(zt_ref).astype(f32) + dot(wot[...], og)
+        yield
+        xhat1, inv1 = normed(z1)
+        zb2 = (xhat1 * gain1).astype(bf16)
+        yield
+        hidden, slopes = [], []
+        for f in range(0, FF, CZ):
+            hid = dot(wint[f : f + CZ], zb2)
+            t = jnp.tanh(hid)
+            sg = 1.0 + t
+            act = hid * sg
+            hidden.append(act.astype(bf16))
+            slopes.append(sg + act * (1.0 - t))
+            yield
+        a = jnp.concatenate(hidden, 0)
+        z2 = z1 + dot(wdownt[...], a)
+        yield
+        xhat2, inv2 = normed(z2)
+        zb3 = (xhat2 * gain2).astype(bf16)
+        logits = dot(wht[...], zb3)
+        yield
+        top = jnp.max(logits, 0, keepdims=True)
+        ex = jnp.exp(logits - top)
+        total = jnp.sum(ex, 0, keepdims=True)
+        hot = lax.broadcasted_iota(jnp.int32, logits.shape, 0) == line(tgt_ref)
+        picked = jnp.sum(jnp.where(hot, logits, 0.0), 0, keepdims=True)
+        column = lax.broadcasted_iota(jnp.int32, (1, 128), 1)
+        length = info_ref[2]
+        valid = jnp.concatenate(
+            [
+                column + at < jnp.where(info_ref[0] * info_ref[3] + first + g < length, length, 0)
+                for g, at in spots
+            ],
+            1,
         )
-    spread(do_ref, jnp.concatenate(parts, 0))
-    spread(nd_ref, jnp.concatenate(minus, 0).astype(bf16))
+        mask = jnp.where((line(nbr_ref) > 0) & valid, 1.0, 0.0)
+        at = slice(0, mask.shape[1])
+        sums[0:1, at] += (jnp.log(total) + top - picked) * mask
+        sums[1:2, at] += mask
+        dl = ex * (mask / total) - jnp.where(hot, mask, 0.0)
+        dl2 = jnp.concatenate(halves(dl), 0)
+        yield
+        add(HEAD_BLOCK, dot_nt(dl2, zb3))
+        dzb3 = rounded(dot(wh2[...], dl2))
+        yield
+        dz2 = normed_back(dzb3 * gain2, xhat2, inv2)
+        high2, low2 = halves(dz2)
+        both2 = jnp.concatenate([high2, low2], 0)
+        yield
+        dh = []
+        for f in range(0, FF, CZ):
+            dh.append((dot(wdown2[f : f + CZ], both2) * slopes[f // CZ]).astype(bf16))
+            yield
+        dh = jnp.concatenate(dh, 0)
+        add(DOWN_BLOCK, dot_nt(high2, a))
+        yield
+        dzb2 = rounded(dot(wide_ref[:, 5 * CZ :], dh))
+        yield
+        add(IN_BLOCK, dot_nt(zb2, dh))
+        dz1 = dz2 + normed_back(dzb2 * gain1, xhat1, inv1)
+        high1, low1 = halves(dz1)
+        yield
+        add(OUT_BLOCK, dot_nt(og, high1))
+        dog = rounded(dot(wo2[...], jnp.concatenate([high1, low1], 0)))
+        yield
+        do = dog * gate
+        doo = do * o
+        add(GATE_BLOCK, dot_nt(zb, (doo * (1.0 - gate)).astype(bf16)))
+        yield
+        r = mine(r_ref)
+        parts, minus = [], []
+        for h in range(HEADS):
+            x, y = h * HEAD_DIM, (h + 1) * HEAD_DIM
+            share = r[h : h + 1]
+            parts.append((do[x:y] * share).astype(bf16))
+            less = -jnp.sum(doo[x:y], 0, keepdims=True) * share
+            upper = rounded(less)
+            minus.append(
+                jnp.concatenate([upper, less - upper, jnp.zeros((14, less.shape[1]), f32)], 0)
+            )
+        out(do_ref, jnp.concatenate(parts, 0))
+        out(nd_ref, jnp.concatenate(minus, 0).astype(bf16))
+
+    blocks = group * width // 128
+    running = [
+        stages(low, min(low + MIDDLE_PART, blocks)) for low in range(0, blocks, MIDDLE_PART)
+    ]
+    turn = 0
+    waiting = list(enumerate(running))
+    while waiting:
+        for item in list(waiting):
+            if turn >= item[0] * MIDDLE_LAG and next(item[1], item) is item:
+                waiting.remove(item)
+        turn += 1
 
     @pl.when(step == pl.num_programs(0) - 1)
     def _():
@@ -416,7 +468,7 @@
         scalars_ref[...] = out.astype(bf16)
 
 
-def score_kernel(p_ref, vn_ref, do_ref, nd_ref, dbias_ref, acc, dobd, vv):
+def score_kernel(info_ref, p_ref, vn_ref, do_ref, nd_ref, keep_ref, give_ref, acc, dobd, vv, nat):
     group, _, width = do_ref.shape
     step = pl.program_id(0)
 
@@ -434,11 +486,25 @@
 
     @pl.when(step == pl.num_programs(0) - 1)
     def _():
-        owners, _, lines, _ = dbias_ref.shape
+        chips, tall, _ = keep_ref.shape
+        lines = width // (2 * chips)
+        first = (info_ref[0] & 1) == 0
         for h in range(HEADS):
-            mine = acc[:, h * width : (h + 1) * width].T
-            for r in range(owners):
-                dbias_ref[r, h] = mine[r * lines : (r + 1) * lines].astype(bf16)
+            nat[h] = acc[:, h * width : (h + 1) * width].T
+        for chip in range(chips):
+            sides = [
+                jnp.concatenate(
+                    [
+                        nat[h, (2 * chip + side) * lines : (2 * chip + side + 1) * lines, c : c + CZ]
+                        for c in range(0, width, CZ)
+                        for h in range(HEADS)
+                    ],
+                    0,
+                )
+                for side in range(2)
+            ]
+            keep_ref[chip] = jnp.where(first, sides[0], sides[1]).astype(bf16)
+            give_ref[chip] = jnp.where(first, sides[1], sides[0]).astype(bf16)
 
 
 def prepare(dobd, vv):
@@ -504,7 +570,7 @@
     update = weight_step(update, clip)
     scratch[...] = rows_new
     own_rows = jnp.broadcast_to(scratch[pl.ds(row_start, lines), :], (lines, CZ))
-    rows_out[...] = own_rows.T[:1]
+    rows_out[...] = own_rows.T[0]
 
     def own(x):
         part = x[:, :span]
@@ -513,7 +579,7 @@
         return part
 
     grad_out[...] = own(mine)
-    cols_out[...] = own(cols_new)
+    cols_out[...] = own(cols_new)[0]
     new_out[...] = weight_ref[...] - own(update)
 
 
@@ -532,14 +598,15 @@
 
 
 def finish_kernel(
+    crops,
+    rows,
     info_ref,
-    late_ref,
-    early_ref,
+    keep_ref,
+    other_ref,
+    spread_ref,
+    packs_ref,
+    other_packs_ref,
     full_ref,
-    wide_rows_ref,
-    wide_cols_ref,
-    down_rows_ref,
-    down_cols_ref,
     wide_ref,
     down_ref,
     gains_ref,
@@ -548,14 +615,31 @@
     small_second_ref,
     *refs,
 ):
-    outs, (flat, wide_s, down_s, wide_c, down_c) = refs[:14], refs[14:]
-    devices, lines, _ = early_ref.shape
-    lines -= 16
+    outs, (flat, late_ref, wide_s, down_s, wide_c, down_c, table, wide_cols, down_cols) = (
+        refs[:14],
+        refs[14:],
+    )
+    row, crop = info_ref[0], info_ref[1]
+    side = row & 1
+    half = keep_ref.shape[0]
+    mine, other = keep_ref[...], other_ref[...]
+    late_ref[:half, :] = jnp.where(side == 0, mine, other)
+    late_ref[half:, :] = jnp.where(side == 0, other, mine)
+
+    lines = BLOCKS * CZ // (crops * rows)
+    height = lines + 16
     tail = jnp.zeros((1, CZ), f32)
-    for d in range(devices):
-        block = early_ref[d].astype(f32)
-        flat[d * lines : (d + 1) * lines, :] = block[:lines]
-        tail += block[lines : lines + 1]
+    for c in range(crops):
+        for r in range(rows):
+            at = (c * rows + r) * lines
+            which = ((r % 2) ^ side) + 2 * (c ^ crop)
+            start = spread_ref.shape[1] - 2 * crops * height
+            block = jnp.zeros((height, CZ), f32)
+            for p in range(2 * crops):
+                some = spread_ref[r // 2, start + p * height : start + (p + 1) * height]
+                block = jnp.where(which == p, some.astype(f32), block)
+            flat[at : at + lines, :] = block[:lines]
+            tail += block[lines : lines + 1]
     scale = 1.0 / (tail[:, 1:2] + tail[:, 3:4] + tail[:, 5:6])
 
     def early(block):
@@ -578,27 +662,44 @@
     through = wide_s[...] * full_ref[...].astype(f32)
     behind = small_grad * rounded(small)
     lane = lax.broadcasted_iota(jnp.int32, (CZ, CZ), 1)
-    table = jnp.where(
+    gain_grad = jnp.where(
         lane == 0,
         jnp.sum(through[:, : 4 * CZ], 1, keepdims=True),
         jnp.sum(through[:, 5 * CZ :], 1, keepdims=True),
     ).T
-    table = jnp.concatenate(
-        [
-            table[:1] + jnp.sum(behind[:HEADS], 0, keepdims=True),
-            table[1:2],
+    gain_grad = jnp.concatenate(
+        [
+            gain_grad[:1] + jnp.sum(behind[:HEADS], 0, keepdims=True),
+            gain_grad[1:2],
             jnp.sum(behind[HEADS:], 0, keepdims=True),
         ],
         0,
     )
     gains = gains_ref[...]
-    plain(gains, table / gains, gain_second_ref[...], 0.3, outs[8:11])
-
-    row, crop = info_ref[0], info_ref[1]
+    plain(gains, gain_grad / gains, gain_second_ref[...], 0.3, outs[8:11])
+
+    per, down_per = CZ // rows, FF // rows
+    for r in range(rows):
+        block = pick(info_ref, packs_ref, other_packs_ref, 0, r, rows)
+        table[r : r + 1, :] = block[0:1, :CZ] + block[1:2, :CZ]
+
+    def column(size, start):
+        tall = jnp.broadcast_to(table[...][:, None, :], (rows, size, CZ)).reshape(rows * size, CZ)
+        lane = lax.broadcasted_iota(jnp.int32, tall.shape, 1)
+        line = lax.broadcasted_iota(jnp.int32, tall.shape, 0)
+        return jnp.sum(jnp.where(lane == start + line % size, tall, 0.0), 1, keepdims=True)
+
+    cols, span = WIDE // crops, CZ // crops
+    for c in range(crops):
+        block = pick(info_ref, packs_ref, other_packs_ref, c, 0, rows)[:, :STATS]
+        block = block[2:5] + block[5:8]
+        stats = jnp.concatenate([block[part : part + 1] for part in range(3)], 1)
+        wide_cols[:, c * cols : (c + 1) * cols] = stats[:, :cols]
+        down_cols[:, c * span : (c + 1) * span] = stats[:, cols : cols + span]
     factored(
         wide_s,
-        wide_rows_ref[...],
-        wide_cols_ref[...],
+        column(per, 0),
+        wide_cols[...],
         wide_ref,
         crop,
         row * wide_ref.shape[0],
@@ -607,14 +708,51 @@
     )
     factored(
         down_s,
-        down_rows_ref[...],
-        down_cols_ref[...],
+        column(down_per, per),
+        down_cols[...],
         down_ref,
         crop,
         row * down_ref.shape[0],
         down_c,
         outs[4:8],
     )
+
+
+def late_kernel(info_ref, spread_ref, dqkv_ref, zbt_ref, keep_ref, give_ref, dbias, acc, stack):
+    group, _, width = zbt_ref.shape
+    tall = dbias.shape[0]
+    lines = tall // (HEADS * (width // CZ))
+    step = pl.program_id(0)
+
+    @pl.when(step == 0)
+    def _():
+        total = spread_ref[0, :tall].astype(f32)
+        for chip in range(1, spread_ref.shape[0]):
+            total += spread_ref[chip, :tall].astype(f32)
+        dbias[...] = rounded(total)
+        acc[...] = jnp.zeros_like(acc)
+
+    some = jnp.concatenate(
+        [
+            dbias[pl.ds(c * HEADS * lines + step * group + g, HEADS, stride=lines), :]
+            for g in range(group)
+            for c in range(width // CZ)
+        ],
+        1,
+    )
+    some = jnp.concatenate([some, jnp.zeros((16 - HEADS, some.shape[1]), f32)], 0)
+    acc[...] += dot_nt(lanes(zbt_ref), some.astype(bf16))
+
+    @pl.when(step == pl.num_programs(0) - 1)
+    def _():
+        for block in range(3):
+            stack[block * CZ : (block + 1) * CZ, :] = dqkv_ref[block]
+        stack[3 * CZ :, :] = acc[...].T
+        half = keep_ref.shape[0]
+        first = (info_ref[0] & 1) == 0
+        one, two = stack[:half, :], stack[half:, :]
+        keep_ref[...] = jnp.where(first, one, two)
+        give_ref[...] = jnp.where(first, two, one)
 
 
 def whole(shape):
@@ -652,61 +790,76 @@
     return next(g for g in range(most, 0, -1) if count % g == 0)
 
 
-def front(pair, gains, small, wide, down, stats):
+def pack_weights(peers, wide, down, *stats):
+    args = (wide, down, *stats)
+    shape = (peers, 8, STATS + wide.shape[1] + (FF // CZ) * down.shape[1])
+    return call(
+        pack_kernel,
+        "pack",
+        1,
+        1,
+        [whole(x.shape) for x in args],
+        [(whole(shape), shape, bf16)],
+        [pltpu.VMEM(shape[1:], f32)],
+        args,
+    )[0]
+
+
+def front(pair, gains, small):
     count, width = pair.shape[0], pair.shape[1]
-    columns = wide.shape[1] + (FF // CZ) * down.shape[1] + CZ
-    g = group_of(count, 4)
+    g = group_of(count, FRONT_ROWS)
     return call(
         front_kernel,
         "front",
         6,
         count // g,
-        [rows_of(g, width, CZ)] + [whole(x.shape) for x in (gains, small, wide, down, stats)],
+        [rows_of(g, width, CZ), whole(gains.shape), whole(small.shape)],
         [
             (rows_of(g, CZ, width), (count, CZ, width), bf16),
             (rows_of(g, CZ, width), (count, CZ, width), bf16),
             (whole((HEADS, count, width)), (HEADS, count, width), bf16),
-            (whole((8, columns)), (8, columns), bf16),
         ],
         [
             pltpu.VMEM((CZ, CZ), f32),
             pltpu.VMEM((16, CZ), bf16),
             pltpu.VMEM((HEADS, count, width), f32),
-            pltpu.VMEM((8, columns), f32),
-        ],
-        (pair, gains, small, wide, down, stats),
-    )
-
-
-def project(crops, rows, masks, info, packs, zbt):
+        ],
+        (pair, gains, small),
+    )
+
+
+def project(crops, rows, info, mine, other, zbt):
     count, _, width = zbt.shape
-    g = group_of(count, 4)
+    g = group_of(count, 6)
     return call(
-        partial(project_kernel, crops, rows, masks),
+        partial(project_kernel, crops, rows),
         "project",
-        8,
+        40,
         count // g,
-        [SMEM, whole(packs.shape), rows_of(g, CZ, width)],
+        [SMEM, whole(mine.shape), whole(other.shape), rows_of(g, CZ, width)],
         [
             (rows_of(g, 3 * CZ, width), (count, 3 * CZ, width), bf16),
-            (rows_of(g, CZ, width), (count, CZ, width), f32),
-            (rows_of(g, width, 2 * CZ), (count, width, 2 * CZ), bf16),
+            (rows_of(g, width, CZ), (count, width, CZ), bf16),
             (pl.BlockSpec((8, g * width), lambda i: (0, i)), (8, count * width), f32),
             (whole((CZ, WIDE)), (CZ, WIDE), bf16),
             (whole((FF, CZ)), (FF, CZ), bf16),
-        ],
-        [pltpu.VMEM((CZ, WIDE), f32), pltpu.VMEM((FF, CZ), f32), pltpu.VMEM((4 * CZ, CZ), bf16)],
-        (info, packs, zbt),
-    )
-
-
+            (whole((1, 1)), (1, 1), f32),
+        ],
+        [pltpu.VMEM((CZ, WIDE), f32), pltpu.VMEM((FF, CZ), f32), pltpu.VMEM((3 * CZ, CZ), bf16)],
+        (info, mine, other, zbt),
+    )
+
+
+FRONT_ROWS = 12
 ATTEND_ROWS = 4
-MIDDLE_ROWS = 4
-SCORE_ROWS = 3
+MIDDLE_ROWS = 8
+MIDDLE_PART = 2
+MIDDLE_LAG = 1
+SCORE_ROWS = 6
 BACK_ROWS = 3
 
 
-def attend(masks, info, norms, bias, kvn, qkv):
+def attend(masks, info, norms, bias, other_bias, qkv):
     count, _, width = qkv.shape
     g = group_of(count, ATTEND_ROWS)
     return call(
@@ -718,8 +871,9 @@
             SMEM,
             pl.BlockSpec((8, g * width), lambda i: (0, i)),
             whole(bias.shape),
+            whole(bias.shape),
             rows_of(g, CZ, width),
-            rows_of(g, width, CZ),
+            rows_of(g, CZ, width, 1),
             rows_of(g, CZ, width, 2),
         ],
         [
@@ -734,11 +888,11 @@
             pltpu.VMEM((g, width, 2 * CZ), bf16),
             pltpu.SMEM((1,), f32),
         ],
-        (info, norms, bias, qkv, kvn, qkv),
-    )
-
-
-def middle(info, wide, down, small, gains, zt, zbt, o, gate, r, tgt, nbr):
+        (info, norms, bias, other_bias, qkv, qkv, qkv),
+    )
+
+
+def middle(info, wide, down, small, gains, zt, zbt, o, r, tgt, nbr):
     count, _, width = zt.shape
     g = group_of(count, MIDDLE_ROWS)
     return call(
@@ -755,7 +909,6 @@
             rows_of(g, CZ, width),
             rows_of(g, CZ, width),
             rows_of(g, CZ, width),
-            rows_of(g, CZ, width),
             rows_of(g, 8, width),
             whole(tgt.shape),
             whole(nbr.shape),
@@ -768,9 +921,10 @@
         ],
         [
             pltpu.VMEM((BLOCKS, CZ, CZ), f32),
-            pltpu.VMEM((2, g * width), f32),
+            pltpu.VMEM((2, 128 * MIDDLE_PART), f32),
             pltpu.VMEM((CZ, CZ), f32),
             pltpu.VMEM((CZ, CZ), f32),
+            pltpu.VMEM((CZ, CZ), bf16),
             pltpu.VMEM((CZ, CZ), bf16),
             pltpu.VMEM((FF, CZ), bf16),
             pltpu.VMEM((CZ, FF), bf16),
@@ -779,36 +933,58 @@
             pltpu.VMEM((FF, 2 * CZ), bf16),
             pltpu.VMEM((CZ, 2 * BINS), bf16),
         ],
-        (info, wide, down, small, gains, zt, zbt, o, gate, r, tgt, nbr),
-    )
-
-
-def score(p, kvn, do, nd):
+        (info, wide, down, small, gains, zt, zbt, o, r, tgt, nbr),
+    )
+
+
+def score(info, p, vn, do, nd):
     count, _, width = do.shape
     g = group_of(count, SCORE_ROWS)
-    shape = (width // count, HEADS, count, width)
+    shape = (width // count // 2, HEADS * count * (width // CZ), CZ)
     return call(
         score_kernel,
         "score",
         17,
         count // g,
         [
+            SMEM,
             rows_of(g, width, HEADS * width),
-            rows_of(g, width, CZ, 0, 1),
+            rows_of(g, width, CZ),
             rows_of(g, CZ, width),
             rows_of(g, 16 * HEADS, width),
         ],
-        [(whole(shape), shape, bf16)],
+        [(whole(shape), shape, bf16)] * 2,
         [
             pltpu.VMEM((width, HEADS * width), f32),
             pltpu.VMEM((g, 2 * CZ, HEADS * width), bf16),
             pltpu.VMEM((g, width, 2 * CZ), bf16),
-        ],
-        (p, kvn, do, nd),
-    )[0]
-
-
-def back(p, qkv, kvn, do, nd, zbt):
+            pltpu.VMEM((HEADS, width, width), f32),
+        ],
+        (info, p, vn, do, nd),
+    )
+
+
+def late_sums(info, spread_out, d_qkv, zbt):
+    count, _, width = zbt.shape
+    g = group_of(count, 8)
+    half = (3 * CZ + 16) // 2
+    return call(
+        late_kernel,
+        "late",
+        3,
+        count // g,
+        [SMEM, whole(spread_out.shape), whole(d_qkv.shape), rows_of(g, CZ, width)],
+        [(whole((half, CZ)), (half, CZ), f32)] * 2,
+        [
+            pltpu.VMEM((HEADS * count * (width // CZ), CZ), f32),
+            pltpu.VMEM((CZ, 16), f32),
+            pltpu.VMEM((2 * half, CZ), f32),
+        ],
+        (info, spread_out, d_qkv, zbt),
+    )
+
+
+def back(p, qkv, vn, do, nd, zbt):
     count, _, width = zbt.shape
     g = group_of(count, BACK_ROWS)
     return call(
@@ -820,7 +996,7 @@
             rows_of(g, width, HEADS * width),
             rows_of(g, CZ, width),
             rows_of(g, CZ, width, 1),
-            rows_of(g, width, CZ, 0, 1),
+            rows_of(g, width, CZ),
             rows_of(g, CZ, width),
             rows_of(g, 16 * HEADS, width),
             rows_of(g, CZ, width),
@@ -832,18 +1008,18 @@
             pltpu.VMEM((g, width, 2 * CZ), bf16),
             pltpu.VMEM((3 * CZ, g * width), bf16),
         ],
-        (p, qkv, qkv, kvn, do, nd, zbt),
+        (p, qkv, qkv, vn, do, nd, zbt),
     )[0]
 
 
-def finish(*args):
-    wide, down, gains, small = args[8], args[9], args[10], args[12]
+def finish(crops, rows, *args):
+    wide, down, gains, small = args[7], args[8], args[9], args[11]
     shapes = []
     for weight in (wide, down):
-        shapes += [weight.shape, (1, weight.shape[0]), (1, weight.shape[1]), weight.shape]
+        shapes += [weight.shape, weight.shape[:1], weight.shape[1:], weight.shape]
     shapes += [gains.shape] * 3 + [small.shape] * 3
     return call(
-        finish_kernel,
+        partial(finish_kernel, crops, rows),
         "finish",
         4,
         1,
@@ -851,10 +1027,14 @@
         [(whole(shape), shape, f32) for shape in shapes],
         [
             pltpu.VMEM((BLOCKS * CZ, CZ), f32),
+            pltpu.VMEM((3 * CZ + 16, CZ), f32),
             pltpu.VMEM((CZ, WIDE), f32),
             pltpu.VMEM((FF, CZ), f32),
             pltpu.VMEM((CZ, 1), f32),
             pltpu.VMEM((FF, 1), f32),
+            pltpu.VMEM((rows, CZ), f32),
+            pltpu.VMEM((1, WIDE), f32),
+            pltpu.VMEM((1, CZ), f32),
         ],
         args,
     )
@@ -883,27 +1063,14 @@
     return place
 
 
-def exact_halves(v):
-    high = lax.reduce_precision(v, 8, 7)
-    return high.astype(bf16), (v - high).astype(bf16)
-
-
 def build(crops, rows):
     both = ("crop", "row")
     devices = crops * rows
     row_masks = bits(rows)
     all_masks = row_masks[:-1] + [m * rows for m in bits(crops)] + row_masks[-1:]
 
-    def total(x, core):
-        half = x.shape[0] // 2
-        keep = lax.dynamic_slice_in_dim(x, core * half, half)
-        give = lax.dynamic_slice_in_dim(x, (1 - core) * half, half)
-        keep = keep + swap(give, both, devices, 1)
-        for mask in all_masks[:-1]:
-            keep = keep + swap(keep, both, devices, mask)
-        other = swap(keep, both, devices, 1)
-        first = core == 0
-        return jnp.concatenate([jnp.where(first, keep, other), jnp.where(first, other, keep)], 0)
+    sides = [[2 * chip + side for chip in range(devices // 2)] for side in range(2)]
+    row_sides = [[2 * chip + side for chip in range(rows // 2)] for side in range(2)]
 
     def body(
         pair,
@@ -926,31 +1093,26 @@
         count_rows, width = pair.shape[1], pair.shape[2]
         info = jnp.stack([row_index, crop_index, crop_len[0], jnp.int32(count_rows)])
 
-        lines, cols = wide.shape
-        cols_stat = jnp.concatenate([wide_cols, down_cols])
-        cols_stat = jnp.pad(cols_stat, (0, -cols_stat.size % rows))
-        share = cols_stat.size // rows
-        stats = jnp.concatenate(
-            [
-                wide_rows,
-                down_rows,
-                lax.dynamic_slice_in_dim(cols_stat, row_index * share, share),
-            ]
+        pack = pack_weights(
+            devices // 2, wide, down, wide_rows, down_rows, wide_cols, down_cols
         )
         small_t = small.T
-        zt, zbt, bias_part, pack = front(pair[0], gains, small_t, wide, down, stats[None, :])
-        packs = gathered(pack, both, devices, all_masks)
+        packs = lax.all_to_all(pack, both, 0, 0, axis_index_groups=sides, tiled=True)
+        zt, zbt, bias_part = front(pair[0], gains, small_t)
         bias = gathered(bias_part, "row", rows, row_masks[:-1])
-        qkv, gate, kvn, norms, wide_full, down_full = project(
-            crops, rows, all_masks, info, packs, zbt
+        other_packs = swap(packs, both, devices, 1)
+        qkv, vn, norms, wide_full, down_full, done = project(
+            crops, rows, info, packs, other_packs, zbt
         )
-        bias, norms = lax.optimization_barrier((bias, norms))
-        bias = jnp.concatenate([bias, swap(bias, "row", rows, row_masks[-1])], 0)
+        bias = bias + done.astype(bf16)[..., None, None]
+        other_bias = swap(bias, "row", rows, row_masks[-1])
         if count_rows % 8:
+            bias = jnp.concatenate([bias, other_bias], 0)
             bias = jnp.take(bias, places(row_index, rows, row_masks), axis=0)
             bias = bias.transpose(1, 0, 2, 3).reshape(1, HEADS, width, width)
+            other_bias = bias
         bias_masks = [] if count_rows % 8 else row_masks
-        p, o, r = attend(bias_masks, info, norms, bias, kvn, qkv)
+        p, o, r = attend(bias_masks, info, norms, bias, other_bias, qkv)
         do, nd, early, scalars = middle(
             info,
             wide_full,
@@ -960,47 +1122,33 @@
             zt,
             zbt,
             o,
-            gate,
             r,
             targets,
             neighbours,
         )
 
         early = lax.all_to_all(early.reshape(devices, -1, CZ), both, 0, 0, tiled=True)
-        d_bias = score(p, kvn, do, nd)
-        early, d_bias = lax.optimization_barrier((early, d_bias))
-        early = jnp.sum(early.astype(f32), 0).astype(bf16)
-        early = jnp.concatenate([early, scalars], 0)
-        early = jnp.broadcast_to(early[None], (devices, *early.shape))
-        early, d_bias, do = lax.optimization_barrier((early, d_bias, do))
-        early = lax.all_to_all(early, both, 0, 0, tiled=True)
-        scalars = jnp.sum(early[:, -16, :6].astype(f32), 0).reshape(3, 2)
+        keep, give = score(info, p, vn, do, nd)
+        early, keep, give = lax.optimization_barrier((early, keep, give))
+        got = swap(give, both, devices, 1)
+        early = jnp.concatenate([jnp.sum(early.astype(f32), 0).astype(bf16), scalars], 0)
+        early_lines = early.shape[0]
+        early = gathered(early, both, devices, [1] + [m * rows for m in bits(crops)])
+        early = early.reshape(-1, CZ)
+        early = jnp.broadcast_to(early[None], (rows // 2, *early.shape))
+        parcel = jnp.concatenate([(keep.astype(f32) + got.astype(f32)).astype(bf16), early], 1)
+        parcel, do = lax.optimization_barrier((parcel, do))
+        parcel = lax.all_to_all(parcel, "row", 0, 0, axis_index_groups=row_sides, tiled=True)
+        d_qkv = back(p, qkv, vn, do, nd, zbt)
+
+        keep, give = late_sums(info, parcel, d_qkv, zbt)
+        keep = keep + swap(give, both, devices, 1)
+        for mask in all_masks[:-1]:
+            keep = keep + swap(keep, both, devices, mask)
+        other = swap(keep, both, devices, 1)
+        scalars = parcel[:, -2 * crops * early_lines :].reshape(rows // 2, 2 * crops, -1, CZ)
+        scalars = jnp.sum(scalars[:, :, -16, :6].astype(f32), (0, 1)).reshape(3, 2)
         loss_sum, pair_count = jnp.sum(scalars[:, 0]), jnp.sum(scalars[:, 1])
-
-        d_bias = lax.all_to_all(d_bias, "row", 0, 0, tiled=True)
-        d_qkv = back(p, qkv, kvn, do, nd, zbt)
-        d_bias = jnp.sum(d_bias.astype(f32), 0).astype(bf16)
-        d_pbias = lax.dot_general(
-            d_bias, zbt, (((1, 2), (0, 2)), ((), ())), preferred_element_type=f32
-        )
-        late = total(
-            jnp.concatenate(
-                [d_qkv.reshape(3 * CZ, CZ), jnp.pad(d_pbias, ((0, 16 - HEADS), (0, 0)))], 0
-            ),
-            row_index & 1,
-        )
-
-        after = cols + (FF // CZ) * down.shape[1]
-        extras = jnp.sum(packs[:, :2, after : after + stats.size].astype(f32), 1)
-        extras = jnp.take(
-            extras, places(crop_index * rows + row_index, devices, all_masks), axis=0
-        )
-        wide_rows_all = extras[:rows, :lines].reshape(-1)
-        down_rows_all = extras[:rows, lines : lines + down_rows.size].reshape(-1)
-        cols_all = extras[:, lines + down_rows.size :].reshape(crops, -1)
-        wide_cols_all = cols_all[:, :cols].reshape(-1)
-        down_cols_all = cols_all[:, cols : cols + down_cols.size].reshape(-1)
-
         (
             wide_g,
             wide_r_new,
@@ -1017,14 +1165,15 @@
             small_s,
             small_n,
         ) = finish(
+            crops,
+            rows,
             info,
-            late,
-            early,
+            keep,
+            other,
+            parcel,
+            packs,
+            other_packs,
             wide_full,
-            wide_rows_all[:, None],
-            wide_cols_all[None, :],
-            down_rows_all[:, None],
-            down_cols_all[None, :],
             wide,
             down,
             gains,
@@ -1036,12 +1185,12 @@
             loss_sum,
             pair_count,
             wide_g,
-            wide_r_new.reshape(-1),
-            wide_c_new.reshape(-1),
+            wide_r_new,
+            wide_c_new,
             wide_new,
             down_g,
-            down_r_new.reshape(-1),
-            down_c_new.reshape(-1),
+            down_r_new,
+            down_c_new,
             down_new,
             gain_grad,
             gain_s,

time: 226 us -> 209 us (0.925)
  other arithmetic: 13.5 us -> 6.65 us
  starting transfers between devices: 36.3 us -> 32.1 us
  local copies, waits for them, and re-layouts: 6.55 us -> 3.37 us
  Pallas kernels: 135 us -> 132 us
    ppermute x15 -> x14, starting transfers between devices: 19.2 us -> 14 us  [swap(): return lax.ppermute(x, axes, [(i, i ^ mask) for i in range(size)])]
    pallas_call x7 -> x9, Pallas kernels: 135 us -> 132 us  [call(): pl.pallas_call(kernel, grid=(grid,), in_specs=in_specs, out_specs=[o[0] f...]
    another operation x4 -> x0, local copies, waits for them, and re-layouts: 2.97 us -> none  [the longest x1 0.98 us: body(): down_rows_all[:, None]]
    reduce_sum x4 -> x2, other arithmetic: 2.79 us -> 0.12 us  [the longest x1 0.07 us: body(): jnp.sum(early.astype(f32), 0).astype(bf16)]
    all_to_all x2, waiting for transfers between devices: 0.01 us -> 2.58 us  [the longest x1 2.57 us: body(): lax.all_to_all(pack, both, 0, 0, axis_index_groups=sides, tiled=True)]
    ppermute x15 -> x14, waiting for transfers between devices: 29.4 us -> 28.7 us  [swap(): return lax.ppermute(x, axes, [(i, i ^ mask) for i in range(size)])]
  transfers between devices with their start and end apart: 18 -> 17, of which waited for: 11 -> 12; matrix products, arithmetic and copies ran while one was open for 6% -> 2% of each run, Pallas kernels for 28% -> 31%
where the time goes in v3:
time: 209 us; the launch traced here: 208 us
  Pallas kernels  132 us (63%)
  starting transfers between devices  32.1 us (15%)
  waiting for transfers between devices  31.3 us (15%)
  other arithmetic  6.65 us (3%)
  local copies, waits for them, and re-layouts  3.37 us (2%)
  between operations  2.3 us (1%)
    pallas_call x9, Pallas kernels, call(): pl.pallas_call(kernel, grid=(grid,), in_specs=in_specs, out_specs=[o[0] f...  132 us
    ppermute x14, waiting for transfers between devices, swap(): return lax.ppermute(x, axes, [(i, i ^ mask) for i in range(size)])  28.7 us
    ppermute x14, starting transfers between devices, swap(): return lax.ppermute(x, axes, [(i, i ^ mask) for i in range(size)])  14 us
    all_to_all x1, starting transfers between devices, body(): lax.all_to_all(pack, both, 0, 0, axis_index_groups=sides, tiled=True)  8.31 us
    all_to_all x1, starting transfers between devices, body(): lax.all_to_all(parcel, 'row', 0, 0, axis_index_groups=row_sides, tiled=True)  5.61 us
  transfers between devices with their start and end apart: 17, of which 12 were waited for; matrix products, arithmetic and copies ran while one was open for 2% of the time, Pallas kernels for 31%

profile of v3, /device:TPU:0, one launch (start us, length us, event | category | flops | bytes accessed | tf_op | source)
XLA Modules:
  0.0 207.9 jit_solution(17615541255782414502)
XLA Ops:
  0.6 1.6 pack.1
  2.2 8.3 %all-to-all-start = ((bf16[16,8,1088]{2,1,0:T(8,128)(2,1)}), bf16[16,8,1088]{2,1,0:T(8,128)(2,1)S(1)}, u32[]{:S(2)}, u32[]{:S(2)}) async-start(bf16[16,8,1088]{2,1,0:T(8,128)(2,1)} %pack.1), calls=%async_computation | async-start | bytes 589824 | tf_op jit(solution)/shard_map/all_to_all | solution.py:1100
  10.5 5.2 %front.1 = (bf16[24,128,384]{2,1,0:T(8,128)(2,1)}, bf16[24,128,384]{2,1,0:T(8,128)(2,1)}, bf16[4,24,384]{2,1,0:T(8,128)(2,1)}) custom-call(bf16[24,384,128]{2,1,0:T(8,128)(2,1)} %bitcast.22, f32[3,128]{1,0:T(4,128)} %gains_ref.5, f32[68,128]{1,0:T(8,128)} %bitcast.23), custom_call_target="tpu_custom_call" | custom-call | flops 4800000000 | bytes 1048576 | tf_op jit(solution)/shard_map/front/pallas_call | solution.py:774
  15.8 2.9 %collective-permute-start.1 = (bf16[1,4,24,384]{3,2,1,0:T(8,128)(2,1)}, bf16[1,4,24,384]{3,2,1,0:T(8,128)(2,1)S(1)}, u32[]{:S(2)}, u32[]{:S(2)}) collective-permute-start(bf16[1,4,24,384]{3,2,1,0:T(8,128)(2,1)} %bitcast.16), channel_id=1, source_target_pairs={{0,8},{1,9},{2,10},{3,11},{4,12},{5,13},{6,14},{7,15},{8,0},{9,1},... | collective-permute-start | bytes 221192 | tf_op jit(solution)/shard_map/ppermute | solution.py:1048
  18.7 2.6 %all-to-all-done.mine_ref.packs_ref = bf16[16,8,1088]{2,1,0:T(8,128)(2,1)S(1)} async-done(((bf16[16,8,1088]{2,1,0:T(8,128)(2,1)}), bf16[16,8,1088]{2,1,0:T(8,128)(2,1)S(1)}, u32[]{:S(2)}, u32[]{:S(2)}) %all-to-all-start) | async-done | bytes 278560 | tf_op jit(solution)/shard_map/all_to_all | solution.py:1100
  21.2 1.9 collective-permute-done.1
  25.6 3.7 %collective-permute-done.2 = bf16[2,4,24,384]{3,2,1,0:T(8,128)(2,1)S(1)} collective-permute-done((bf16[2,4,24,384]{3,2,1,0:T(8,128)(2,1)S(1)}, bf16[2,4,24,384]{3,2,1,0:T(8,128)(2,1)S(1)}, u32[]{:S(2)}, u32[]{:S(2)}) %collective-permute-start.2) | collective-permute-done | bytes 147488 | tf_op jit(solution)/shard_map/ppermute | solution.py:1048
  32.4 7.3 %project.1 = (bf16[24,384,384]{2,1,0:T(8,128)(2,1)}, bf16[24,384,128]{2,1,0:T(8,128)(2,1)}, f32[8,9216]{1,0:T(8,128)}, bf16[128,1152]{1,0:T(8,128)(2,1)}, bf16[512,128]{1,0:T(8,128)(2,1)}, /*index=5*/f32[1,1]{1,0:T(1,128)}) custom-call(s32[4]{0:T(128)} %pad_add_fusion.info_ref, bf16[16,8,1088]{2,1,0:T(8,128)(2,1)} %copy-done.3, ...), custom_call_target="tpu_custom_call" | custom-call | flops 32000000000 | bytes 1048576 | tf_op jit(solution)/shard_map/project/pallas_call | solution.py:774
  40.6 2.0 collective-permute-done.4.other_bias_ref
  43.4 27.9 %attend.1 = (bf16[24,384,1536]{2,1,0:T(8,128)(2,1)}, f32[24,128,384]{2,1,0:T(8,128)}, f32[24,8,384]{2,1,0:T(8,128)}) custom-call(s32[4]{0:T(128)} %pad_add_fusion.info_ref, f32[8,9216]{1,0:T(8,128)} %get-tuple-element.59.norm_ref, bf16[8,4,24,384]{3,2,1,0:T(8,128)(2,1)} %copy-done.2, bf16[8,4,24,384]{3,2,1,0:T(8,128)(2,1)} %copy-done.6, ...), custom_call_target="tpu_custom_call" | custom-call | flops 20000000000 | bytes 1048576 | tf_op jit(solution)/shard_map/attend/pallas_call | solution.py:774
  71.4 30.8 %middle.1 = (bf16[24,128,384]{2,1,0:T(8,128)(2,1)}, bf16[24,64,384]{2,1,0:T(8,128)(2,1)}, bf16[12,128,128]{2,1,0:T(8,128)(2,1)}, bf16[16,128]{1,0:T(8,128)(2,1)}) custom-call(s32[4]{0:T(128)} %pad_add_fusion.info_ref, bf16[128,1152]{1,0:T(8,128)(2,1)} %get-tuple-element.56.wide_ref.full_ref, bf16[512,128]{1,0:T(8,128)(2,1)} %get-tuple-element.57.down_ref, ...), custom_call_target="tpu_custom_call" | custom-call | flops 24000000000 | bytes 1048576 | tf_op jit(solution)/shard_map/middle/pallas_call | solution.py:774
  102.2 4.1 %all-to-all-start.1 = ((bf16[32,48,128]{2,1,0:T(8,128)(2,1)}), bf16[32,48,128]{2,1,0:T(8,128)(2,1)S(1)}, u32[]{:S(2)}, u32[]{:S(2)}) async-start(bf16[32,48,128]{2,1,0:T(8,128)(2,1)} %bitcast.20), calls=%async_computation.1 | async-start | bytes 786432 | tf_op jit(solution)/shard_map/all_to_all | solution.py:1130
  106.3 15.3 %score.1 = (bf16[8,288,128]{2,1,0:T(8,128)(2,1)}, bf16[8,288,128]{2,1,0:T(8,128)(2,1)}) custom-call(s32[4]{0:T(128)} %pad_add_fusion.info_ref, bf16[24,384,1536]{2,1,0:T(8,128)(2,1)} %get-tuple-element.66.p_ref, bf16[24,384,128]{2,1,0:T(8,128)(2,1)} %get-tuple-element.67.vn_ref, bf16[24,128,384]{2,1,0:T(8,128)(2,1)} %get-tuple-element.77.do_ref, ...), custom_call_target="tpu_custom_call" | custom-call | flops 13600000000 | bytes 1048576 | tf_op jit(solution)/shard_map/score/pallas_call | solution.py:774
  125.2 2.4 %collective-permute-done.7 = bf16[2,64,128]{2,1,0:T(8,128)(2,1)S(1)} collective-permute-done((bf16[2,64,128]{2,1,0:T(8,128)(2,1)S(1)}, bf16[2,64,128]{2,1,0:T(8,128)(2,1)S(1)}, u32[]{:S(2)}, u32[]{:S(2)}) %collective-permute-start.7) | collective-permute-done | bytes 32800 | tf_op jit(solution)/shard_map/ppermute | solution.py:1048
  130.0 5.6 %all-to-all-start.2 = ((bf16[8,544,128]{2,1,0:T(8,128)(2,1)}), bf16[8,544,128]{2,1,0:T(8,128)(2,1)S(1)}, u32[]{:S(2)}, u32[]{:S(2)}) async-start(bf16[8,544,128]{2,1,0:T(8,128)(2,1)} %pad_maximum_fusion), calls=%async_computation.2 | async-start | bytes 2228224 | tf_op jit(solution)/shard_map/all_to_all | solution.py:1141
  135.6 36.4 %back.1.dqkv_ref = f32[3,128,128]{2,1,0:T(8,128)} custom-call(bf16[24,384,1536]{2,1,0:T(8,128)(2,1)} %get-tuple-element.66.p_ref, bf16[24,384,384]{2,1,0:T(8,128)(2,1)} %get-tuple-element.62.q_ref.k_ref.v_ref, bf16[24,384,384]{2,1,0:T(8,128)(2,1)} %get-tuple-element.62.q_ref.k_ref.v_ref, bf16[24,384,128]{2,1,0:T(8,128)(2,1)} %get-tuple-element.67.vn_ref, ...), custom_call_target="tpu_custom_call" | custom-call | flops 30400000000 | bytes 1048576 | tf_op jit(solution)/shard_map/back/pallas_call | solution.py:774
  173.0 4.2 %late.1 = (f32[200,128]{1,0:T(8,128)}, f32[200,128]{1,0:T(8,128)}) custom-call(s32[4]{0:T(128)} %pad_add_fusion.info_ref, bf16[8,544,128]{2,1,0:T(8,128)(2,1)} %copy-done, f32[3,128,128]{2,1,0:T(8,128)} %back.1.dqkv_ref, bf16[24,128,384]{2,1,0:T(8,128)(2,1)} %get-tuple-element.55.zbt_ref), custom_call_target="tpu_custom_call" | custom-call | flops 2400000000 | bytes 1048576 | tf_op jit(solution)/shard_map/late/pallas_call | solution.py:774
  179.6 3.0 %collective-permute-start.9 = (f32[200,128]{1,0:T(8,128)S(1)}, f32[200,128]{1,0:T(8,128)S(1)}, u32[]{:S(2)}, u32[]{:S(2)}) collective-permute-start(f32[200,128]{1,0:T(8,128)S(1)} %add.32), channel_id=1, source_target_pairs={{0,8},{1,9},{2,10},{3,11},{4,12},{5,13},{6,14},{7,15},{8,0},{9,1},... | collective-permute-start | bytes 307208 | tf_op jit(solution)/shard_map/ppermute | solution.py:1048
  182.6 5.4 %collective-permute-done.9 = f32[200,128]{1,0:T(8,128)S(1)} collective-permute-done((f32[200,128]{1,0:T(8,128)S(1)}, f32[200,128]{1,0:T(8,128)S(1)}, u32[]{:S(2)}, u32[]{:S(2)}) %collective-permute-start.9) | collective-permute-done | bytes 102432 | tf_op jit(solution)/shard_map/ppermute | solution.py:1048
  188.8 3.9 %collective-permute-done.10 = f32[200,128]{1,0:T(8,128)S(1)} collective-permute-done((f32[200,128]{1,0:T(8,128)S(1)}, f32[200,128]{1,0:T(8,128)S(1)}, u32[]{:S(2)}, u32[]{:S(2)}) %collective-permute-start.10) | collective-permute-done | bytes 102432 | tf_op jit(solution)/shard_map/ppermute | solution.py:1048
  192.7 1.8 collective-permute-start.11
  194.5 2.9 %collective-permute-done.11 = f32[200,128]{1,0:T(8,128)S(1)} collective-permute-done((f32[200,128]{1,0:T(8,128)S(1)}, f32[200,128]{1,0:T(8,128)S(1)}, u32[]{:S(2)}, u32[]{:S(2)}) %collective-permute-start.11) | collective-permute-done | bytes 102432 | tf_op jit(solution)/shard_map/ppermute | solution.py:1048
  199.2 3.0 %collective-permute-done.12 = f32[200,128]{1,0:T(8,128)S(1)} collective-permute-done((f32[200,128]{1,0:T(8,128)S(1)}, f32[200,128]{1,0:T(8,128)S(1)}, u32[]{:S(2)}, u32[]{:S(2)}) %collective-permute-start.12) | collective-permute-done | bytes 102432 | tf_op jit(solution)/shard_map/ppermute | solution.py:1048
  204.3 3.5 %finish.1 = (f32[8,576]{1,0:T(8,128)}, f32[8]{0:T(128)}, f32[576]{0:T(1024)}, f32[8,576]{1,0:T(8,128)}, f32[32,64]{1,0:T(8,128)}, /*index=5*/f32[32]{0:T(128)}, ...) custom-call(s32[4]{0:T(128)} %pad_add_fusion.info_ref, ...), custom_call_target="tpu_custom_call" | custom-call | flops 3200000000 | bytes 1048576 | tf_op jit(solution)/shard_map/finish/pallas_call | solution.py:774
  (58 shorter events, 19.9 us)
Async XLA Ops:
  2.2 19.0 %all-to-all-start = ((bf16[16,8,1088]{2,1,0:T(8,128)(2,1)}), bf16[16,8,1088]{2,1,0:T(8,128)(2,1)S(1)}, u32[]{:S(2)}, u32[]{:S(2)}) async-start(bf16[16,8,1088]{2,1,0:T(8,128)(2,1)} %pack.1), calls=%async_computation | async-start | bytes 589824 | tf_op jit(solution)/shard_map/all_to_all | solution.py:1100
  15.8 7.4 %collective-permute-start.1 = (bf16[1,4,24,384]{3,2,1,0:T(8,128)(2,1)}, bf16[1,4,24,384]{3,2,1,0:T(8,128)(2,1)S(1)}, u32[]{:S(2)}, u32[]{:S(2)}) collective-permute-start(bf16[1,4,24,384]{3,2,1,0:T(8,128)(2,1)} %bitcast.16), channel_id=1, source_target_pairs={{0,8},{1,9},{2,10},{3,11},{4,12},{5,13},{6,14},{7,15},{8,0},{9,1},... | collective-permute-start | bytes 221192 | tf_op jit(solution)/shard_map/ppermute | solution.py:1048
  21.2 10.5 %copy-start.3 = (bf16[16,8,1088]{2,1,0:T(8,128)(2,1)}, bf16[16,8,1088]{2,1,0:T(8,128)(2,1)S(1)}, u32[]{:S(2)}) copy-start(bf16[16,8,1088]{2,1,0:T(8,128)(2,1)S(1)} %all-to-all-done.mine_ref.packs_ref) | copy-start | bytes 835588
  21.2 10.5 %collective-permute-start = (bf16[16,8,1088]{2,1,0:T(8,128)(2,1)S(1)}, bf16[16,8,1088]{2,1,0:T(8,128)(2,1)S(1)}, u32[]{:S(2)}, u32[]{:S(2)}) collective-permute-start(bf16[16,8,1088]{2,1,0:T(8,128)(2,1)S(1)} %all-to-all-done.mine_ref.packs_ref), channel_id=1, source_target_pairs={{0,1},{1,0},{2,3},{3,2},{4,5},{5,4},{6,7},{7,6},{8,9},{9,8},{10,11... | collective-permute-start | bytes 835592 | tf_op jit(solution)/shard_map/ppermute | solution.py:1048
  24.1 5.2 %collective-permute-start.2 = (bf16[2,4,24,384]{3,2,1,0:T(8,128)(2,1)S(1)}, bf16[2,4,24,384]{3,2,1,0:T(8,128)(2,1)S(1)}, u32[]{:S(2)}, u32[]{:S(2)}) collective-permute-start(bf16[2,4,24,384]{3,2,1,0:T(8,128)(2,1)S(1)} %pad_maximum_fusion.2), channel_id=1, source_target_pairs={{0,4},{1,5},{2,6},{3,7},{4,0},{5,1},{6,2},{7,3},{8,12},{9,13},{10,... | collective-permute-start | bytes 442376 | tf_op jit(solution)/shard_map/ppermute | solution.py:1048
  30.2 10.2 %collective-permute-start.3 = (bf16[4,4,24,384]{3,2,1,0:T(8,128)(2,1)S(1)}, bf16[4,4,24,384]{3,2,1,0:T(8,128)(2,1)S(1)}, u32[]{:S(2)}, u32[]{:S(2)}) collective-permute-start(bf16[4,4,24,384]{3,2,1,0:T(8,128)(2,1)S(1)} %pad_maximum_fusion.1), channel_id=1, source_target_pairs={{0,2},{1,3},{2,0},{3,1},{4,6},{5,7},{6,4},{7,5},{8,10},{9,11},{10,... | collective-permute-start | bytes 884744 | tf_op jit(solution)/shard_map/ppermute | solution.py:1048
  32.4 8.0 %copy-start.1 = (bf16[4,24,384]{2,1,0:T(8,128)(2,1)S(1)}, bf16[4,24,384]{2,1,0:T(8,128)(2,1)}, u32[]{:S(2)}) copy-start(bf16[4,24,384]{2,1,0:T(8,128)(2,1)} %get-tuple-element.60) | copy-start | bytes 221188
  40.5 2.1 %copy-start.2 = (bf16[8,4,24,384]{3,2,1,0:T(8,128)(2,1)}, bf16[8,4,24,384]{3,2,1,0:T(8,128)(2,1)S(1)}, u32[]{:S(2)}) copy-start(bf16[8,4,24,384]{3,2,1,0:T(8,128)(2,1)S(1)} %maximum_add_fusion.bias_ref) | copy-start | bytes 1769476
  40.5 2.1 collective-permute-start.4
  102.2 19.5 %all-to-all-start.1 = ((bf16[32,48,128]{2,1,0:T(8,128)(2,1)}), bf16[32,48,128]{2,1,0:T(8,128)(2,1)S(1)}, u32[]{:S(2)}, u32[]{:S(2)}) async-start(bf16[32,48,128]{2,1,0:T(8,128)(2,1)} %bitcast.20), calls=%async_computation.1 | async-start | bytes 786432 | tf_op jit(solution)/shard_map/all_to_all | solution.py:1130
  106.3 15.5 %copy-start.5 = (bf16[16,128]{1,0:T(8,128)(2,1)S(1)}, bf16[16,128]{1,0:T(8,128)(2,1)}, u32[]{:S(2)}) copy-start(bf16[16,128]{1,0:T(8,128)(2,1)} %get-tuple-element.75) | copy-start | bytes 12292
  121.6 6.0 %collective-permute-start.5 = (bf16[8,288,128]{2,1,0:T(8,128)(2,1)}, bf16[8,288,128]{2,1,0:T(8,128)(2,1)S(1)}, u32[]{:S(2)}, u32[]{:S(2)}) collective-permute-start(bf16[8,288,128]{2,1,0:T(8,128)(2,1)} %get-tuple-element.73), channel_id=1, source_target_pairs={{0,1},{1,0},{2,3},{3,2},{4,5},{5,4},{6,7},{7,6},{8,9},{9,8},{10,11... | collective-permute-start | bytes 1769480 | tf_op jit(solution)/shard_map/ppermute | solution.py:1048
  121.8 1.9 collective-permute-start.6
  123.7 3.9 %collective-permute-start.7 = (bf16[2,64,128]{2,1,0:T(8,128)(2,1)S(1)}, bf16[2,64,128]{2,1,0:T(8,128)(2,1)S(1)}, u32[]{:S(2)}, u32[]{:S(2)}) collective-permute-start(bf16[2,64,128]{2,1,0:T(8,128)(2,1)S(1)} %pad_maximum_fusion.4), channel_id=1, source_target_pairs={{0,16},{1,17},{2,18},{3,19},{4,20},{5,21},{6,22},{7,23},{8,24},{9,... | collective-permute-start | bytes 98312 | tf_op jit(solution)/shard_map/ppermute | solution.py:1048
  130.0 42.0 %all-to-all-start.2 = ((bf16[8,544,128]{2,1,0:T(8,128)(2,1)}), bf16[8,544,128]{2,1,0:T(8,128)(2,1)S(1)}, u32[]{:S(2)}, u32[]{:S(2)}) async-start(bf16[8,544,128]{2,1,0:T(8,128)(2,1)} %pad_maximum_fusion), calls=%async_computation.2 | async-start | bytes 2228224 | tf_op jit(solution)/shard_map/all_to_all | solution.py:1141
  172.0 1.0 copy-start
  177.2 21.9 %slice-start = ((bf16[8,544,128]{2,1,0:T(8,128)(2,1)}), bf16[8,256,128]{2,1,0:T(8,128)(2,1)S(1)}, s32[]{:S(2)}) async-start(bf16[8,544,128]{2,1,0:T(8,128)(2,1)} %copy-done), calls=%async_computation.3 | async-start | bytes 1048576 | tf_op jit(solution)/shard_map/slice | solution.py:1149
  177.2 1.5 collective-permute-start.8
  179.6 8.4 %collective-permute-start.9 = (f32[200,128]{1,0:T(8,128)S(1)}, f32[200,128]{1,0:T(8,128)S(1)}, u32[]{:S(2)}, u32[]{:S(2)}) collective-permute-start(f32[200,128]{1,0:T(8,128)S(1)} %add.32), channel_id=1, source_target_pairs={{0,8},{1,9},{2,10},{3,11},{4,12},{5,13},{6,14},{7,15},{8,0},{9,1},... | collective-permute-start | bytes 307208 | tf_op jit(solution)/shard_map/ppermute | solution.py:1048
  188.0 4.7 %collective-permute-start.10 = (f32[200,128]{1,0:T(8,128)S(1)}, f32[200,128]{1,0:T(8,128)S(1)}, u32[]{:S(2)}, u32[]{:S(2)}) collective-permute-start(f32[200,128]{1,0:T(8,128)S(1)} %add.33), channel_id=1, source_target_pairs={{0,4},{1,5},{2,6},{3,7},{4,0},{5,1},{6,2},{7,3},{8,12},{9,13},{10,... | collective-permute-start | bytes 307208 | tf_op jit(solution)/shard_map/ppermute | solution.py:1048
  192.7 4.7 %collective-permute-start.11 = (f32[200,128]{1,0:T(8,128)S(1)}, f32[200,128]{1,0:T(8,128)S(1)}, u32[]{:S(2)}, u32[]{:S(2)}) collective-permute-start(f32[200,128]{1,0:T(8,128)S(1)} %add.34), channel_id=1, source_target_pairs={{0,2},{1,3},{2,0},{3,1},{4,6},{5,7},{6,4},{7,5},{8,10},{9,11},{10,... | collective-permute-start | bytes 307208 | tf_op jit(solution)/shard_map/ppermute | solution.py:1048
  197.5 4.7 %collective-permute-start.12 = (f32[200,128]{1,0:T(8,128)S(1)}, f32[200,128]{1,0:T(8,128)S(1)}, u32[]{:S(2)}, u32[]{:S(2)}) collective-permute-start(f32[200,128]{1,0:T(8,128)S(1)} %add.35), channel_id=1, source_target_pairs={{0,16},{1,17},{2,18},{3,19},{4,20},{5,21},{6,22},{7,23},{8,24},{9,... | collective-permute-start | bytes 307208 | tf_op jit(solution)/shard_map/ppermute | solution.py:1048
  202.2 1.4 copy-start.4
  202.2 1.4 collective-permute-start.13
  (3 other events, 2.2 us)

commit v4 on v3

--- a/solution.py
+++ b/solution.py
@@ -523,13 +523,28 @@
 
 
 def back_kernel(
-    p_ref, q_ref, k_ref, vn_ref, do_ref, nd_ref, zbt_ref, dwq_ref, dobd, dst, vv, dproj
+    info_ref,
+    p_ref,
+    q_ref,
+    k_ref,
+    vn_ref,
+    do_ref,
+    nd_ref,
+    zbt_ref,
+    keep_ref,
+    give_ref,
+    dwq,
+    dobd,
+    dst,
+    vv,
+    dproj,
 ):
     group, _, width = do_ref.shape
-
-    @pl.when(pl.program_id(0) == 0)
-    def _():
-        dwq_ref[...] = jnp.zeros_like(dwq_ref)
+    step = pl.program_id(0)
+
+    @pl.when(step == 0)
+    def _():
+        dwq[...] = jnp.zeros_like(dwq)
         prepare(dobd, vv)
 
     for g in range(group):
@@ -548,7 +563,15 @@
             ).astype(bf16)
     grad = dot_nt(lanes(zbt_ref), dproj[...])
     for block in range(3):
-        dwq_ref[block] += grad[:, block * CZ : (block + 1) * CZ]
+        dwq[block * CZ : (block + 1) * CZ, :] += grad[:, block * CZ : (block + 1) * CZ]
+
+    @pl.when(step == pl.num_programs(0) - 1)
+    def _():
+        half = keep_ref.shape[0]
+        first = (info_ref[0] & 1) == 0
+        one, two = dwq[:half, :], dwq[half:, :]
+        keep_ref[...] = jnp.where(first, one, two)
+        give_ref[...] = jnp.where(first, two, one)
 
 
 def factored(grad_ref, rows, cols, weight_ref, crop, row_start, scratch, outs):
@@ -604,6 +627,7 @@
     keep_ref,
     other_ref,
     spread_ref,
+    across_ref,
     packs_ref,
     other_packs_ref,
     full_ref,
@@ -621,23 +645,26 @@
     )
     row, crop = info_ref[0], info_ref[1]
     side = row & 1
-    half = keep_ref.shape[0]
+    half = 3 * CZ // 2
     mine, other = keep_ref[...], other_ref[...]
-    late_ref[:half, :] = jnp.where(side == 0, mine, other)
-    late_ref[half:, :] = jnp.where(side == 0, other, mine)
+    late_ref[:half, :] = jnp.where(side == 0, mine[:half], other[:half])
+    late_ref[half:, :] = jnp.where(side == 0, other[:half], mine[:half])
+    pbias = mine[half:] + other[half:]
 
     lines = BLOCKS * CZ // (crops * rows)
     height = lines + 16
+    start = spread_ref.shape[1] - 2 * height
     tail = jnp.zeros((1, CZ), f32)
     for c in range(crops):
         for r in range(rows):
             at = (c * rows + r) * lines
-            which = ((r % 2) ^ side) + 2 * (c ^ crop)
-            start = spread_ref.shape[1] - 2 * crops * height
+            which = (r % 2) ^ side
             block = jnp.zeros((height, CZ), f32)
-            for p in range(2 * crops):
-                some = spread_ref[r // 2, start + p * height : start + (p + 1) * height]
-                block = jnp.where(which == p, some.astype(f32), block)
+            for p in range(2):
+                part = slice(start + p * height, start + (p + 1) * height)
+                here = spread_ref[r // 2, part].astype(f32)
+                there = across_ref[r // 2, p * height : (p + 1) * height].astype(f32)
+                block = jnp.where(which == p, jnp.where(c == crop, here, there), block)
             flat[at : at + lines, :] = block[:lines]
             tail += block[lines : lines + 1]
     scale = 1.0 / (tail[:, 1:2] + tail[:, 3:4] + tail[:, 5:6])
@@ -654,8 +681,8 @@
     for block in range(DOWN_BLOCK, HEAD_BLOCK):
         down_s[(block - DOWN_BLOCK) * CZ : (block - DOWN_BLOCK + 1) * CZ, :] = early(block).T
     head = early(HEAD_BLOCK)
-    pbias = late_ref[3 * CZ : 3 * CZ + 16, :] * scale
-    small_grad = jnp.concatenate([pbias[:HEADS], head[:BINS] + head[BINS:]], 0)
+    pbias = pbias[:HEADS] * scale
+    small_grad = jnp.concatenate([pbias, head[:BINS] + head[BINS:]], 0)
     small = small_ref[...]
     plain(small, small_grad, small_second_ref[...], 0.03, outs[11:])
 
@@ -718,7 +745,7 @@
     )
 
 
-def late_kernel(info_ref, spread_ref, dqkv_ref, zbt_ref, keep_ref, give_ref, dbias, acc, stack):
+def late_kernel(spread_ref, keep_ref, got_ref, zbt_ref, out_ref, send_ref, dbias, acc):
     group, _, width = zbt_ref.shape
     tall = dbias.shape[0]
     lines = tall // (HEADS * (width // CZ))
@@ -745,14 +772,10 @@
 
     @pl.when(step == pl.num_programs(0) - 1)
     def _():
-        for block in range(3):
-            stack[block * CZ : (block + 1) * CZ, :] = dqkv_ref[block]
-        stack[3 * CZ :, :] = acc[...].T
         half = keep_ref.shape[0]
-        first = (info_ref[0] & 1) == 0
-        one, two = stack[:half, :], stack[half:, :]
-        keep_ref[...] = jnp.where(first, one, two)
-        give_ref[...] = jnp.where(first, two, one)
+        for at, x in ((0, keep_ref[...] + got_ref[...]), (half, acc[...].T[:8])):
+            out_ref[at : at + x.shape[0], :] = rounded(x)
+        send_ref[...] = out_ref[...].astype(bf16)
 
 
 def whole(shape):
@@ -770,7 +793,7 @@
 SMEM = pl.BlockSpec(memory_space=pltpu.SMEM)
 
 
-def call(kernel, name, micros, grid, in_specs, outs, scratch, args):
+def call(kernel, name, micros, grid, in_specs, outs, scratch, args, mebibytes=52):
     return pl.pallas_call(
         kernel,
         grid=(grid,),
@@ -778,7 +801,7 @@
         out_specs=[o[0] for o in outs],
         out_shape=[of(o[1], o[2]) for o in outs],
         scratch_shapes=scratch,
-        compiler_params=pltpu.CompilerParams(vmem_limit_bytes=56 * 1024 * 1024),
+        compiler_params=pltpu.CompilerParams(vmem_limit_bytes=mebibytes << 20),
         cost_estimate=pl.CostEstimate(
             flops=int(micros * 8e8), bytes_accessed=1 << 20, transcendentals=0
         ),
@@ -802,6 +825,7 @@
         [(whole(shape), shape, bf16)],
         [pltpu.VMEM(shape[1:], f32)],
         args,
+        60,
     )[0]
 
 
@@ -857,6 +881,7 @@
 MIDDLE_LAG = 1
 SCORE_ROWS = 6
 BACK_ROWS = 3
+LATE_ROWS = 12
 
 
 def attend(masks, info, norms, bias, other_bias, qkv):
@@ -964,28 +989,31 @@
     )
 
 
-def late_sums(info, spread_out, d_qkv, zbt):
+def late_sums(parcel, keep, got, zbt):
     count, _, width = zbt.shape
-    g = group_of(count, 8)
-    half = (3 * CZ + 16) // 2
+    shape = (keep.shape[0] + 8, CZ)
+    g = group_of(count, LATE_ROWS)
+    tall = HEADS * count * (width // CZ)
     return call(
         late_kernel,
         "late",
         3,
         count // g,
-        [SMEM, whole(spread_out.shape), whole(d_qkv.shape), rows_of(g, CZ, width)],
-        [(whole((half, CZ)), (half, CZ), f32)] * 2,
-        [
-            pltpu.VMEM((HEADS * count * (width // CZ), CZ), f32),
-            pltpu.VMEM((CZ, 16), f32),
-            pltpu.VMEM((2 * half, CZ), f32),
-        ],
-        (info, spread_out, d_qkv, zbt),
-    )
-
-
-def back(p, qkv, vn, do, nd, zbt):
+        [
+            whole((parcel.shape[0], tall if tall % 16 == 0 else parcel.shape[1], CZ)),
+            whole(keep.shape),
+            whole(keep.shape),
+            rows_of(g, CZ, width),
+        ],
+        [(whole(shape), shape, f32), (whole(shape), shape, bf16)],
+        [pltpu.VMEM((tall, CZ), f32), pltpu.VMEM((CZ, 16), f32)],
+        (parcel, keep, got, zbt),
+    )
+
+
+def back(info, p, qkv, vn, do, nd, zbt):
     count, _, width = zbt.shape
+    half = 3 * CZ // 2
     g = group_of(count, BACK_ROWS)
     return call(
         back_kernel,
@@ -993,6 +1021,7 @@
         38,
         count // g,
         [
+            SMEM,
             rows_of(g, width, HEADS * width),
             rows_of(g, CZ, width),
             rows_of(g, CZ, width, 1),
@@ -1001,19 +1030,20 @@
             rows_of(g, 16 * HEADS, width),
             rows_of(g, CZ, width),
         ],
-        [(whole((3, CZ, CZ)), (3, CZ, CZ), f32)],
-        [
+        [(whole((half, CZ)), (half, CZ), f32)] * 2,
+        [
+            pltpu.VMEM((3 * CZ, CZ), f32),
             pltpu.VMEM((g, 2 * CZ, HEADS * width), bf16),
             pltpu.VMEM((g, width, HEADS * width), bf16),
             pltpu.VMEM((g, width, 2 * CZ), bf16),
             pltpu.VMEM((3 * CZ, g * width), bf16),
         ],
-        (p, qkv, qkv, vn, do, nd, zbt),
-    )[0]
+        (info, p, qkv, qkv, vn, do, nd, zbt),
+    )
 
 
 def finish(crops, rows, *args):
-    wide, down, gains, small = args[7], args[8], args[9], args[11]
+    wide, down, gains, small = args[8], args[9], args[10], args[12]
     shapes = []
     for weight in (wide, down):
         shapes += [weight.shape, weight.shape[:1], weight.shape[1:], weight.shape]
@@ -1027,7 +1057,7 @@
         [(whole(shape), shape, f32) for shape in shapes],
         [
             pltpu.VMEM((BLOCKS * CZ, CZ), f32),
-            pltpu.VMEM((3 * CZ + 16, CZ), f32),
+            pltpu.VMEM((3 * CZ, CZ), f32),
             pltpu.VMEM((CZ, WIDE), f32),
             pltpu.VMEM((FF, CZ), f32),
             pltpu.VMEM((CZ, 1), f32),
@@ -1133,21 +1163,27 @@
         got = swap(give, both, devices, 1)
         early = jnp.concatenate([jnp.sum(early.astype(f32), 0).astype(bf16), scalars], 0)
         early_lines = early.shape[0]
-        early = gathered(early, both, devices, [1] + [m * rows for m in bits(crops)])
+        early = gathered(early, both, devices, [1])
         early = early.reshape(-1, CZ)
         early = jnp.broadcast_to(early[None], (rows // 2, *early.shape))
         parcel = jnp.concatenate([(keep.astype(f32) + got.astype(f32)).astype(bf16), early], 1)
         parcel, do = lax.optimization_barrier((parcel, do))
         parcel = lax.all_to_all(parcel, "row", 0, 0, axis_index_groups=row_sides, tiled=True)
-        d_qkv = back(p, qkv, vn, do, nd, zbt)
-
-        keep, give = late_sums(info, parcel, d_qkv, zbt)
-        keep = keep + swap(give, both, devices, 1)
-        for mask in all_masks[:-1]:
-            keep = keep + swap(keep, both, devices, mask)
+        keep, give = back(info, p, qkv, vn, do, nd, zbt)
+        got = swap(give, both, devices, 1)
+        across = swap(parcel[:, -2 * early_lines :], both, devices, rows)
+        keep, send = late_sums(parcel, keep, got, zbt)
+        for n, mask in enumerate(all_masks[:-1]):
+            if n == 0:
+                keep = keep + swap(send, both, devices, mask).astype(f32)
+            else:
+                if n == len(all_masks) - 2:
+                    keep = keep + across[0, -16:-15].astype(f32) * 0.0
+                keep = keep + swap(keep, both, devices, mask)
         other = swap(keep, both, devices, 1)
-        scalars = parcel[:, -2 * crops * early_lines :].reshape(rows // 2, 2 * crops, -1, CZ)
-        scalars = jnp.sum(scalars[:, :, -16, :6].astype(f32), (0, 1)).reshape(3, 2)
+        scalars = jnp.stack([parcel[:, -2 * early_lines :], across])
+        scalars = scalars.reshape(crops, rows, -1, CZ)[:, :, -16, :6]
+        scalars = jnp.sum(scalars.astype(f32), (0, 1)).reshape(3, 2)
         loss_sum, pair_count = jnp.sum(scalars[:, 0]), jnp.sum(scalars[:, 1])
         (
             wide_g,
@@ -1171,6 +1207,7 @@
             keep,
             other,
             parcel,
+            across,
             packs,
             other_packs,
             wide_full,

time: 209 us -> 192 us (0.919)
  waiting for transfers between devices: 31.3 us -> 23.3 us
  Pallas kernels: 132 us -> 128 us
  other arithmetic: 6.65 us -> 3.39 us
  local copies, waits for them, and re-layouts: 3.37 us -> 0.18 us
  starting transfers between devices: 32.1 us -> 34.3 us
    ppermute x14, waiting for transfers between devices: 28.7 us -> 19.8 us  [swap(): return lax.ppermute(x, axes, [(i, i ^ mask) for i in range(size)])]
    pallas_call x9, Pallas kernels: 132 us -> 128 us  [call(): pl.pallas_call(kernel, grid=(grid,), in_specs=in_specs, out_specs=[o[0] f...]
    unnamed x18 -> x20, local copies, waits for them, and re-layouts: 3.21 us -> 0.04 us
    ppermute x14, starting transfers between devices: 14 us -> 16.6 us  [swap(): return lax.ppermute(x, axes, [(i, i ^ mask) for i in range(size)])]
  transfers between devices with their start and end apart: 17 -> 17, of which waited for: 12 -> 12; matrix products, arithmetic and copies ran while one was open for 2% -> 1% of each run, Pallas kernels for 31% -> 33%
where the time goes in v4:
time: 192 us; the launch traced here: 191 us
  Pallas kernels  128 us (67%)
  starting transfers between devices  34.3 us (18%)
  waiting for transfers between devices  23.3 us (12%)
  other arithmetic  3.39 us (2%)
  between operations  2.35 us (1%)
    pallas_call x9, Pallas kernels, call(): pl.pallas_call(kernel, grid=(grid,), in_specs=in_specs, out_specs=[o[0] f...  128 us
    ppermute x14, waiting for transfers between devices, swap(): return lax.ppermute(x, axes, [(i, i ^ mask) for i in range(size)])  19.8 us
    ppermute x14, starting transfers between devices, swap(): return lax.ppermute(x, axes, [(i, i ^ mask) for i in range(size)])  16.6 us
    all_to_all x1, starting transfers between devices, body(): lax.all_to_all(pack, both, 0, 0, axis_index_groups=sides, tiled=True)  8.31 us
    all_to_all x1, starting transfers between devices, body(): lax.all_to_all(parcel, 'row', 0, 0, axis_index_groups=row_sides, tiled=True)  5.62 us
    all_to_all x1, starting transfers between devices, body(): lax.all_to_all(early.reshape(devices, -1, CZ), both, 0, 0, tiled=True)  3.85 us
  transfers between devices with their start and end apart: 17, of which 12 were waited for; matrix products, arithmetic and copies ran while one was open for 1% of the time, Pallas kernels for 33%

profile of v4, /device:TPU:0, one launch (start us, length us, event | category | flops | bytes accessed | tf_op | source)
XLA Modules:
  0.0 191.3 jit_solution(5548711576246740618)
XLA Ops:
  0.7 1.6 pack.1
  2.2 8.3 %all-to-all-start = ((bf16[16,8,1088]{2,1,0:T(8,128)(2,1)}), bf16[16,8,1088]{2,1,0:T(8,128)(2,1)S(1)}, u32[]{:S(2)}, u32[]{:S(2)}) async-start(bf16[16,8,1088]{2,1,0:T(8,128)(2,1)} %pack.1), calls=%async_computation | async-start | bytes 589824 | tf_op jit(solution)/shard_map/all_to_all | solution.py:1130
  10.6 5.2 %front.1 = (bf16[24,128,384]{2,1,0:T(8,128)(2,1)}, bf16[24,128,384]{2,1,0:T(8,128)(2,1)}, bf16[4,24,384]{2,1,0:T(8,128)(2,1)S(1)}) custom-call(bf16[24,384,128]{2,1,0:T(8,128)(2,1)} %bitcast.29, f32[3,128]{1,0:T(4,128)S(1)} %copy-done.7, f32[68,128]{1,0:T(8,128)S(1)} %bitcast.23), custom_call_target="tpu_custom_call" | custom-call | flops 4800000000 | bytes 1048576 | tf_op jit(solution)/shard_map/front/pallas_call | solution.py:797
  15.8 2.8 %collective-permute-start.1 = (bf16[1,4,24,384]{3,2,1,0:T(8,128)(2,1)S(1)}, bf16[1,4,24,384]{3,2,1,0:T(8,128)(2,1)S(1)}, u32[]{:S(2)}, u32[]{:S(2)}) collective-permute-start(bf16[1,4,24,384]{3,2,1,0:T(8,128)(2,1)S(1)} %bitcast.18), channel_id=1, source_target_pairs={{0,8},{1,9},{2,10},{3,11},{4,12},{5,13},{6,14},{7,15},{8,0},{9,1},... | collective-permute-start | bytes 221192 | tf_op jit(solution)/shard_map/ppermute | solution.py:1078
  18.6 3.5 %all-to-all-done.mine_ref.packs_ref = bf16[16,8,1088]{2,1,0:T(8,128)(2,1)S(1)} async-done(((bf16[16,8,1088]{2,1,0:T(8,128)(2,1)}), bf16[16,8,1088]{2,1,0:T(8,128)(2,1)S(1)}, u32[]{:S(2)}, u32[]{:S(2)}) %all-to-all-start) | async-done | bytes 278560 | tf_op jit(solution)/shard_map/all_to_all | solution.py:1130
  24.0 4.4 %collective-permute-done.2 = bf16[2,4,24,384]{3,2,1,0:T(8,128)(2,1)S(1)} collective-permute-done((bf16[2,4,24,384]{3,2,1,0:T(8,128)(2,1)S(1)}, bf16[2,4,24,384]{3,2,1,0:T(8,128)(2,1)S(1)}, u32[]{:S(2)}, u32[]{:S(2)}) %collective-permute-start.2) | collective-permute-done | bytes 147488 | tf_op jit(solution)/shard_map/ppermute | solution.py:1078
  30.0 7.1 %project.1 = (bf16[24,384,384]{2,1,0:T(8,128)(2,1)}, bf16[24,384,128]{2,1,0:T(8,128)(2,1)}, f32[8,9216]{1,0:T(8,128)S(1)}, bf16[128,1152]{1,0:T(8,128)(2,1)S(1)}...) custom-call(s32[4]{0:T(128)S(1)} %pad_add_fusion.info_ref, bf16[16,8,1088]{2,1,0:T(8,128)(2,1)S(1)} %all-to-all-done.mine_ref.packs_ref, ...), custom_call_target="tpu_custom_call" | custom-call | flops 32000000000 | bytes 1048576 | tf_op jit(solution)/shard_map/project/pallas_call | solution.py:797
  37.9 2.0 %collective-permute-done.4.other_bias_ref = bf16[8,4,24,384]{3,2,1,0:T(8,128)(2,1)S(1)} collective-permute-done((bf16[8,4,24,384]{3,2,1,0:T(8,128)(2,1)S(1)}, bf16[8,4,24,384]{3,2,1,0:T(8,128)(2,1)S(1)}, u32[]{:S(2)}, u32[]{:S(2)}) %collective-permute-start.4) | collective-permute-done | bytes 589856 | tf_op jit(solution)/shard_map/ppermute | solution.py:1078
  39.9 27.5 %attend.1 = (bf16[24,384,1536]{2,1,0:T(8,128)(2,1)}, f32[24,128,384]{2,1,0:T(8,128)}, f32[24,8,384]{2,1,0:T(8,128)S(1)}) custom-call(s32[4]{0:T(128)S(1)} %pad_add_fusion.info_ref, f32[8,9216]{1,0:T(8,128)S(1)} %get-tuple-element.61.norm_ref, bf16[8,4,24,384]{3,2,1,0:T(8,128)(2,1)S(1)} %maximum_add_fusion.bias_ref, ...), custom_call_target="tpu_custom_call" | custom-call | flops 20000000000 | bytes 1048576 | tf_op jit(solution)/shard_map/attend/pallas_call | solution.py:797
  67.4 30.7 %middle.1 = (bf16[24,128,384]{2,1,0:T(8,128)(2,1)}, bf16[24,64,384]{2,1,0:T(8,128)(2,1)}, bf16[12,128,128]{2,1,0:T(8,128)(2,1)}, bf16[16,128]{1,0:T(8,128)(2,1)S(1)}) custom-call(s32[4]{0:T(128)S(1)} %pad_add_fusion.info_ref, bf16[128,1152]{1,0:T(8,128)(2,1)S(1)} %get-tuple-element.58.wide_ref.full_ref, bf16[512,128]{1,0:T(8,128)(2,1)S(1)} %get-tuple-element.59.down_ref, ...), custom_call_target="tpu_custom_call" | custom-call | flops 24000000000 | bytes 1048576 | tf_op jit(solution)/shard_map/middle/pallas_call | solution.py:797
  98.1 3.9 %all-to-all-start.1 = ((bf16[32,48,128]{2,1,0:T(8,128)(2,1)}), bf16[32,48,128]{2,1,0:T(8,128)(2,1)S(1)}, u32[]{:S(2)}, u32[]{:S(2)}) async-start(bf16[32,48,128]{2,1,0:T(8,128)(2,1)} %bitcast.6), calls=%async_computation.1 | async-start | bytes 786432 | tf_op jit(solution)/shard_map/all_to_all | solution.py:1160
  102.0 14.3 %score.1 = (bf16[8,288,128]{2,1,0:T(8,128)(2,1)S(1)}, bf16[8,288,128]{2,1,0:T(8,128)(2,1)S(1)}) custom-call(s32[4]{0:T(128)S(1)} %pad_add_fusion.info_ref, bf16[24,384,1536]{2,1,0:T(8,128)(2,1)} %get-tuple-element.68.p_ref, bf16[24,384,128]{2,1,0:T(8,128)(2,1)} %get-tuple-element.69.vn_ref, bf16[24,128,384]{2,1,0:T(8,128)(2,1)} %get-tuple-element.79.do_ref, ...), custom_call_target="tpu_custom_call" | custom-call | flops 13600000000 | bytes 1048576 | tf_op jit(solution)/shard_map/score/pallas_call | solution.py:797
  120.8 5.6 %all-to-all-start.2 = ((bf16[8,416,128]{2,1,0:T(8,128)(2,1)}), bf16[8,416,128]{2,1,0:T(8,128)(2,1)S(1)}, u32[]{:S(2)}, u32[]{:S(2)}) async-start(bf16[8,416,128]{2,1,0:T(8,128)(2,1)} %pad_maximum_fusion), calls=%async_computation.2 | async-start | bytes 1703936 | tf_op jit(solution)/shard_map/all_to_all | solution.py:1171
  126.4 35.8 %back.1 = (f32[192,128]{1,0:T(8,128)S(1)}, f32[192,128]{1,0:T(8,128)S(1)}) custom-call(s32[4]{0:T(128)S(1)} %pad_add_fusion.info_ref, bf16[24,384,1536]{2,1,0:T(8,128)(2,1)} %get-tuple-element.68.p_ref, bf16[24,384,384]{2,1,0:T(8,128)(2,1)} %get-tuple-element.64.q_ref.k_ref.v_ref, bf16[24,384,384]{2,1,0:T(8,128)(2,1)} %get-tuple-element.64.q_ref.k_ref.v_ref, ...), custom_call_target="tpu_custom_call" | custom-call | flops 30400000000 | bytes 1048576 | tf_op jit(solution)/shard_map/back/pallas_call | solution.py:797
  163.6 2.7 %late.1 = (f32[200,128]{1,0:T(8,128)S(1)}, bf16[200,128]{1,0:T(8,128)(2,1)S(1)}) custom-call(bf16[8,416,128]{2,1,0:T(8,128)(2,1)S(1)} %all-to-all-done.2.spread_ref, f32[192,128]{1,0:T(8,128)S(1)} %get-tuple-element.80.keep_ref, f32[192,128]{1,0:T(8,128)S(1)} %collective-permute-done.8.got_ref, bf16[24,128,384]{2,1,0:T(8,128)(2,1)} %get-tuple-element.57.zbt_ref), custom_call_target="tpu_custom_call" | custom-call | flops 2400000000 | bytes 1048576 | tf_op jit(solution)/shard_map/late/pallas_call | solution.py:797
  166.3 3.0 %collective-permute-start.9 = (bf16[200,128]{1,0:T(8,128)(2,1)S(1)}, bf16[200,128]{1,0:T(8,128)(2,1)S(1)}, u32[]{:S(2)}, u32[]{:S(2)}) collective-permute-start(bf16[200,128]{1,0:T(8,128)(2,1)S(1)} %get-tuple-element.83), channel_id=1, source_target_pairs={{0,8},{1,9},{2,10},{3,11},{4,12},{5,13},{6,14},{7,15},{8,0},{9,1},... | collective-permute-start | bytes 153608 | tf_op jit(solution)/shard_map/ppermute | solution.py:1078
  169.3 1.5 collective-permute-start.7
  171.4 2.1 %collective-permute-start.10 = (f32[200,128]{1,0:T(8,128)S(1)}, f32[200,128]{1,0:T(8,128)S(1)}, u32[]{:S(2)}, u32[]{:S(2)}) collective-permute-start(f32[200,128]{1,0:T(8,128)S(1)} %convert_add_fusion), channel_id=1, source_target_pairs={{0,4},{1,5},{2,6},{3,7},{4,0},{5,1},{6,2},{7,3},{8,12},{9,13},{10,... | collective-permute-start | bytes 307208 | tf_op jit(solution)/shard_map/ppermute | solution.py:1078
  173.4 2.7 %collective-permute-done.10 = f32[200,128]{1,0:T(8,128)S(1)} collective-permute-done((f32[200,128]{1,0:T(8,128)S(1)}, f32[200,128]{1,0:T(8,128)S(1)}, u32[]{:S(2)}, u32[]{:S(2)}) %collective-permute-start.10) | collective-permute-done | bytes 102432 | tf_op jit(solution)/shard_map/ppermute | solution.py:1078
  176.1 3.2 %collective-permute-start.11 = (f32[200,128]{1,0:T(8,128)S(1)}, f32[200,128]{1,0:T(8,128)S(1)}, u32[]{:S(2)}, u32[]{:S(2)}) collective-permute-start(f32[200,128]{1,0:T(8,128)S(1)} %add.38), channel_id=1, source_target_pairs={{0,2},{1,3},{2,0},{3,1},{4,6},{5,7},{6,4},{7,5},{8,10},{9,11},{10,... | collective-permute-start | bytes 307208 | tf_op jit(solution)/shard_map/ppermute | solution.py:1078
  179.3 2.6 %collective-permute-done.11 = f32[200,128]{1,0:T(8,128)S(1)} collective-permute-done((f32[200,128]{1,0:T(8,128)S(1)}, f32[200,128]{1,0:T(8,128)S(1)}, u32[]{:S(2)}, u32[]{:S(2)}) %collective-permute-start.11) | collective-permute-done | bytes 102432 | tf_op jit(solution)/shard_map/ppermute | solution.py:1078
  181.9 1.5 collective-permute-start.12
  183.6 3.0 %collective-permute-done.12 = f32[200,128]{1,0:T(8,128)S(1)} collective-permute-done((f32[200,128]{1,0:T(8,128)S(1)}, f32[200,128]{1,0:T(8,128)S(1)}, u32[]{:S(2)}, u32[]{:S(2)}) %collective-permute-start.12) | collective-permute-done | bytes 102432 | tf_op jit(solution)/shard_map/ppermute | solution.py:1078
  188.1 3.0 %finish.1 = (f32[8,576]{1,0:T(8,128)}, f32[8]{0:T(128)}, f32[576]{0:T(1024)}, f32[8,576]{1,0:T(8,128)}, f32[32,64]{1,0:T(8,128)}, /*index=5*/f32[32]{0:T(128)}, ...) custom-call(s32[4]{0:T(128)S(1)} %pad_add_fusion.info_ref, ...), custom_call_target="tpu_custom_call" | custom-call | flops 3200000000 | bytes 1048576 | tf_op jit(solution)/shard_map/finish/pallas_call | solution.py:797
  (58 shorter events, 11.0 us)
Async XLA Ops:
  0.6 9.9 %copy-start.7 = (f32[3,128]{1,0:T(4,128)S(1)}, f32[3,128]{1,0:T(4,128)}, u32[]{:S(2)}) copy-start(f32[3,128]{1,0:T(4,128)} %gains_ref.5) | copy-start | bytes 4612
  2.2 19.8 %all-to-all-start = ((bf16[16,8,1088]{2,1,0:T(8,128)(2,1)}), bf16[16,8,1088]{2,1,0:T(8,128)(2,1)S(1)}, u32[]{:S(2)}, u32[]{:S(2)}) async-start(bf16[16,8,1088]{2,1,0:T(8,128)(2,1)} %pack.1), calls=%async_computation | async-start | bytes 589824 | tf_op jit(solution)/shard_map/all_to_all | solution.py:1130
  15.8 7.4 %collective-permute-start.1 = (bf16[1,4,24,384]{3,2,1,0:T(8,128)(2,1)S(1)}, bf16[1,4,24,384]{3,2,1,0:T(8,128)(2,1)S(1)}, u32[]{:S(2)}, u32[]{:S(2)}) collective-permute-start(bf16[1,4,24,384]{3,2,1,0:T(8,128)(2,1)S(1)} %bitcast.18), channel_id=1, source_target_pairs={{0,8},{1,9},{2,10},{3,11},{4,12},{5,13},{6,14},{7,15},{8,0},{9,1},... | collective-permute-start | bytes 221192 | tf_op jit(solution)/shard_map/ppermute | solution.py:1078
  22.1 7.9 %collective-permute-start = (bf16[16,8,1088]{2,1,0:T(8,128)(2,1)S(1)}, bf16[16,8,1088]{2,1,0:T(8,128)(2,1)S(1)}, u32[]{:S(2)}, u32[]{:S(2)}) collective-permute-start(bf16[16,8,1088]{2,1,0:T(8,128)(2,1)S(1)} %all-to-all-done.mine_ref.packs_ref), channel_id=1, source_target_pairs={{0,1},{1,0},{2,3},{3,2},{4,5},{5,4},{6,7},{7,6},{8,9},{9,8},{10,11... | collective-permute-start | bytes 835592 | tf_op jit(solution)/shard_map/ppermute | solution.py:1078
  23.2 5.2 %collective-permute-start.2 = (bf16[2,4,24,384]{3,2,1,0:T(8,128)(2,1)S(1)}, bf16[2,4,24,384]{3,2,1,0:T(8,128)(2,1)S(1)}, u32[]{:S(2)}, u32[]{:S(2)}) collective-permute-start(bf16[2,4,24,384]{3,2,1,0:T(8,128)(2,1)S(1)} %pad_maximum_fusion.2), channel_id=1, source_target_pairs={{0,4},{1,5},{2,6},{3,7},{4,0},{5,1},{6,2},{7,3},{8,12},{9,13},{10,... | collective-permute-start | bytes 442376 | tf_op jit(solution)/shard_map/ppermute | solution.py:1078
  28.5 9.2 %collective-permute-start.3 = (bf16[4,4,24,384]{3,2,1,0:T(8,128)(2,1)S(1)}, bf16[4,4,24,384]{3,2,1,0:T(8,128)(2,1)S(1)}, u32[]{:S(2)}, u32[]{:S(2)}) collective-permute-start(bf16[4,4,24,384]{3,2,1,0:T(8,128)(2,1)S(1)} %pad_maximum_fusion.1), channel_id=1, source_target_pairs={{0,2},{1,3},{2,0},{3,1},{4,6},{5,7},{6,4},{7,5},{8,10},{9,11},{10,... | collective-permute-start | bytes 884744 | tf_op jit(solution)/shard_map/ppermute | solution.py:1078
  37.8 2.1 %collective-permute-start.4 = (bf16[8,4,24,384]{3,2,1,0:T(8,128)(2,1)S(1)}, bf16[8,4,24,384]{3,2,1,0:T(8,128)(2,1)S(1)}, u32[]{:S(2)}, u32[]{:S(2)}) collective-permute-start(bf16[8,4,24,384]{3,2,1,0:T(8,128)(2,1)S(1)} %maximum_add_fusion.bias_ref), channel_id=1, source_target_pairs={{0,1},{1,0},{2,3},{3,2},{4,5},{5,4},{6,7},{7,6},{8,9},{9,8},{10,11... | collective-permute-start | bytes 1769480 | tf_op jit(solution)/shard_map/ppermute | solution.py:1078
  39.9 27.5 %copy-start.1 = (s32[1,24,384]{2,1,0:T(8,128)S(1)}, s32[1,24,384]{2,1,0:T(8,128)}, u32[]{:S(2)}) copy-start(s32[1,24,384]{2,1,0:T(8,128)} %tgt_ref.1) | copy-start | bytes 110596
  39.9 27.5 %copy-start.2 = (s32[1,24,384]{2,1,0:T(8,128)S(1)}, s32[1,24,384]{2,1,0:T(8,128)}, u32[]{:S(2)}) copy-start(s32[1,24,384]{2,1,0:T(8,128)} %nbr_ref.1) | copy-start | bytes 110596
  98.1 18.2 %all-to-all-start.1 = ((bf16[32,48,128]{2,1,0:T(8,128)(2,1)}), bf16[32,48,128]{2,1,0:T(8,128)(2,1)S(1)}, u32[]{:S(2)}, u32[]{:S(2)}) async-start(bf16[32,48,128]{2,1,0:T(8,128)(2,1)} %bitcast.6), calls=%async_computation.1 | async-start | bytes 786432 | tf_op jit(solution)/shard_map/all_to_all | solution.py:1160
  116.3 2.2 %collective-permute-start.5 = (bf16[8,288,128]{2,1,0:T(8,128)(2,1)S(1)}, bf16[8,288,128]{2,1,0:T(8,128)(2,1)}, u32[]{:S(2)}, u32[]{:S(2)}) collective-permute-start(bf16[8,288,128]{2,1,0:T(8,128)(2,1)S(1)} %get-tuple-element.75), channel_id=1, source_target_pairs={{0,1},{1,0},{2,3},{3,2},{4,5},{5,4},{6,7},{7,6},{8,9},{9,8},{10,11... | collective-permute-start | bytes 1769480 | tf_op jit(solution)/shard_map/ppermute | solution.py:1078
  116.5 1.9 collective-permute-start.6
  120.8 42.8 %all-to-all-start.2 = ((bf16[8,416,128]{2,1,0:T(8,128)(2,1)}), bf16[8,416,128]{2,1,0:T(8,128)(2,1)S(1)}, u32[]{:S(2)}, u32[]{:S(2)}) async-start(bf16[8,416,128]{2,1,0:T(8,128)(2,1)} %pad_maximum_fusion), calls=%async_computation.2 | async-start | bytes 1703936 | tf_op jit(solution)/shard_map/all_to_all | solution.py:1171
  162.2 1.4 collective-permute-start.8
  163.6 24.5 %copy-start.4 = (f32[128,68]{0,1:T(8,128)S(1)}, f32[128,68]{0,1:T(8,128)}, u32[]{:S(2)}) copy-start(f32[128,68]{0,1:T(8,128)} %param.27) | copy-start | bytes 104452
  163.6 24.5 %copy-start.5 = (f32[8,576]{1,0:T(8,128)S(1)}, f32[8,576]{1,0:T(8,128)}, u32[]{:S(2)}) copy-start(f32[8,576]{1,0:T(8,128)} %wide_ref.3) | copy-start | bytes 55300
  163.6 24.5 %copy-start.6 = (f32[32,64]{1,0:T(8,128)S(1)}, f32[32,64]{1,0:T(8,128)}, u32[]{:S(2)}) copy-start(f32[32,64]{1,0:T(8,128)} %down_ref.3) | copy-start | bytes 24580
  163.6 24.5 %copy-start.8 = (f32[3,128]{1,0:T(4,128)S(1)}, f32[3,128]{1,0:T(4,128)}, u32[]{:S(2)}) copy-start(f32[3,128]{1,0:T(4,128)} %gain_second_ref.1) | copy-start | bytes 4612
  166.3 5.1 %collective-permute-start.9 = (bf16[200,128]{1,0:T(8,128)(2,1)S(1)}, bf16[200,128]{1,0:T(8,128)(2,1)S(1)}, u32[]{:S(2)}, u32[]{:S(2)}) collective-permute-start(bf16[200,128]{1,0:T(8,128)(2,1)S(1)} %get-tuple-element.83), channel_id=1, source_target_pairs={{0,8},{1,9},{2,10},{3,11},{4,12},{5,13},{6,14},{7,15},{8,0},{9,1},... | collective-permute-start | bytes 153608 | tf_op jit(solution)/shard_map/ppermute | solution.py:1078
  169.3 10.0 %collective-permute-start.7 = (bf16[8,128,128]{2,1,0:T(8,128)(2,1)S(1)}, bf16[8,128,128]{2,1,0:T(8,128)(2,1)S(1)}, u32[]{:S(2)}, u32[]{:S(2)}) collective-permute-start(bf16[8,128,128]{2,1,0:T(8,128)(2,1)S(1)} %slice.21), channel_id=1, source_target_pairs={{0,16},{1,17},{2,18},{3,19},{4,20},{5,21},{6,22},{7,23},{8,24},{9,... | collective-permute-start | bytes 786440 | tf_op jit(solution)/shard_map/ppermute | solution.py:1078
  171.4 4.7 %collective-permute-start.10 = (f32[200,128]{1,0:T(8,128)S(1)}, f32[200,128]{1,0:T(8,128)S(1)}, u32[]{:S(2)}, u32[]{:S(2)}) collective-permute-start(f32[200,128]{1,0:T(8,128)S(1)} %convert_add_fusion), channel_id=1, source_target_pairs={{0,4},{1,5},{2,6},{3,7},{4,0},{5,1},{6,2},{7,3},{8,12},{9,13},{10,... | collective-permute-start | bytes 307208 | tf_op jit(solution)/shard_map/ppermute | solution.py:1078
  176.1 5.8 %collective-permute-start.11 = (f32[200,128]{1,0:T(8,128)S(1)}, f32[200,128]{1,0:T(8,128)S(1)}, u32[]{:S(2)}, u32[]{:S(2)}) collective-permute-start(f32[200,128]{1,0:T(8,128)S(1)} %add.38), channel_id=1, source_target_pairs={{0,2},{1,3},{2,0},{3,1},{4,6},{5,7},{6,4},{7,5},{8,10},{9,11},{10,... | collective-permute-start | bytes 307208 | tf_op jit(solution)/shard_map/ppermute | solution.py:1078
  181.9 4.7 %collective-permute-start.12 = (f32[200,128]{1,0:T(8,128)S(1)}, f32[200,128]{1,0:T(8,128)S(1)}, u32[]{:S(2)}, u32[]{:S(2)}) collective-permute-start(f32[200,128]{1,0:T(8,128)S(1)} %add_add_fusion), channel_id=1, source_target_pairs={{0,16},{1,17},{2,18},{3,19},{4,20},{5,21},{6,22},{7,23},{8,24},{9,... | collective-permute-start | bytes 307208 | tf_op jit(solution)/shard_map/ppermute | solution.py:1078
  186.7 1.4 collective-permute-start.13
  (3 other events, 23.6 us)

commit v5 on v4

--- a/solution.py
+++ b/solution.py
@@ -433,13 +433,9 @@
             x, y = h * HEAD_DIM, (h + 1) * HEAD_DIM
             share = r[h : h + 1]
             parts.append((do[x:y] * share).astype(bf16))
-            less = -jnp.sum(doo[x:y], 0, keepdims=True) * share
-            upper = rounded(less)
-            minus.append(
-                jnp.concatenate([upper, less - upper, jnp.zeros((14, less.shape[1]), f32)], 0)
-            )
+            minus.append(-jnp.sum(doo[x:y], 0, keepdims=True) * share)
         out(do_ref, jnp.concatenate(parts, 0))
-        out(nd_ref, jnp.concatenate(minus, 0).astype(bf16))
+        out(nd_ref, jnp.concatenate(minus + minus, 0))
 
     blocks = group * width // 128
     running = [
@@ -519,7 +515,11 @@
         a, b = h * HEAD_DIM, (h + 1) * HEAD_DIM
         at = slice(h * width, (h + 1) * width)
         dobd[g, a:b, at] = do_ref[g, a:b]
-        dobd[g, CZ : CZ + 16, at] = nd_ref[g, 16 * h : 16 * (h + 1)]
+        minus = nd_ref[g, h : h + 1]
+        upper = rounded(minus)
+        dobd[g, CZ : CZ + 16, at] = jnp.concatenate(
+            [upper, minus - upper, jnp.zeros((14, width), f32)], 0
+        ).astype(bf16)
 
 
 def back_kernel(
@@ -653,7 +653,6 @@
 
     lines = BLOCKS * CZ // (crops * rows)
     height = lines + 16
-    start = spread_ref.shape[1] - 2 * height
     tail = jnp.zeros((1, CZ), f32)
     for c in range(crops):
         for r in range(rows):
@@ -661,9 +660,9 @@
             which = (r % 2) ^ side
             block = jnp.zeros((height, CZ), f32)
             for p in range(2):
-                part = slice(start + p * height, start + (p + 1) * height)
+                part = slice(p * height, (p + 1) * height)
                 here = spread_ref[r // 2, part].astype(f32)
-                there = across_ref[r // 2, p * height : (p + 1) * height].astype(f32)
+                there = across_ref[r // 2, part].astype(f32)
                 block = jnp.where(which == p, jnp.where(c == crop, here, there), block)
             flat[at : at + lines, :] = block[:lines]
             tail += block[lines : lines + 1]
@@ -854,7 +853,7 @@
 
 def project(crops, rows, info, mine, other, zbt):
     count, _, width = zbt.shape
-    g = group_of(count, 6)
+    g = group_of(count, 8)
     return call(
         partial(project_kernel, crops, rows),
         "project",
@@ -875,12 +874,12 @@
 
 
 FRONT_ROWS = 12
-ATTEND_ROWS = 4
+ATTEND_ROWS = 3
 MIDDLE_ROWS = 8
 MIDDLE_PART = 2
 MIDDLE_LAG = 1
 SCORE_ROWS = 6
-BACK_ROWS = 3
+BACK_ROWS = 4
 LATE_ROWS = 12
 
 
@@ -940,7 +939,7 @@
         ],
         [
             (rows_of(g, CZ, width), (count, CZ, width), bf16),
-            (rows_of(g, 16 * HEADS, width), (count, 16 * HEADS, width), bf16),
+            (rows_of(g, 2 * HEADS, width), (count, 2 * HEADS, width), f32),
             (whole((BLOCKS, CZ, CZ)), (BLOCKS, CZ, CZ), bf16),
             (whole((16, CZ)), (16, CZ), bf16),
         ],
@@ -976,7 +975,7 @@
             rows_of(g, width, HEADS * width),
             rows_of(g, width, CZ),
             rows_of(g, CZ, width),
-            rows_of(g, 16 * HEADS, width),
+            rows_of(g, 2 * HEADS, width),
         ],
         [(whole(shape), shape, bf16)] * 2,
         [
@@ -1027,7 +1026,7 @@
             rows_of(g, CZ, width, 1),
             rows_of(g, width, CZ),
             rows_of(g, CZ, width),
-            rows_of(g, 16 * HEADS, width),
+            rows_of(g, 2 * HEADS, width),
             rows_of(g, CZ, width),
         ],
         [(whole((half, CZ)), (half, CZ), f32)] * 2,
@@ -1171,7 +1170,8 @@
         parcel = lax.all_to_all(parcel, "row", 0, 0, axis_index_groups=row_sides, tiled=True)
         keep, give = back(info, p, qkv, vn, do, nd, zbt)
         got = swap(give, both, devices, 1)
-        across = swap(parcel[:, -2 * early_lines :], both, devices, rows)
+        ours = parcel[:, -2 * early_lines :]
+        across = swap(ours, both, devices, rows)
         keep, send = late_sums(parcel, keep, got, zbt)
         for n, mask in enumerate(all_masks[:-1]):
             if n == 0:
@@ -1181,7 +1181,7 @@
                     keep = keep + across[0, -16:-15].astype(f32) * 0.0
                 keep = keep + swap(keep, both, devices, mask)
         other = swap(keep, both, devices, 1)
-        scalars = jnp.stack([parcel[:, -2 * early_lines :], across])
+        scalars = jnp.stack([ours, across])
         scalars = scalars.reshape(crops, rows, -1, CZ)[:, :, -16, :6]
         scalars = jnp.sum(scalars.astype(f32), (0, 1)).reshape(3, 2)
         loss_sum, pair_count = jnp.sum(scalars[:, 0]), jnp.sum(scalars[:, 1])
@@ -1206,7 +1206,7 @@
             info,
             keep,
             other,
-            parcel,
+            ours,
             across,
             packs,
             other_packs,

time: 192 us -> 189 us (0.984)
  Pallas kernels: 128 us -> 126 us
  transfers between devices with their start and end apart: 17 -> 17, of which waited for: 12 -> 11; matrix products, arithmetic and copies ran while one was open for 1% -> 1% of each run, Pallas kernels for 33% -> 33%
where the time goes in v5:
time: 189 us
  Pallas kernels  126 us (67%)
  starting transfers between devices  34.4 us (18%)
  waiting for transfers between devices  23.1 us (12%)
  between operations  2.34 us (1%)
  other arithmetic  2.23 us (1%)
    pallas_call x9, Pallas kernels, call(): pl.pallas_call(kernel, grid=(grid,), in_specs=in_specs, out_specs=[o[0] f...  126 us
    ppermute x14, waiting for transfers between devices, swap(): return lax.ppermute(x, axes, [(i, i ^ mask) for i in range(size)])  19.6 us
    ppermute x14, starting transfers between devices, swap(): return lax.ppermute(x, axes, [(i, i ^ mask) for i in range(size)])  16.6 us
    all_to_all x1, starting transfers between devices, body(): lax.all_to_all(pack, both, 0, 0, axis_index_groups=sides, tiled=True)  8.31 us
    all_to_all x1, starting transfers between devices, body(): lax.all_to_all(parcel, 'row', 0, 0, axis_index_groups=row_sides, tiled=True)  5.62 us
    all_to_all x1, starting transfers between devices, body(): lax.all_to_all(early.reshape(devices, -1, CZ), both, 0, 0, tiled=True)  3.85 us
  transfers between devices with their start and end apart: 17, of which 11 were waited for; matrix products, arithmetic and copies ran while one was open for 1% of the time, Pallas kernels for 33%

profile of v5, /device:TPU:0, one launch (start us, length us, event | category | flops | bytes accessed | tf_op | source)
XLA Modules:
  0.0 188.6 jit_solution(4594797980203127110)
XLA Ops:
  0.7 1.6 pack.1
  2.2 8.3 %all-to-all-start = ((bf16[16,8,1088]{2,1,0:T(8,128)(2,1)}), bf16[16,8,1088]{2,1,0:T(8,128)(2,1)S(1)}, u32[]{:S(2)}, u32[]{:S(2)}) async-start(bf16[16,8,1088]{2,1,0:T(8,128)(2,1)} %pack.1), calls=%async_computation | async-start | bytes 589824 | tf_op jit(solution)/shard_map/all_to_all | solution.py:1129
  10.6 5.2 %front.1 = (bf16[24,128,384]{2,1,0:T(8,128)(2,1)}, bf16[24,128,384]{2,1,0:T(8,128)(2,1)}, bf16[4,24,384]{2,1,0:T(8,128)(2,1)S(1)}) custom-call(bf16[24,384,128]{2,1,0:T(8,128)(2,1)} %bitcast.29, f32[3,128]{1,0:T(4,128)S(1)} %copy-done.6, f32[68,128]{1,0:T(8,128)S(1)} %bitcast.24), custom_call_target="tpu_custom_call" | custom-call | flops 4800000000 | bytes 1048576 | tf_op jit(solution)/shard_map/front/pallas_call | solution.py:796
  15.8 2.8 %collective-permute-start.1 = (bf16[1,4,24,384]{3,2,1,0:T(8,128)(2,1)S(1)}, bf16[1,4,24,384]{3,2,1,0:T(8,128)(2,1)S(1)}, u32[]{:S(2)}, u32[]{:S(2)}) collective-permute-start(bf16[1,4,24,384]{3,2,1,0:T(8,128)(2,1)S(1)} %bitcast.19), channel_id=1, source_target_pairs={{0,8},{1,9},{2,10},{3,11},{4,12},{5,13},{6,14},{7,15},{8,0},{9,1},... | collective-permute-start | bytes 221192 | tf_op jit(solution)/shard_map/ppermute | solution.py:1077
  18.6 3.5 %all-to-all-done.mine_ref.packs_ref = bf16[16,8,1088]{2,1,0:T(8,128)(2,1)S(1)} async-done(((bf16[16,8,1088]{2,1,0:T(8,128)(2,1)}), bf16[16,8,1088]{2,1,0:T(8,128)(2,1)S(1)}, u32[]{:S(2)}, u32[]{:S(2)}) %all-to-all-start) | async-done | bytes 278560 | tf_op jit(solution)/shard_map/all_to_all | solution.py:1129
  24.0 4.4 %collective-permute-done.2 = bf16[2,4,24,384]{3,2,1,0:T(8,128)(2,1)S(1)} collective-permute-done((bf16[2,4,24,384]{3,2,1,0:T(8,128)(2,1)S(1)}, bf16[2,4,24,384]{3,2,1,0:T(8,128)(2,1)S(1)}, u32[]{:S(2)}, u32[]{:S(2)}) %collective-permute-start.2) | collective-permute-done | bytes 147488 | tf_op jit(solution)/shard_map/ppermute | solution.py:1077
  30.0 6.7 %project.1 = (bf16[24,384,384]{2,1,0:T(8,128)(2,1)}, bf16[24,384,128]{2,1,0:T(8,128)(2,1)}, f32[8,9216]{1,0:T(8,128)S(1)}, bf16[128,1152]{1,0:T(8,128)(2,1)S(1)}...) custom-call(s32[4]{0:T(128)S(1)} %pad_add_fusion.info_ref, bf16[16,8,1088]{2,1,0:T(8,128)(2,1)S(1)} %all-to-all-done.mine_ref.packs_ref, ...), custom_call_target="tpu_custom_call" | custom-call | flops 32000000000 | bytes 1048576 | tf_op jit(solution)/shard_map/project/pallas_call | solution.py:796
  37.5 2.0 %collective-permute-done.4.other_bias_ref = bf16[8,4,24,384]{3,2,1,0:T(8,128)(2,1)S(1)} collective-permute-done((bf16[8,4,24,384]{3,2,1,0:T(8,128)(2,1)S(1)}, bf16[8,4,24,384]{3,2,1,0:T(8,128)(2,1)S(1)}, u32[]{:S(2)}, u32[]{:S(2)}) %collective-permute-start.4) | collective-permute-done | bytes 589856 | tf_op jit(solution)/shard_map/ppermute | solution.py:1077
  39.5 27.9 %attend.1 = (bf16[24,384,1536]{2,1,0:T(8,128)(2,1)}, f32[24,128,384]{2,1,0:T(8,128)}, f32[24,8,384]{2,1,0:T(8,128)S(1)}) custom-call(s32[4]{0:T(128)S(1)} %pad_add_fusion.info_ref, f32[8,9216]{1,0:T(8,128)S(1)} %get-tuple-element.61.norm_ref, bf16[8,4,24,384]{3,2,1,0:T(8,128)(2,1)S(1)} %maximum_add_fusion.bias_ref, ...), custom_call_target="tpu_custom_call" | custom-call | flops 20000000000 | bytes 1048576 | tf_op jit(solution)/shard_map/attend/pallas_call | solution.py:796
  67.5 30.3 %middle.1 = (bf16[24,128,384]{2,1,0:T(8,128)(2,1)}, f32[24,8,384]{2,1,0:T(8,128)S(1)}, bf16[12,128,128]{2,1,0:T(8,128)(2,1)}, bf16[16,128]{1,0:T(8,128)(2,1)S(1)}) custom-call(s32[4]{0:T(128)S(1)} %pad_add_fusion.info_ref, bf16[128,1152]{1,0:T(8,128)(2,1)S(1)} %get-tuple-element.58.wide_ref.full_ref, bf16[512,128]{1,0:T(8,128)(2,1)S(1)} %get-tuple-element.59.down_ref, ...), custom_call_target="tpu_custom_call" | custom-call | flops 24000000000 | bytes 1048576 | tf_op jit(solution)/shard_map/middle/pallas_call | solution.py:796
  97.7 3.8 %all-to-all-start.1 = ((bf16[32,48,128]{2,1,0:T(8,128)(2,1)}), bf16[32,48,128]{2,1,0:T(8,128)(2,1)S(1)}, u32[]{:S(2)}, u32[]{:S(2)}) async-start(bf16[32,48,128]{2,1,0:T(8,128)(2,1)} %bitcast.6), calls=%async_computation.1 | async-start | bytes 786432 | tf_op jit(solution)/shard_map/all_to_all | solution.py:1159
  101.6 14.1 %score.1 = (bf16[8,288,128]{2,1,0:T(8,128)(2,1)S(1)}, bf16[8,288,128]{2,1,0:T(8,128)(2,1)S(1)}) custom-call(s32[4]{0:T(128)S(1)} %pad_add_fusion.info_ref, bf16[24,384,1536]{2,1,0:T(8,128)(2,1)} %get-tuple-element.68.p_ref, bf16[24,384,128]{2,1,0:T(8,128)(2,1)} %get-tuple-element.69.vn_ref, bf16[24,128,384]{2,1,0:T(8,128)(2,1)} %get-tuple-element.79.do_ref, ...), custom_call_target="tpu_custom_call" | custom-call | flops 13600000000 | bytes 1048576 | tf_op jit(solution)/shard_map/score/pallas_call | solution.py:796
  119.0 5.6 %all-to-all-start.2 = ((bf16[8,416,128]{2,1,0:T(8,128)(2,1)}), bf16[8,416,128]{2,1,0:T(8,128)(2,1)S(1)}, u32[]{:S(2)}, u32[]{:S(2)}) async-start(bf16[8,416,128]{2,1,0:T(8,128)(2,1)} %pad_maximum_fusion), calls=%async_computation.2 | async-start | bytes 1703936 | tf_op jit(solution)/shard_map/all_to_all | solution.py:1170
  124.6 35.8 %back.1 = (f32[192,128]{1,0:T(8,128)S(1)}, f32[192,128]{1,0:T(8,128)S(1)}) custom-call(s32[4]{0:T(128)S(1)} %pad_add_fusion.info_ref, bf16[24,384,1536]{2,1,0:T(8,128)(2,1)} %get-tuple-element.68.p_ref, bf16[24,384,384]{2,1,0:T(8,128)(2,1)} %get-tuple-element.64.q_ref.k_ref.v_ref, bf16[24,384,384]{2,1,0:T(8,128)(2,1)} %get-tuple-element.64.q_ref.k_ref.v_ref, ...), custom_call_target="tpu_custom_call" | custom-call | flops 30400000000 | bytes 1048576 | tf_op jit(solution)/shard_map/back/pallas_call | solution.py:796
  161.8 2.4 %late.1 = (f32[200,128]{1,0:T(8,128)S(1)}, bf16[200,128]{1,0:T(8,128)(2,1)S(1)}) custom-call(bf16[8,416,128]{2,1,0:T(8,128)(2,1)S(1)} %all-to-all-done.2.spread_ref, f32[192,128]{1,0:T(8,128)S(1)} %get-tuple-element.80.keep_ref, f32[192,128]{1,0:T(8,128)S(1)} %collective-permute-done.8.got_ref, bf16[24,128,384]{2,1,0:T(8,128)(2,1)} %get-tuple-element.57.zbt_ref), custom_call_target="tpu_custom_call" | custom-call | flops 2400000000 | bytes 1048576 | tf_op jit(solution)/shard_map/late/pallas_call | solution.py:796
  164.2 3.0 %collective-permute-start.9 = (bf16[200,128]{1,0:T(8,128)(2,1)S(1)}, bf16[200,128]{1,0:T(8,128)(2,1)S(1)}, u32[]{:S(2)}, u32[]{:S(2)}) collective-permute-start(bf16[200,128]{1,0:T(8,128)(2,1)S(1)} %get-tuple-element.83), channel_id=1, source_target_pairs={{0,8},{1,9},{2,10},{3,11},{4,12},{5,13},{6,14},{7,15},{8,0},{9,1},... | collective-permute-start | bytes 153608 | tf_op jit(solution)/shard_map/ppermute | solution.py:1077
  167.2 1.5 collective-permute-start.7
  169.3 2.1 %collective-permute-start.10 = (f32[200,128]{1,0:T(8,128)S(1)}, f32[200,128]{1,0:T(8,128)S(1)}, u32[]{:S(2)}, u32[]{:S(2)}) collective-permute-start(f32[200,128]{1,0:T(8,128)S(1)} %convert_add_fusion), channel_id=1, source_target_pairs={{0,4},{1,5},{2,6},{3,7},{4,0},{5,1},{6,2},{7,3},{8,12},{9,13},{10,... | collective-permute-start | bytes 307208 | tf_op jit(solution)/shard_map/ppermute | solution.py:1077
  171.3 2.6 %collective-permute-done.10 = f32[200,128]{1,0:T(8,128)S(1)} collective-permute-done((f32[200,128]{1,0:T(8,128)S(1)}, f32[200,128]{1,0:T(8,128)S(1)}, u32[]{:S(2)}, u32[]{:S(2)}) %collective-permute-start.10) | collective-permute-done | bytes 102432 | tf_op jit(solution)/shard_map/ppermute | solution.py:1077
  174.0 3.2 %collective-permute-start.11 = (f32[200,128]{1,0:T(8,128)S(1)}, f32[200,128]{1,0:T(8,128)S(1)}, u32[]{:S(2)}, u32[]{:S(2)}) collective-permute-start(f32[200,128]{1,0:T(8,128)S(1)} %add.38), channel_id=1, source_target_pairs={{0,2},{1,3},{2,0},{3,1},{4,6},{5,7},{6,4},{7,5},{8,10},{9,11},{10,... | collective-permute-start | bytes 307208 | tf_op jit(solution)/shard_map/ppermute | solution.py:1077
  177.2 2.6 %collective-permute-done.11 = f32[200,128]{1,0:T(8,128)S(1)} collective-permute-done((f32[200,128]{1,0:T(8,128)S(1)}, f32[200,128]{1,0:T(8,128)S(1)}, u32[]{:S(2)}, u32[]{:S(2)}) %collective-permute-start.11) | collective-permute-done | bytes 102432 | tf_op jit(solution)/shard_map/ppermute | solution.py:1077
  179.8 1.6 collective-permute-start.12
  181.5 3.0 %collective-permute-done.12 = f32[200,128]{1,0:T(8,128)S(1)} collective-permute-done((f32[200,128]{1,0:T(8,128)S(1)}, f32[200,128]{1,0:T(8,128)S(1)}, u32[]{:S(2)}, u32[]{:S(2)}) %collective-permute-start.12) | collective-permute-done | bytes 102432 | tf_op jit(solution)/shard_map/ppermute | solution.py:1077
  186.0 2.4 %finish.1 = (f32[8,576]{1,0:T(8,128)}, f32[8]{0:T(128)}, f32[576]{0:T(1024)}, f32[8,576]{1,0:T(8,128)}, f32[32,64]{1,0:T(8,128)}, /*index=5*/f32[32]{0:T(128)}, ...) custom-call(s32[4]{0:T(128)S(1)} %pad_add_fusion.info_ref, ...), custom_call_target="tpu_custom_call" | custom-call | flops 3200000000 | bytes 1048576 | tf_op jit(solution)/shard_map/finish/pallas_call | solution.py:796
  (54 shorter events, 9.8 us)
Async XLA Ops:
  0.6 9.9 %copy-start.6 = (f32[3,128]{1,0:T(4,128)S(1)}, f32[3,128]{1,0:T(4,128)}, u32[]{:S(2)}) copy-start(f32[3,128]{1,0:T(4,128)} %gains_ref.5) | copy-start | bytes 4612
  2.2 19.8 %all-to-all-start = ((bf16[16,8,1088]{2,1,0:T(8,128)(2,1)}), bf16[16,8,1088]{2,1,0:T(8,128)(2,1)S(1)}, u32[]{:S(2)}, u32[]{:S(2)}) async-start(bf16[16,8,1088]{2,1,0:T(8,128)(2,1)} %pack.1), calls=%async_computation | async-start | bytes 589824 | tf_op jit(solution)/shard_map/all_to_all | solution.py:1129
  15.8 7.4 %collective-permute-start.1 = (bf16[1,4,24,384]{3,2,1,0:T(8,128)(2,1)S(1)}, bf16[1,4,24,384]{3,2,1,0:T(8,128)(2,1)S(1)}, u32[]{:S(2)}, u32[]{:S(2)}) collective-permute-start(bf16[1,4,24,384]{3,2,1,0:T(8,128)(2,1)S(1)} %bitcast.19), channel_id=1, source_target_pairs={{0,8},{1,9},{2,10},{3,11},{4,12},{5,13},{6,14},{7,15},{8,0},{9,1},... | collective-permute-start | bytes 221192 | tf_op jit(solution)/shard_map/ppermute | solution.py:1077
  22.1 7.9 %collective-permute-start = (bf16[16,8,1088]{2,1,0:T(8,128)(2,1)S(1)}, bf16[16,8,1088]{2,1,0:T(8,128)(2,1)S(1)}, u32[]{:S(2)}, u32[]{:S(2)}) collective-permute-start(bf16[16,8,1088]{2,1,0:T(8,128)(2,1)S(1)} %all-to-all-done.mine_ref.packs_ref), channel_id=1, source_target_pairs={{0,1},{1,0},{2,3},{3,2},{4,5},{5,4},{6,7},{7,6},{8,9},{9,8},{10,11... | collective-permute-start | bytes 835592 | tf_op jit(solution)/shard_map/ppermute | solution.py:1077
  23.2 5.2 %collective-permute-start.2 = (bf16[2,4,24,384]{3,2,1,0:T(8,128)(2,1)S(1)}, bf16[2,4,24,384]{3,2,1,0:T(8,128)(2,1)S(1)}, u32[]{:S(2)}, u32[]{:S(2)}) collective-permute-start(bf16[2,4,24,384]{3,2,1,0:T(8,128)(2,1)S(1)} %pad_maximum_fusion.2), channel_id=1, source_target_pairs={{0,4},{1,5},{2,6},{3,7},{4,0},{5,1},{6,2},{7,3},{8,12},{9,13},{10,... | collective-permute-start | bytes 442376 | tf_op jit(solution)/shard_map/ppermute | solution.py:1077
  28.5 8.9 %collective-permute-start.3 = (bf16[4,4,24,384]{3,2,1,0:T(8,128)(2,1)S(1)}, bf16[4,4,24,384]{3,2,1,0:T(8,128)(2,1)S(1)}, u32[]{:S(2)}, u32[]{:S(2)}) collective-permute-start(bf16[4,4,24,384]{3,2,1,0:T(8,128)(2,1)S(1)} %pad_maximum_fusion.1), channel_id=1, source_target_pairs={{0,2},{1,3},{2,0},{3,1},{4,6},{5,7},{6,4},{7,5},{8,10},{9,11},{10,... | collective-permute-start | bytes 884744 | tf_op jit(solution)/shard_map/ppermute | solution.py:1077
  37.5 2.1 %collective-permute-start.4 = (bf16[8,4,24,384]{3,2,1,0:T(8,128)(2,1)S(1)}, bf16[8,4,24,384]{3,2,1,0:T(8,128)(2,1)S(1)}, u32[]{:S(2)}, u32[]{:S(2)}) collective-permute-start(bf16[8,4,24,384]{3,2,1,0:T(8,128)(2,1)S(1)} %maximum_add_fusion.bias_ref), channel_id=1, source_target_pairs={{0,1},{1,0},{2,3},{3,2},{4,5},{5,4},{6,7},{7,6},{8,9},{9,8},{10,11... | collective-permute-start | bytes 1769480 | tf_op jit(solution)/shard_map/ppermute | solution.py:1077
  39.5 27.9 %copy-start = (s32[1,24,384]{2,1,0:T(8,128)S(1)}, s32[1,24,384]{2,1,0:T(8,128)}, u32[]{:S(2)}) copy-start(s32[1,24,384]{2,1,0:T(8,128)} %tgt_ref.1) | copy-start | bytes 110596
  39.5 27.9 %copy-start.1 = (s32[1,24,384]{2,1,0:T(8,128)S(1)}, s32[1,24,384]{2,1,0:T(8,128)}, u32[]{:S(2)}) copy-start(s32[1,24,384]{2,1,0:T(8,128)} %nbr_ref.1) | copy-start | bytes 110596
  97.7 18.0 %all-to-all-start.1 = ((bf16[32,48,128]{2,1,0:T(8,128)(2,1)}), bf16[32,48,128]{2,1,0:T(8,128)(2,1)S(1)}, u32[]{:S(2)}, u32[]{:S(2)}) async-start(bf16[32,48,128]{2,1,0:T(8,128)(2,1)} %bitcast.6), calls=%async_computation.1 | async-start | bytes 786432 | tf_op jit(solution)/shard_map/all_to_all | solution.py:1159
  115.7 2.1 %collective-permute-start.5 = (bf16[8,288,128]{2,1,0:T(8,128)(2,1)S(1)}, bf16[8,288,128]{2,1,0:T(8,128)(2,1)S(1)}, u32[]{:S(2)}, u32[]{:S(2)}) collective-permute-start(bf16[8,288,128]{2,1,0:T(8,128)(2,1)S(1)} %get-tuple-element.75), channel_id=1, source_target_pairs={{0,1},{1,0},{2,3},{3,2},{4,5},{5,4},{6,7},{7,6},{8,9},{9,8},{10,11... | collective-permute-start | bytes 1769480 | tf_op jit(solution)/shard_map/ppermute | solution.py:1077
  115.9 1.9 %collective-permute-start.6 = (bf16[1,64,128]{2,1,0:T(8,128)(2,1)S(1)}, bf16[1,64,128]{2,1,0:T(8,128)(2,1)S(1)}, u32[]{:S(2)}, u32[]{:S(2)}) collective-permute-start(bf16[1,64,128]{2,1,0:T(8,128)(2,1)S(1)} %maximum_bitcast_fusion), channel_id=1, source_target_pairs={{0,1},{1,0},{2,3},{3,2},{4,5},{5,4},{6,7},{7,6},{8,9},{9,8},{10,11... | collective-permute-start | bytes 49160 | tf_op jit(solution)/shard_map/ppermute | solution.py:1077
  119.0 42.8 %all-to-all-start.2 = ((bf16[8,416,128]{2,1,0:T(8,128)(2,1)}), bf16[8,416,128]{2,1,0:T(8,128)(2,1)S(1)}, u32[]{:S(2)}, u32[]{:S(2)}) async-start(bf16[8,416,128]{2,1,0:T(8,128)(2,1)} %pad_maximum_fusion), calls=%async_computation.2 | async-start | bytes 1703936 | tf_op jit(solution)/shard_map/all_to_all | solution.py:1170
  160.4 1.4 collective-permute-start.8
  161.8 24.2 %copy-start.3 = (f32[128,68]{0,1:T(8,128)S(1)}, f32[128,68]{0,1:T(8,128)}, u32[]{:S(2)}) copy-start(f32[128,68]{0,1:T(8,128)} %param.27) | copy-start | bytes 104452
  161.8 24.2 %copy-start.4 = (f32[8,576]{1,0:T(8,128)S(1)}, f32[8,576]{1,0:T(8,128)}, u32[]{:S(2)}) copy-start(f32[8,576]{1,0:T(8,128)} %wide_ref.3) | copy-start | bytes 55300
  161.8 24.2 %copy-start.5 = (f32[32,64]{1,0:T(8,128)S(1)}, f32[32,64]{1,0:T(8,128)}, u32[]{:S(2)}) copy-start(f32[32,64]{1,0:T(8,128)} %down_ref.3) | copy-start | bytes 24580
  161.8 24.2 %copy-start.7 = (f32[3,128]{1,0:T(4,128)S(1)}, f32[3,128]{1,0:T(4,128)}, u32[]{:S(2)}) copy-start(f32[3,128]{1,0:T(4,128)} %gain_second_ref.1) | copy-start | bytes 4612
  164.2 5.1 %collective-permute-start.9 = (bf16[200,128]{1,0:T(8,128)(2,1)S(1)}, bf16[200,128]{1,0:T(8,128)(2,1)S(1)}, u32[]{:S(2)}, u32[]{:S(2)}) collective-permute-start(bf16[200,128]{1,0:T(8,128)(2,1)S(1)} %get-tuple-element.83), channel_id=1, source_target_pairs={{0,8},{1,9},{2,10},{3,11},{4,12},{5,13},{6,14},{7,15},{8,0},{9,1},... | collective-permute-start | bytes 153608 | tf_op jit(solution)/shard_map/ppermute | solution.py:1077
  167.2 10.0 %collective-permute-start.7 = (bf16[8,128,128]{2,1,0:T(8,128)(2,1)S(1)}, bf16[8,128,128]{2,1,0:T(8,128)(2,1)S(1)}, u32[]{:S(2)}, u32[]{:S(2)}) collective-permute-start(bf16[8,128,128]{2,1,0:T(8,128)(2,1)S(1)} %slice.20.spread_ref), channel_id=1, source_target_pairs={{0,16},{1,17},{2,18},{3,19},{4,20},{5,21},{6,22},{7,23},{8,24},{9,... | collective-permute-start | bytes 786440 | tf_op jit(solution)/shard_map/ppermute | solution.py:1077
  169.3 4.7 %collective-permute-start.10 = (f32[200,128]{1,0:T(8,128)S(1)}, f32[200,128]{1,0:T(8,128)S(1)}, u32[]{:S(2)}, u32[]{:S(2)}) collective-permute-start(f32[200,128]{1,0:T(8,128)S(1)} %convert_add_fusion), channel_id=1, source_target_pairs={{0,4},{1,5},{2,6},{3,7},{4,0},{5,1},{6,2},{7,3},{8,12},{9,13},{10,... | collective-permute-start | bytes 307208 | tf_op jit(solution)/shard_map/ppermute | solution.py:1077
  174.0 5.8 %collective-permute-start.11 = (f32[200,128]{1,0:T(8,128)S(1)}, f32[200,128]{1,0:T(8,128)S(1)}, u32[]{:S(2)}, u32[]{:S(2)}) collective-permute-start(f32[200,128]{1,0:T(8,128)S(1)} %add.38), channel_id=1, source_target_pairs={{0,2},{1,3},{2,0},{3,1},{4,6},{5,7},{6,4},{7,5},{8,10},{9,11},{10,... | collective-permute-start | bytes 307208 | tf_op jit(solution)/shard_map/ppermute | solution.py:1077
  179.8 4.7 %collective-permute-start.12 = (f32[200,128]{1,0:T(8,128)S(1)}, f32[200,128]{1,0:T(8,128)S(1)}, u32[]{:S(2)}, u32[]{:S(2)}) collective-permute-start(f32[200,128]{1,0:T(8,128)S(1)} %add_add_fusion), channel_id=1, source_target_pairs={{0,16},{1,17},{2,18},{3,19},{4,20},{5,21},{6,22},{7,23},{8,24},{9,... | collective-permute-start | bytes 307208 | tf_op jit(solution)/shard_map/ppermute | solution.py:1077
  184.6 1.4 collective-permute-start.13
  (1 other events, 9.9 us)

commit v6 on v5

--- a/solution.py
+++ b/solution.py
@@ -266,7 +266,8 @@
                 a, b = h * HEAD_DIM, (h + 1) * HEAD_DIM
                 mine = r[:, h * width : (h + 1) * width]
                 r_ref[g, h : h + 1] = mine
-                o_ref[g, a:b] = dot(v_ref[g, a:b], p_ref[g, :, h * width : (h + 1) * width]) * mine
+                out = dot(v_ref[g, a:b], p_ref[g, :, h * width : (h + 1) * width]) * mine
+                o_ref[g, a:b] = out.astype(bf16)
 
     norms = jnp.max(norm_ref[...], 1, keepdims=True)
     reach = jnp.max(jnp.sqrt(norms[:HEADS] * norms[HEADS:])) * (1.01 * LOG2E * ROOT)
@@ -352,7 +353,7 @@
             for n, (g, at) in enumerate(spots):
                 ref[g, :, at : at + 128] = x[:, n * 128 : (n + 1) * 128]
 
-        o = mine(o_ref)
+        o = mine(o_ref).astype(f32)
         zb = mine(zbt_ref)
         gate = sigmoid(dot(wgt[...], zb))
         gain1 = wider(g1[...], o)
@@ -902,7 +903,7 @@
         ],
         [
             (rows_of(g, width, HEADS * width), (count, width, HEADS * width), bf16),
-            (rows_of(g, CZ, width), (count, CZ, width), f32),
+            (rows_of(g, CZ, width), (count, CZ, width), bf16),
             (rows_of(g, 8, width), (count, 8, width), f32),
         ],
         [

time: 189 us -> 186 us (0.984); the launches traced: 189 us -> 183 us
  Pallas kernels: 126 us -> 122 us
    pallas_call x9, Pallas kernels: 126 us -> 122 us  [call(): pl.pallas_call(kernel, grid=(grid,), in_specs=in_specs, out_specs=[o[0] f...]
  transfers between devices with their start and end apart: 17 -> 17, of which waited for: 11 -> 11; matrix products, arithmetic and copies ran while one was open for 1% -> 1% of each run, Pallas kernels for 33% -> 34%
where the time goes in v6:
time: 186 us; the launch traced here: 183 us
  Pallas kernels  122 us (66%)
  starting transfers between devices  33.5 us (18%)
  waiting for transfers between devices  23.1 us (12%)
  between operations  2.34 us (1%)
  other arithmetic  2.22 us (1%)
    pallas_call x9, Pallas kernels, call(): pl.pallas_call(kernel, grid=(grid,), in_specs=in_specs, out_specs=[o[0] f...  122 us
    ppermute x14, waiting for transfers between devices, swap(): return lax.ppermute(x, axes, [(i, i ^ mask) for i in range(size)])  19.7 us
    ppermute x14, starting transfers between devices, swap(): return lax.ppermute(x, axes, [(i, i ^ mask) for i in range(size)])  16.6 us
    all_to_all x1, starting transfers between devices, body(): lax.all_to_all(pack, both, 0, 0, axis_index_groups=sides, tiled=True)  8.31 us
    all_to_all x1, starting transfers between devices, body(): lax.all_to_all(parcel, 'row', 0, 0, axis_index_groups=row_sides, tiled=True)  5.62 us
  transfers between devices with their start and end apart: 17, of which 11 were waited for; matrix products, arithmetic and copies ran while one was open for 1% of the time, Pallas kernels for 34%

profile of v6, /device:TPU:0, one launch (start us, length us, event | category | flops | bytes accessed | tf_op | source)
XLA Modules:
  0.0 183.0 jit_solution(14276940938801194455)
XLA Ops:
  0.7 1.6 pack.1
  2.2 8.3 %all-to-all-start = ((bf16[16,8,1088]{2,1,0:T(8,128)(2,1)}), bf16[16,8,1088]{2,1,0:T(8,128)(2,1)S(1)}, u32[]{:S(2)}, u32[]{:S(2)}) async-start(bf16[16,8,1088]{2,1,0:T(8,128)(2,1)} %pack.1), calls=%async_computation | async-start | bytes 589824 | tf_op jit(solution)/shard_map/all_to_all | solution.py:1130
  10.6 5.3 %front.1 = (bf16[24,128,384]{2,1,0:T(8,128)(2,1)}, bf16[24,128,384]{2,1,0:T(8,128)(2,1)}, bf16[4,24,384]{2,1,0:T(8,128)(2,1)S(1)}) custom-call(bf16[24,384,128]{2,1,0:T(8,128)(2,1)} %bitcast.29, f32[3,128]{1,0:T(4,128)S(1)} %copy-done.6, f32[68,128]{1,0:T(8,128)S(1)} %bitcast.24), custom_call_target="tpu_custom_call" | custom-call | flops 4800000000 | bytes 1048576 | tf_op jit(solution)/shard_map/front/pallas_call | solution.py:797
  15.9 2.8 %collective-permute-start.1 = (bf16[1,4,24,384]{3,2,1,0:T(8,128)(2,1)S(1)}, bf16[1,4,24,384]{3,2,1,0:T(8,128)(2,1)S(1)}, u32[]{:S(2)}, u32[]{:S(2)}) collective-permute-start(bf16[1,4,24,384]{3,2,1,0:T(8,128)(2,1)S(1)} %bitcast.19), channel_id=1, source_target_pairs={{0,8},{1,9},{2,10},{3,11},{4,12},{5,13},{6,14},{7,15},{8,0},{9,1},... | collective-permute-start | bytes 221192 | tf_op jit(solution)/shard_map/ppermute | solution.py:1078
  18.7 3.3 %all-to-all-done.mine_ref.packs_ref = bf16[16,8,1088]{2,1,0:T(8,128)(2,1)S(1)} async-done(((bf16[16,8,1088]{2,1,0:T(8,128)(2,1)}), bf16[16,8,1088]{2,1,0:T(8,128)(2,1)S(1)}, u32[]{:S(2)}, u32[]{:S(2)}) %all-to-all-start) | async-done | bytes 278560 | tf_op jit(solution)/shard_map/all_to_all | solution.py:1130
  24.0 4.4 %collective-permute-done.2 = bf16[2,4,24,384]{3,2,1,0:T(8,128)(2,1)S(1)} collective-permute-done((bf16[2,4,24,384]{3,2,1,0:T(8,128)(2,1)S(1)}, bf16[2,4,24,384]{3,2,1,0:T(8,128)(2,1)S(1)}, u32[]{:S(2)}, u32[]{:S(2)}) %collective-permute-start.2) | collective-permute-done | bytes 147488 | tf_op jit(solution)/shard_map/ppermute | solution.py:1078
  30.0 6.6 %project.1 = (bf16[24,384,384]{2,1,0:T(8,128)(2,1)}, bf16[24,384,128]{2,1,0:T(8,128)(2,1)}, f32[8,9216]{1,0:T(8,128)S(1)}, bf16[128,1152]{1,0:T(8,128)(2,1)S(1)}...) custom-call(s32[4]{0:T(128)S(1)} %pad_add_fusion.info_ref, bf16[16,8,1088]{2,1,0:T(8,128)(2,1)S(1)} %all-to-all-done.mine_ref.packs_ref, ...), custom_call_target="tpu_custom_call" | custom-call | flops 32000000000 | bytes 1048576 | tf_op jit(solution)/shard_map/project/pallas_call | solution.py:797
  37.5 2.0 %collective-permute-done.4.other_bias_ref = bf16[8,4,24,384]{3,2,1,0:T(8,128)(2,1)S(1)} collective-permute-done((bf16[8,4,24,384]{3,2,1,0:T(8,128)(2,1)S(1)}, bf16[8,4,24,384]{3,2,1,0:T(8,128)(2,1)S(1)}, u32[]{:S(2)}, u32[]{:S(2)}) %collective-permute-start.4) | collective-permute-done | bytes 589856 | tf_op jit(solution)/shard_map/ppermute | solution.py:1078
  39.5 23.3 %attend.1 = (bf16[24,384,1536]{2,1,0:T(8,128)(2,1)}, bf16[24,128,384]{2,1,0:T(8,128)(2,1)}, f32[24,8,384]{2,1,0:T(8,128)S(1)}) custom-call(s32[4]{0:T(128)S(1)} %pad_add_fusion.info_ref, f32[8,9216]{1,0:T(8,128)S(1)} %get-tuple-element.61.norm_ref, bf16[8,4,24,384]{3,2,1,0:T(8,128)(2,1)S(1)} %maximum_add_fusion.bias_ref, ...), custom_call_target="tpu_custom_call" | custom-call | flops 20000000000 | bytes 1048576 | tf_op jit(solution)/shard_map/attend/pallas_call | solution.py:797
  62.8 30.2 %middle.1 = (bf16[24,128,384]{2,1,0:T(8,128)(2,1)}, f32[24,8,384]{2,1,0:T(8,128)S(1)}, bf16[12,128,128]{2,1,0:T(8,128)(2,1)}, bf16[16,128]{1,0:T(8,128)(2,1)S(1)}) custom-call(s32[4]{0:T(128)S(1)} %pad_add_fusion.info_ref, bf16[128,1152]{1,0:T(8,128)(2,1)S(1)} %get-tuple-element.58.wide_ref.full_ref, bf16[512,128]{1,0:T(8,128)(2,1)S(1)} %get-tuple-element.59.down_ref, ...), custom_call_target="tpu_custom_call" | custom-call | flops 24000000000 | bytes 1048576 | tf_op jit(solution)/shard_map/middle/pallas_call | solution.py:797
  93.0 3.0 %all-to-all-start.1 = ((bf16[32,48,128]{2,1,0:T(8,128)(2,1)}), bf16[32,48,128]{2,1,0:T(8,128)(2,1)S(1)}, u32[]{:S(2)}, u32[]{:S(2)}) async-start(bf16[32,48,128]{2,1,0:T(8,128)(2,1)} %bitcast.6), calls=%async_computation.1 | async-start | bytes 786432 | tf_op jit(solution)/shard_map/all_to_all | solution.py:1160
  96.0 14.1 %score.1 = (bf16[8,288,128]{2,1,0:T(8,128)(2,1)S(1)}, bf16[8,288,128]{2,1,0:T(8,128)(2,1)S(1)}) custom-call(s32[4]{0:T(128)S(1)} %pad_add_fusion.info_ref, bf16[24,384,1536]{2,1,0:T(8,128)(2,1)} %get-tuple-element.68.p_ref, bf16[24,384,128]{2,1,0:T(8,128)(2,1)} %get-tuple-element.69.vn_ref, bf16[24,128,384]{2,1,0:T(8,128)(2,1)} %get-tuple-element.79.do_ref, ...), custom_call_target="tpu_custom_call" | custom-call | flops 13600000000 | bytes 1048576 | tf_op jit(solution)/shard_map/score/pallas_call | solution.py:797
  113.5 5.6 %all-to-all-start.2 = ((bf16[8,416,128]{2,1,0:T(8,128)(2,1)}), bf16[8,416,128]{2,1,0:T(8,128)(2,1)S(1)}, u32[]{:S(2)}, u32[]{:S(2)}) async-start(bf16[8,416,128]{2,1,0:T(8,128)(2,1)} %pad_maximum_fusion), calls=%async_computation.2 | async-start | bytes 1703936 | tf_op jit(solution)/shard_map/all_to_all | solution.py:1171
  119.1 35.8 %back.1 = (f32[192,128]{1,0:T(8,128)S(1)}, f32[192,128]{1,0:T(8,128)S(1)}) custom-call(s32[4]{0:T(128)S(1)} %pad_add_fusion.info_ref, bf16[24,384,1536]{2,1,0:T(8,128)(2,1)} %get-tuple-element.68.p_ref, bf16[24,384,384]{2,1,0:T(8,128)(2,1)} %get-tuple-element.64.q_ref.k_ref.v_ref, bf16[24,384,384]{2,1,0:T(8,128)(2,1)} %get-tuple-element.64.q_ref.k_ref.v_ref, ...), custom_call_target="tpu_custom_call" | custom-call | flops 30400000000 | bytes 1048576 | tf_op jit(solution)/shard_map/back/pallas_call | solution.py:797
  156.3 2.4 %late.1 = (f32[200,128]{1,0:T(8,128)S(1)}, bf16[200,128]{1,0:T(8,128)(2,1)S(1)}) custom-call(bf16[8,416,128]{2,1,0:T(8,128)(2,1)S(1)} %all-to-all-done.2.spread_ref, f32[192,128]{1,0:T(8,128)S(1)} %get-tuple-element.80.keep_ref, f32[192,128]{1,0:T(8,128)S(1)} %collective-permute-done.8.got_ref, bf16[24,128,384]{2,1,0:T(8,128)(2,1)} %get-tuple-element.57.zbt_ref), custom_call_target="tpu_custom_call" | custom-call | flops 2400000000 | bytes 1048576 | tf_op jit(solution)/shard_map/late/pallas_call | solution.py:797
  158.6 3.0 %collective-permute-start.9 = (bf16[200,128]{1,0:T(8,128)(2,1)S(1)}, bf16[200,128]{1,0:T(8,128)(2,1)S(1)}, u32[]{:S(2)}, u32[]{:S(2)}) collective-permute-start(bf16[200,128]{1,0:T(8,128)(2,1)S(1)} %get-tuple-element.83), channel_id=1, source_target_pairs={{0,8},{1,9},{2,10},{3,11},{4,12},{5,13},{6,14},{7,15},{8,0},{9,1},... | collective-permute-start | bytes 153608 | tf_op jit(solution)/shard_map/ppermute | solution.py:1078
  161.6 1.5 collective-permute-start.7
  163.7 2.1 %collective-permute-start.10 = (f32[200,128]{1,0:T(8,128)S(1)}, f32[200,128]{1,0:T(8,128)S(1)}, u32[]{:S(2)}, u32[]{:S(2)}) collective-permute-start(f32[200,128]{1,0:T(8,128)S(1)} %convert_add_fusion), channel_id=1, source_target_pairs={{0,4},{1,5},{2,6},{3,7},{4,0},{5,1},{6,2},{7,3},{8,12},{9,13},{10,... | collective-permute-start | bytes 307208 | tf_op jit(solution)/shard_map/ppermute | solution.py:1078
  165.8 2.7 %collective-permute-done.10 = f32[200,128]{1,0:T(8,128)S(1)} collective-permute-done((f32[200,128]{1,0:T(8,128)S(1)}, f32[200,128]{1,0:T(8,128)S(1)}, u32[]{:S(2)}, u32[]{:S(2)}) %collective-permute-start.10) | collective-permute-done | bytes 102432 | tf_op jit(solution)/shard_map/ppermute | solution.py:1078
  168.5 3.2 %collective-permute-start.11 = (f32[200,128]{1,0:T(8,128)S(1)}, f32[200,128]{1,0:T(8,128)S(1)}, u32[]{:S(2)}, u32[]{:S(2)}) collective-permute-start(f32[200,128]{1,0:T(8,128)S(1)} %add.38), channel_id=1, source_target_pairs={{0,2},{1,3},{2,0},{3,1},{4,6},{5,7},{6,4},{7,5},{8,10},{9,11},{10,... | collective-permute-start | bytes 307208 | tf_op jit(solution)/shard_map/ppermute | solution.py:1078
  171.6 2.6 %collective-permute-done.11 = f32[200,128]{1,0:T(8,128)S(1)} collective-permute-done((f32[200,128]{1,0:T(8,128)S(1)}, f32[200,128]{1,0:T(8,128)S(1)}, u32[]{:S(2)}, u32[]{:S(2)}) %collective-permute-start.11) | collective-permute-done | bytes 102432 | tf_op jit(solution)/shard_map/ppermute | solution.py:1078
  174.3 1.5 collective-permute-start.12
  176.0 3.0 %collective-permute-done.12 = f32[200,128]{1,0:T(8,128)S(1)} collective-permute-done((f32[200,128]{1,0:T(8,128)S(1)}, f32[200,128]{1,0:T(8,128)S(1)}, u32[]{:S(2)}, u32[]{:S(2)}) %collective-permute-start.12) | collective-permute-done | bytes 102432 | tf_op jit(solution)/shard_map/ppermute | solution.py:1078
  180.4 2.4 %finish.1 = (f32[8,576]{1,0:T(8,128)}, f32[8]{0:T(128)}, f32[576]{0:T(1024)}, f32[8,576]{1,0:T(8,128)}, f32[32,64]{1,0:T(8,128)}, /*index=5*/f32[32]{0:T(128)}, ...) custom-call(s32[4]{0:T(128)S(1)} %pad_add_fusion.info_ref, ...), custom_call_target="tpu_custom_call" | custom-call | flops 3200000000 | bytes 1048576 | tf_op jit(solution)/shard_map/finish/pallas_call | solution.py:797
  (54 shorter events, 9.9 us)
Async XLA Ops:
  0.6 9.9 %copy-start.6 = (f32[3,128]{1,0:T(4,128)S(1)}, f32[3,128]{1,0:T(4,128)}, u32[]{:S(2)}) copy-start(f32[3,128]{1,0:T(4,128)} %gains_ref.5) | copy-start | bytes 4612
  2.2 19.8 %all-to-all-start = ((bf16[16,8,1088]{2,1,0:T(8,128)(2,1)}), bf16[16,8,1088]{2,1,0:T(8,128)(2,1)S(1)}, u32[]{:S(2)}, u32[]{:S(2)}) async-start(bf16[16,8,1088]{2,1,0:T(8,128)(2,1)} %pack.1), calls=%async_computation | async-start | bytes 589824 | tf_op jit(solution)/shard_map/all_to_all | solution.py:1130
  15.9 7.3 %collective-permute-start.1 = (bf16[1,4,24,384]{3,2,1,0:T(8,128)(2,1)S(1)}, bf16[1,4,24,384]{3,2,1,0:T(8,128)(2,1)S(1)}, u32[]{:S(2)}, u32[]{:S(2)}) collective-permute-start(bf16[1,4,24,384]{3,2,1,0:T(8,128)(2,1)S(1)} %bitcast.19), channel_id=1, source_target_pairs={{0,8},{1,9},{2,10},{3,11},{4,12},{5,13},{6,14},{7,15},{8,0},{9,1},... | collective-permute-start | bytes 221192 | tf_op jit(solution)/shard_map/ppermute | solution.py:1078
  22.0 8.0 %collective-permute-start = (bf16[16,8,1088]{2,1,0:T(8,128)(2,1)S(1)}, bf16[16,8,1088]{2,1,0:T(8,128)(2,1)S(1)}, u32[]{:S(2)}, u32[]{:S(2)}) collective-permute-start(bf16[16,8,1088]{2,1,0:T(8,128)(2,1)S(1)} %all-to-all-done.mine_ref.packs_ref), channel_id=1, source_target_pairs={{0,1},{1,0},{2,3},{3,2},{4,5},{5,4},{6,7},{7,6},{8,9},{9,8},{10,11... | collective-permute-start | bytes 835592 | tf_op jit(solution)/shard_map/ppermute | solution.py:1078
  23.2 5.2 %collective-permute-start.2 = (bf16[2,4,24,384]{3,2,1,0:T(8,128)(2,1)S(1)}, bf16[2,4,24,384]{3,2,1,0:T(8,128)(2,1)S(1)}, u32[]{:S(2)}, u32[]{:S(2)}) collective-permute-start(bf16[2,4,24,384]{3,2,1,0:T(8,128)(2,1)S(1)} %pad_maximum_fusion.2), channel_id=1, source_target_pairs={{0,4},{1,5},{2,6},{3,7},{4,0},{5,1},{6,2},{7,3},{8,12},{9,13},{10,... | collective-permute-start | bytes 442376 | tf_op jit(solution)/shard_map/ppermute | solution.py:1078
  28.5 8.8 %collective-permute-start.3 = (bf16[4,4,24,384]{3,2,1,0:T(8,128)(2,1)S(1)}, bf16[4,4,24,384]{3,2,1,0:T(8,128)(2,1)S(1)}, u32[]{:S(2)}, u32[]{:S(2)}) collective-permute-start(bf16[4,4,24,384]{3,2,1,0:T(8,128)(2,1)S(1)} %pad_maximum_fusion.1), channel_id=1, source_target_pairs={{0,2},{1,3},{2,0},{3,1},{4,6},{5,7},{6,4},{7,5},{8,10},{9,11},{10,... | collective-permute-start | bytes 884744 | tf_op jit(solution)/shard_map/ppermute | solution.py:1078
  37.4 2.1 %collective-permute-start.4 = (bf16[8,4,24,384]{3,2,1,0:T(8,128)(2,1)S(1)}, bf16[8,4,24,384]{3,2,1,0:T(8,128)(2,1)S(1)}, u32[]{:S(2)}, u32[]{:S(2)}) collective-permute-start(bf16[8,4,24,384]{3,2,1,0:T(8,128)(2,1)S(1)} %maximum_add_fusion.bias_ref), channel_id=1, source_target_pairs={{0,1},{1,0},{2,3},{3,2},{4,5},{5,4},{6,7},{7,6},{8,9},{9,8},{10,11... | collective-permute-start | bytes 1769480 | tf_op jit(solution)/shard_map/ppermute | solution.py:1078
  39.5 23.3 %copy-start = (s32[1,24,384]{2,1,0:T(8,128)S(1)}, s32[1,24,384]{2,1,0:T(8,128)}, u32[]{:S(2)}) copy-start(s32[1,24,384]{2,1,0:T(8,128)} %tgt_ref.1) | copy-start | bytes 110596
  39.5 23.3 %copy-start.1 = (s32[1,24,384]{2,1,0:T(8,128)S(1)}, s32[1,24,384]{2,1,0:T(8,128)}, u32[]{:S(2)}) copy-start(s32[1,24,384]{2,1,0:T(8,128)} %nbr_ref.1) | copy-start | bytes 110596
  93.0 17.2 %all-to-all-start.1 = ((bf16[32,48,128]{2,1,0:T(8,128)(2,1)}), bf16[32,48,128]{2,1,0:T(8,128)(2,1)S(1)}, u32[]{:S(2)}, u32[]{:S(2)}) async-start(bf16[32,48,128]{2,1,0:T(8,128)(2,1)} %bitcast.6), calls=%async_computation.1 | async-start | bytes 786432 | tf_op jit(solution)/shard_map/all_to_all | solution.py:1160
  110.2 2.1 %collective-permute-start.5 = (bf16[8,288,128]{2,1,0:T(8,128)(2,1)S(1)}, bf16[8,288,128]{2,1,0:T(8,128)(2,1)S(1)}, u32[]{:S(2)}, u32[]{:S(2)}) collective-permute-start(bf16[8,288,128]{2,1,0:T(8,128)(2,1)S(1)} %get-tuple-element.75), channel_id=1, source_target_pairs={{0,1},{1,0},{2,3},{3,2},{4,5},{5,4},{6,7},{7,6},{8,9},{9,8},{10,11... | collective-permute-start | bytes 1769480 | tf_op jit(solution)/shard_map/ppermute | solution.py:1078
  110.4 1.9 %collective-permute-start.6 = (bf16[1,64,128]{2,1,0:T(8,128)(2,1)S(1)}, bf16[1,64,128]{2,1,0:T(8,128)(2,1)S(1)}, u32[]{:S(2)}, u32[]{:S(2)}) collective-permute-start(bf16[1,64,128]{2,1,0:T(8,128)(2,1)S(1)} %maximum_bitcast_fusion), channel_id=1, source_target_pairs={{0,1},{1,0},{2,3},{3,2},{4,5},{5,4},{6,7},{7,6},{8,9},{9,8},{10,11... | collective-permute-start | bytes 49160 | tf_op jit(solution)/shard_map/ppermute | solution.py:1078
  113.5 42.8 %all-to-all-start.2 = ((bf16[8,416,128]{2,1,0:T(8,128)(2,1)}), bf16[8,416,128]{2,1,0:T(8,128)(2,1)S(1)}, u32[]{:S(2)}, u32[]{:S(2)}) async-start(bf16[8,416,128]{2,1,0:T(8,128)(2,1)} %pad_maximum_fusion), calls=%async_computation.2 | async-start | bytes 1703936 | tf_op jit(solution)/shard_map/all_to_all | solution.py:1171
  154.9 1.4 collective-permute-start.8
  156.2 24.2 %copy-start.3 = (f32[128,68]{0,1:T(8,128)S(1)}, f32[128,68]{0,1:T(8,128)}, u32[]{:S(2)}) copy-start(f32[128,68]{0,1:T(8,128)} %param.27) | copy-start | bytes 104452
  156.2 24.2 %copy-start.4 = (f32[8,576]{1,0:T(8,128)S(1)}, f32[8,576]{1,0:T(8,128)}, u32[]{:S(2)}) copy-start(f32[8,576]{1,0:T(8,128)} %wide_ref.3) | copy-start | bytes 55300
  156.2 24.2 %copy-start.5 = (f32[32,64]{1,0:T(8,128)S(1)}, f32[32,64]{1,0:T(8,128)}, u32[]{:S(2)}) copy-start(f32[32,64]{1,0:T(8,128)} %down_ref.3) | copy-start | bytes 24580
  156.2 24.2 %copy-start.7 = (f32[3,128]{1,0:T(4,128)S(1)}, f32[3,128]{1,0:T(4,128)}, u32[]{:S(2)}) copy-start(f32[3,128]{1,0:T(4,128)} %gain_second_ref.1) | copy-start | bytes 4612
  158.6 5.1 %collective-permute-start.9 = (bf16[200,128]{1,0:T(8,128)(2,1)S(1)}, bf16[200,128]{1,0:T(8,128)(2,1)S(1)}, u32[]{:S(2)}, u32[]{:S(2)}) collective-permute-start(bf16[200,128]{1,0:T(8,128)(2,1)S(1)} %get-tuple-element.83), channel_id=1, source_target_pairs={{0,8},{1,9},{2,10},{3,11},{4,12},{5,13},{6,14},{7,15},{8,0},{9,1},... | collective-permute-start | bytes 153608 | tf_op jit(solution)/shard_map/ppermute | solution.py:1078
  161.6 10.0 %collective-permute-start.7 = (bf16[8,128,128]{2,1,0:T(8,128)(2,1)S(1)}, bf16[8,128,128]{2,1,0:T(8,128)(2,1)S(1)}, u32[]{:S(2)}, u32[]{:S(2)}) collective-permute-start(bf16[8,128,128]{2,1,0:T(8,128)(2,1)S(1)} %slice.20.spread_ref), channel_id=1, source_target_pairs={{0,16},{1,17},{2,18},{3,19},{4,20},{5,21},{6,22},{7,23},{8,24},{9,... | collective-permute-start | bytes 786440 | tf_op jit(solution)/shard_map/ppermute | solution.py:1078
  163.7 4.7 %collective-permute-start.10 = (f32[200,128]{1,0:T(8,128)S(1)}, f32[200,128]{1,0:T(8,128)S(1)}, u32[]{:S(2)}, u32[]{:S(2)}) collective-permute-start(f32[200,128]{1,0:T(8,128)S(1)} %convert_add_fusion), channel_id=1, source_target_pairs={{0,4},{1,5},{2,6},{3,7},{4,0},{5,1},{6,2},{7,3},{8,12},{9,13},{10,... | collective-permute-start | bytes 307208 | tf_op jit(solution)/shard_map/ppermute | solution.py:1078
  168.5 5.8 %collective-permute-start.11 = (f32[200,128]{1,0:T(8,128)S(1)}, f32[200,128]{1,0:T(8,128)S(1)}, u32[]{:S(2)}, u32[]{:S(2)}) collective-permute-start(f32[200,128]{1,0:T(8,128)S(1)} %add.38), channel_id=1, source_target_pairs={{0,2},{1,3},{2,0},{3,1},{4,6},{5,7},{6,4},{7,5},{8,10},{9,11},{10,... | collective-permute-start | bytes 307208 | tf_op jit(solution)/shard_map/ppermute | solution.py:1078
  174.3 4.7 %collective-permute-start.12 = (f32[200,128]{1,0:T(8,128)S(1)}, f32[200,128]{1,0:T(8,128)S(1)}, u32[]{:S(2)}, u32[]{:S(2)}) collective-permute-start(f32[200,128]{1,0:T(8,128)S(1)} %add_add_fusion), channel_id=1, source_target_pairs={{0,16},{1,17},{2,18},{3,19},{4,20},{5,21},{6,22},{7,23},{8,24},{9,... | collective-permute-start | bytes 307208 | tf_op jit(solution)/shard_map/ppermute | solution.py:1078
  179.0 1.4 collective-permute-start.13
  (1 other events, 9.9 us)
